TPU v7x, 32 devices: a whole 2x2x4 slice. The times are simulated.
32 devices in a mesh: col: 8 (over y, x, core), slab: 4 (over z).
Axes of the slice: x: 2, y: 2, z: 4, core: 2. Of those that a mesh axis runs over, the one named last changes fastest.
Arguments:
- offsets: float32 [2, 16, 256, 128], P(None, 'col', 'slab'), may hold values from 0 to 1
- velocity: float32 [2, 16, 256, 128], P(None, 'col', 'slab'), may hold values from -8 to 8
- particle_mass: float32 [16, 256, 128], P('col', 'slab'), may hold values from 0.5 to 2
- pressure_start: float32 [16, 256, 128], P('col', 'slab'), may hold values from -4 to 4
- counts: int32 [16, 256], P('col', 'slab'), may hold values from 1 to 128
- leaving_slot: int32 [64, 4, 128], P('col', 'slab'), may hold values from 0 to 16383
- leaving_count: int32 [64, 4], P('col', 'slab'), may hold values from 1 to 128
- leaving_side: int32 [64, 4], P('col', 'slab'), may hold values from 0 to 1
Outputs:
- density_ratio: float32 [16, 256, 128], P('col', 'slab')
- pressure: float32 [16, 256, 128], P('col', 'slab')
- acceleration: float32 [2, 16, 256, 128], P(None, 'col', 'slab')
- velocity_new: float32 [2, 16, 256, 128], P(None, 'col', 'slab')
- offsets_new: float32 [2, 16, 256, 128], P(None, 'col', 'slab')
- arrived: float32 [2, 6, 64, 4, 128], P(None, None, 'col', 'slab')
Inputs may be any that keep to these rules, and one draw needn't show every extreme that they name: `counts`: a cell's particles fill its slots 0 to count - 1. `leaving_slot`: a slot of the sending device's own block of cells. `leaving_count`: the block's slots 0 to count - 1 carry particles. `leaving_side`: 0 sends the block to the lower col index, 1 to the higher.
All inputs are finite; a program needn't handle non-finite values.
Results may differ from a plain program's by a relative error of at most 0.0001.
Values sent between devices are 32-bit elements; how exact they have to be, the bound alone decides.
No kernel may reach another device: no remote copies, remote signals or barrier semaphores. Data moves between devices by JAX's collectives and lax.ppermute only.
A program may use at most 64 MiB of HBM per device.

v0:
```python
import jax
import jax.numpy as jnp
from jax import lax
from jax.sharding import PartitionSpec as P

ITERS = 3


TIME_STEP = 0.1
REST_DENSITY = 50.0
COMPRESSION = 2.0
RELAXATION = 0.5
GRAVITY = 1.0


def with_halo(array, sides, width):
    for axis, dim in sides:
        peers, length = (lax.axis_size(axis), array.shape[dim])
        up = [(i, (i + 1) % peers) for i in range(peers - 1)]
        down = [(j, i) for i, j in up]
        last = lax.slice_in_dim(array, length - width, length, axis=dim)
        initial = lax.slice_in_dim(array, 0, width, axis=dim)
        before = lax.ppermute(last, axis, up)
        after = lax.ppermute(initial, axis, down)
        array = jnp.concatenate([before, array, after], axis=dim)
    return array


def from_behind(block, axis, distance):
    devices = range(lax.axis_size(axis))
    route = [(i - distance, i) for i in devices if i - distance in devices]
    return lax.ppermute(block, axis, route)


def geometry(center, neighbor, shift_x, shift_z):
    delta_x = center[0][:, :, None] - neighbor[0][:, None, :] - shift_x
    delta_z = center[1][:, :, None] - neighbor[1][:, None, :] - shift_z
    support = jnp.maximum(1.0 - delta_x * delta_x - delta_z * delta_z, 0.0)
    return (delta_x, delta_z, support)


def density_terms(center, neighbor, shift_x, shift_z):
    delta_x, delta_z, support = geometry(center, neighbor, shift_x, shift_z)
    kernel = support * support * support
    slope = 6.0 * support * support
    masses = neighbor[4][:, None, :]
    approach = (center[2][:, :, None] - neighbor[2][:, None, :]) * delta_x + (
        center[3][:, :, None] - neighbor[3][:, None, :]
    ) * delta_z
    return jnp.stack([jnp.sum(masses * kernel, -1), -jnp.sum(masses * slope * approach, -1)])


def jacobi_terms(center, neighbor, shift_x, shift_z):
    delta_x, delta_z, support = geometry(center, neighbor, shift_x, shift_z)
    slope = 6.0 * support * support
    return jnp.stack(
        [jnp.sum(neighbor[2][:, None, :] * slope, -1), jnp.sum(neighbor[3][:, None, :] * slope, -1)]
    )


def update_terms(center, neighbor, shift_x, shift_z):
    delta_x, delta_z, support = geometry(center, neighbor, shift_x, shift_z)
    slope = 6.0 * support * support
    return jnp.sum(neighbor[3][:, None, :] * slope, -1)[None]


def force_terms(center, neighbor, shift_x, shift_z):
    delta_x, delta_z, support = geometry(center, neighbor, shift_x, shift_z)
    slope = 6.0 * support * support
    lifted = neighbor[2][:, None, :] * (neighbor[3][:, None, :] - center[3][:, :, None]) * slope
    return jnp.stack([jnp.sum(lifted * delta_x, -1), jnp.sum(lifted * delta_z, -1)])


def column_pass(extended, column_index, depth_cells, pair_terms):
    column_block = lax.dynamic_slice_in_dim(extended, column_index, 3, 1)
    center = column_block[:, 1, 1 : depth_cells + 1]
    totals = None
    for shift_x in (-1, 0, 1):
        for shift_z in (-1, 0, 1):
            neighbor = column_block[:, 1 + shift_x, 1 + shift_z : 1 + shift_z + depth_cells]
            term = pair_terms(center, neighbor, float(shift_x), float(shift_z))
            totals = term if totals is None else totals + term
    return totals


def sweep(extended, columns, depth_cells, pair_terms):

    def one_column(column_index):
        return column_pass(extended, column_index, depth_cells, pair_terms)

    totals = lax.map(one_column, jnp.arange(columns, dtype=jnp.int32))
    return jnp.moveaxis(totals, 0, 1)


def spread_pressure(pressure):
    deeper = with_halo(pressure, (("slab", 1),), 1)
    return with_halo(deeper, (("col", 0),), 1)


def per_device(
    offsets,
    velocity,
    particle_mass,
    pressure_start,
    counts,
    leaving_slot,
    leaving_count,
    leaving_side,
):
    columns, depth_cells, slot_count = (counts.shape[0], counts.shape[1], offsets.shape[-1])
    alive_mask = jnp.arange(slot_count, dtype=jnp.int32)[None, None, :] < counts[:, :, None]
    live_mass = jnp.where(alive_mask, particle_mass, 0.0)
    base_fields = jnp.concatenate([offsets, velocity, live_mass[None]], 0)
    nearby = with_halo(base_fields, (("col", 1), ("slab", 2)), 1)
    totals = sweep(nearby, columns, depth_cells, density_terms)
    density = jnp.where(alive_mask, totals[0], 0.0)
    diverge = totals[1]
    weight = jnp.where(alive_mask, live_mass / jnp.where(alive_mask, density, 1.0), 0.0)
    weight_ext = with_halo(weight, (("col", 0), ("slab", 1)), 1)
    geometry_ext = nearby[0:2]
    density_ratio = density / REST_DENSITY
    source = jnp.where(
        alive_mask, (density + TIME_STEP * diverge - REST_DENSITY) / REST_DENSITY, 0.0
    )
    pressure = jnp.where(alive_mask, pressure_start, 0.0)
    diagonal = None
    for sweep_index in range(ITERS):
        pressure_ext = spread_pressure(pressure)
        stacked = jnp.concatenate(
            [geometry_ext, weight_ext[None], (weight_ext * pressure_ext)[None]], 0
        )
        if sweep_index == 0:
            totals = sweep(stacked, columns, depth_cells, jacobi_terms)
            diagonal = COMPRESSION + totals[0]
            pulled_sum = totals[1]
        else:
            pulled_sum = sweep(stacked, columns, depth_cells, update_terms)[0]
        updated = (1.0 - RELAXATION) * pressure + RELAXATION * (source + pulled_sum) / diagonal
        pressure = jnp.where(alive_mask, updated, 0.0)
    pressure_ext = spread_pressure(pressure)
    stacked = jnp.concatenate([geometry_ext, weight_ext[None], pressure_ext[None]], 0)
    acceleration = jnp.where(
        alive_mask[None], sweep(stacked, columns, depth_cells, force_terms), 0.0
    )
    pulled = jnp.stack([acceleration[0], acceleration[1] - GRAVITY])
    velocity_new = jnp.where(alive_mask[None], velocity + TIME_STEP * pulled, 0.0)
    offsets_new = jnp.where(alive_mask[None], offsets + TIME_STEP * velocity_new, 0.0)
    state = jnp.concatenate(
        [offsets_new, velocity_new, pressure[None], live_mass[None]], 0
    ).reshape(6, -1)
    block_rows = leaving_slot.shape[0]
    blocks = state[:, leaving_slot.reshape(-1)].reshape(6, block_rows, 1, slot_count)
    filled = jnp.arange(slot_count, dtype=jnp.int32)[None, None, :] < leaving_count[:, :, None]
    upward = jnp.where(filled & (leaving_side[:, :, None] == 1), blocks, 0.0)
    downward = jnp.where(filled & (leaving_side[:, :, None] == 0), blocks, 0.0)
    from_lower = from_behind(upward, "col", 1)
    from_higher = from_behind(downward, "col", -1)
    arrived = jnp.stack([from_lower, from_higher])
    return (density_ratio, pressure, acceleration, velocity_new, offsets_new, arrived)


def solution(mesh):
    return jax.shard_map(
        per_device,
        mesh=mesh,
        in_specs=(
            P(None, "col", "slab", None),
            P(None, "col", "slab", None),
            P("col", "slab", None),
            P("col", "slab", None),
            P("col", "slab"),
            P("col", "slab", None),
            P("col", "slab"),
            P("col", "slab"),
        ),
        out_specs=(
            P("col", "slab", None),
            P("col", "slab", None),
            P(None, "col", "slab", None),
            P(None, "col", "slab", None),
            P(None, "col", "slab", None),
            P(None, None, "col", "slab", None),
        ),
        check_vma=False,
    )
```

profile of v0, /device:TPU:28, one launch (start us, length us, event | category | flops | bytes accessed | tf_op | source)
XLA Modules:
  0.0 467.5 jit_solution(4442649441193274390)
XLA Ops:
  8.2 4.7 %collective-permute-done = f32[5,1,64,128]{3,2,1,0:T(8,128)S(1)} collective-permute-done((f32[5,1,64,128]{3,2,1,0:T(8,128)S(1)}, f32[5,1,64,128]{3,2,1,0:T(8,128)S(1)}, u32[]{:S(2)}, u32[]{:S(2)}) %collective-permute-start) | collective-permute-done | bytes 163872 | tf_op jit(solution)/shard_map/ppermute | solution.py:23
  22.7 95.9 %while.70 = (s32[]{:T(128)}, f32[2,2,64,128]{3,2,0,1:T(8,128)S(1)}, s32[2]{0:T(128)S(1)}, f32[5,4,66,128]{3,2,1,0:T(8,128)S(1)}) while((s32[]{:T(128)}, f32[2,2,64,128]{3,2,0,1:T(8,128)S(1)}, s32[2]{0:T(128)S(1)}, f32[5,4,66,128]{3,2,1,0:T(8,128)S(1)}) %tuple.482), condition=%wide.region_19.20_spmd.clone, body=%wide.region_0.19_spmd.sunk.clone | while | flops 210968576 | bytes 6521043 | solution.py:91
  25.6 15.2 %fusion.219 = (f32[64,128]{1,0:T(8,128)S(1)}, f32[64,128]{1,0:T(8,128)S(1)}, f32[64,128]{1,0:T(8,128)S(1)}, f32[64,128]{1,0:T(8,128)S(1)}, f32[64,128]{1,0:T(8,128)S(1)}, /*index=5*/f32[64,128]{1,0:T(8,128)S(1)}) fusion(f32[64,128]{1,0:T(8,128)S(1)} %get-tuple-element.1445, f32[64,128]{1,0:T(8,128)S(1)} %get-tuple-element.1446, ...), kind=kLoop, calls=%fused_computation.63.clone.1.clone | loop fusion | flops 71254016 | bytes 819200 | tf_op jit(solution)/shard_map/while/body/eval_jaxpr/reduce_sum | solution.py:50
  40.8 14.4 %fusion.220 = (f32[64,128]{1,0:T(8,128)S(1)}, f32[64,128]{1,0:T(8,128)S(1)}, f32[64,128]{1,0:T(8,128)S(1)}, f32[64,128]{1,0:T(8,128)S(1)}, f32[64,128]{1,0:T(8,128)S(1)}, /*index=5*/f32[64,128]{1,0:T(8,128)S(1)}) fusion(f32[64,128]{1,0:T(8,128)S(1)} %get-tuple-element.1466, f32[64,128]{1,0:T(8,128)S(1)} %get-tuple-element.1467, ...), kind=kLoop, calls=%fused_computation.71.clone.1.clone | loop fusion | flops 69156864 | bytes 688128 | tf_op jit(solution)/shard_map/while/body/eval_jaxpr/reduce_sum | solution.py:50
  55.2 15.3 %fusion.221 = (f32[64,128]{1,0:T(8,128)S(1)}, f32[64,128]{1,0:T(8,128)S(1)}, f32[64,128]{1,0:T(8,128)S(1)}, f32[64,128]{1,0:T(8,128)S(1)}, f32[64,128]{1,0:T(8,128)S(1)}, /*index=5*/f32[64,128]{1,0:T(8,128)S(1)}) fusion(f32[64,128]{1,0:T(8,128)S(1)} %get-tuple-element.1478, f32[64,128]{1,0:T(8,128)S(1)} %get-tuple-element.1479, ...), kind=kLoop, calls=%fused_computation.68.clone.1.clone | loop fusion | flops 70205440 | bytes 819200 | tf_op jit(solution)/shard_map/while/body/eval_jaxpr/reduce_sum | solution.py:50
  73.5 15.2 %fusion.219 = (f32[64,128]{1,0:T(8,128)S(1)}, f32[64,128]{1,0:T(8,128)S(1)}, f32[64,128]{1,0:T(8,128)S(1)}, f32[64,128]{1,0:T(8,128)S(1)}, f32[64,128]{1,0:T(8,128)S(1)}, /*index=5*/f32[64,128]{1,0:T(8,128)S(1)}) fusion(f32[64,128]{1,0:T(8,128)S(1)} %get-tuple-element.1445, f32[64,128]{1,0:T(8,128)S(1)} %get-tuple-element.1446, ...), kind=kLoop, calls=%fused_computation.63.clone.1.clone | loop fusion | flops 71254016 | bytes 819200 | tf_op jit(solution)/shard_map/while/body/eval_jaxpr/reduce_sum | solution.py:50
  88.8 14.4 %fusion.220 = (f32[64,128]{1,0:T(8,128)S(1)}, f32[64,128]{1,0:T(8,128)S(1)}, f32[64,128]{1,0:T(8,128)S(1)}, f32[64,128]{1,0:T(8,128)S(1)}, f32[64,128]{1,0:T(8,128)S(1)}, /*index=5*/f32[64,128]{1,0:T(8,128)S(1)}) fusion(f32[64,128]{1,0:T(8,128)S(1)} %get-tuple-element.1466, f32[64,128]{1,0:T(8,128)S(1)} %get-tuple-element.1467, ...), kind=kLoop, calls=%fused_computation.71.clone.1.clone | loop fusion | flops 69156864 | bytes 688128 | tf_op jit(solution)/shard_map/while/body/eval_jaxpr/reduce_sum | solution.py:50
  103.1 15.3 %fusion.221 = (f32[64,128]{1,0:T(8,128)S(1)}, f32[64,128]{1,0:T(8,128)S(1)}, f32[64,128]{1,0:T(8,128)S(1)}, f32[64,128]{1,0:T(8,128)S(1)}, f32[64,128]{1,0:T(8,128)S(1)}, /*index=5*/f32[64,128]{1,0:T(8,128)S(1)}) fusion(f32[64,128]{1,0:T(8,128)S(1)} %get-tuple-element.1478, f32[64,128]{1,0:T(8,128)S(1)} %get-tuple-element.1479, ...), kind=kLoop, calls=%fused_computation.68.clone.1.clone | loop fusion | flops 70205440 | bytes 819200 | tf_op jit(solution)/shard_map/while/body/eval_jaxpr/reduce_sum | solution.py:50
  143.1 67.0 %while.71 = (s32[]{:T(128)}, f32[2,2,64,128]{3,2,0,1:T(8,128)S(1)}, s32[2]{0:T(128)S(1)}, f32[4,4,66,128]{3,2,1,0:T(8,128)S(1)}) while((s32[]{:T(128)}, f32[2,2,64,128]{3,2,0,1:T(8,128)S(1)}, s32[2]{0:T(128)S(1)}, f32[4,4,66,128]{3,2,1,0:T(8,128)S(1)}) %tuple.485), condition=%wide.region_39.40_spmd.clone, body=%wide.region_20.39_spmd.sunk.clone | while | flops 144834560 | bytes 4849859 | solution.py:91
  145.8 15.6 %multiply_reduce_fusion.40 = (f32[64,128]{1,0:T(8,128)S(1)}, f32[64,128]{1,0:T(8,128)S(1)}, f32[64,128]{1,0:T(8,128)S(1)}, f32[64,128]{1,0:T(8,128)S(1)}, f32[64...) fusion(f32[64,128]{1,0:T(8,128)S(1)} %get-tuple-element.1532, ...), kind=kLoop, calls=%fused_computation.186.clone.1.clone | loop fusion | flops 72278016 | bytes 917504 | tf_op jit(solution)/shard_map/while/body/eval_jaxpr/reduce_sum | solution.py:57
  161.5 15.0 %multiply_reduce_fusion.41 = (f32[64,128]{1,0:T(8,128)S(1)}, f32[64,128]{1,0:T(8,128)S(1)}, f32[64,128]{1,0:T(8,128)S(1)}, f32[64,128]{1,0:T(8,128)S(1)}, f32[64...) fusion(f32[64,128]{1,0:T(8,128)S(1)} %get-tuple-element.1553, ...), kind=kLoop, calls=%fused_computation.184.clone.1.clone | loop fusion | flops 72278016 | bytes 917504 | tf_op jit(solution)/shard_map/while/body/eval_jaxpr/reduce_sum | solution.py:57
  179.3 15.6 %multiply_reduce_fusion.40 = (f32[64,128]{1,0:T(8,128)S(1)}, f32[64,128]{1,0:T(8,128)S(1)}, f32[64,128]{1,0:T(8,128)S(1)}, f32[64,128]{1,0:T(8,128)S(1)}, f32[64...) fusion(f32[64,128]{1,0:T(8,128)S(1)} %get-tuple-element.1532, ...), kind=kLoop, calls=%fused_computation.186.clone.1.clone | loop fusion | flops 72278016 | bytes 917504 | tf_op jit(solution)/shard_map/while/body/eval_jaxpr/reduce_sum | solution.py:57
  195.0 15.0 %multiply_reduce_fusion.41 = (f32[64,128]{1,0:T(8,128)S(1)}, f32[64,128]{1,0:T(8,128)S(1)}, f32[64,128]{1,0:T(8,128)S(1)}, f32[64,128]{1,0:T(8,128)S(1)}, f32[64...) fusion(f32[64,128]{1,0:T(8,128)S(1)} %get-tuple-element.1553, ...), kind=kLoop, calls=%fused_computation.184.clone.1.clone | loop fusion | flops 72278016 | bytes 917504 | tf_op jit(solution)/shard_map/while/body/eval_jaxpr/reduce_sum | solution.py:57
  226.3 49.0 %while.72 = (s32[]{:T(128)}, f32[2,1,64,128]{3,2,1,0:T(8,128)S(1)}, s32[2]{0:T(128)S(1)}, f32[4,4,66,128]{3,2,1,0:T(8,128)S(1)}) while((s32[]{:T(128)}, f32[2,1,64,128]{3,2,1,0:T(8,128)S(1)}, s32[2]{0:T(128)S(1)}, f32[4,4,66,128]{3,2,1,0:T(8,128)S(1)}) %tuple.488), condition=%wide.region_50.51_spmd.clone, body=%wide.region_40.50_spmd.sunk.clone | while | flops 116383752 | bytes 3342531 | solution.py:91
  229.0 8.0 %fusion.224 = (f32[64,128]{1,0:T(8,128)S(1)}, f32[64,128]{1,0:T(8,128)S(1)}, f32[64,128]{1,0:T(8,128)S(1)}) fusion(f32[64,128]{1,0:T(8,128)S(1)} %get-tuple-element.1601, f32[64,128]{1,0:T(8,128)S(1)} %get-tuple-element.1602, f32[64,128]{1,0:T(8,128)S(1)} %get-tuple-element.1603, f32[64,128]{1,0:T(8,128)S(1)} %get-tuple-element.1604, ...), kind=kLoop, calls=%fused_computation.257.clone.1.clone | loop fusion | flops 39821312 | bytes 458752 | tf_op jit(solution)/shard_map/while/body/eval_jaxpr/reduce_sum | solution.py:64
  237.0 13.8 %fusion.225 = (f32[64,128]{1,0:T(8,128)S(1)}, f32[64,128]{1,0:T(8,128)S(1)}, f32[64,128]{1,0:T(8,128)S(1)}, f32[64,128]{1,0:T(8,128)S(1)}, f32[64,128]{1,0:T(8,128)S(1)}, /*index=5*/f32[64,128]{1,0:T(8,128)S(1)}) fusion(f32[64,128]{1,0:T(8,128)S(1)} %get-tuple-element.1614, f32[64,128]{1,0:T(8,128)S(1)} %get-tuple-element.1615, ...), kind=kLoop, calls=%fused_computation.259.clone.1.clone | loop fusion | flops 76496896 | bytes 786432 | tf_op jit(solution)/shard_map/while/body/eval_jaxpr/reduce_sum | solution.py:64
  253.5 8.0 %fusion.224 = (f32[64,128]{1,0:T(8,128)S(1)}, f32[64,128]{1,0:T(8,128)S(1)}, f32[64,128]{1,0:T(8,128)S(1)}) fusion(f32[64,128]{1,0:T(8,128)S(1)} %get-tuple-element.1601, f32[64,128]{1,0:T(8,128)S(1)} %get-tuple-element.1602, f32[64,128]{1,0:T(8,128)S(1)} %get-tuple-element.1603, f32[64,128]{1,0:T(8,128)S(1)} %get-tuple-element.1604, ...), kind=kLoop, calls=%fused_computation.257.clone.1.clone | loop fusion | flops 39821312 | bytes 458752 | tf_op jit(solution)/shard_map/while/body/eval_jaxpr/reduce_sum | solution.py:64
  261.5 13.8 %fusion.225 = (f32[64,128]{1,0:T(8,128)S(1)}, f32[64,128]{1,0:T(8,128)S(1)}, f32[64,128]{1,0:T(8,128)S(1)}, f32[64,128]{1,0:T(8,128)S(1)}, f32[64,128]{1,0:T(8,128)S(1)}, /*index=5*/f32[64,128]{1,0:T(8,128)S(1)}) fusion(f32[64,128]{1,0:T(8,128)S(1)} %get-tuple-element.1614, f32[64,128]{1,0:T(8,128)S(1)} %get-tuple-element.1615, ...), kind=kLoop, calls=%fused_computation.259.clone.1.clone | loop fusion | flops 76496896 | bytes 786432 | tf_op jit(solution)/shard_map/while/body/eval_jaxpr/reduce_sum | solution.py:64
  291.2 49.0 %while.73 = (s32[]{:T(128)}, f32[2,1,64,128]{3,2,1,0:T(8,128)S(1)}, s32[2]{0:T(128)S(1)}, f32[4,4,66,128]{3,2,1,0:T(8,128)S(1)}) while((s32[]{:T(128)}, f32[2,1,64,128]{3,2,1,0:T(8,128)S(1)}, s32[2]{0:T(128)S(1)}, f32[4,4,66,128]{3,2,1,0:T(8,128)S(1)}) %tuple.491), condition=%wide.region_61.62_spmd.clone, body=%wide.region_51.61_spmd.sunk.clone | while | flops 116383752 | bytes 3342531 | solution.py:91
  293.9 8.0 %fusion.226 = (f32[64,128]{1,0:T(8,128)S(1)}, f32[64,128]{1,0:T(8,128)S(1)}, f32[64,128]{1,0:T(8,128)S(1)}) fusion(f32[64,128]{1,0:T(8,128)S(1)} %get-tuple-element.1652, f32[64,128]{1,0:T(8,128)S(1)} %get-tuple-element.1653, f32[64,128]{1,0:T(8,128)S(1)} %get-tuple-element.1654, f32[64,128]{1,0:T(8,128)S(1)} %get-tuple-element.1655, ...), kind=kLoop, calls=%fused_computation.312.clone.1.clone | loop fusion | flops 39821312 | bytes 458752 | tf_op jit(solution)/shard_map/while/body/eval_jaxpr/reduce_sum | solution.py:64
  301.9 13.8 %fusion.227 = (f32[64,128]{1,0:T(8,128)S(1)}, f32[64,128]{1,0:T(8,128)S(1)}, f32[64,128]{1,0:T(8,128)S(1)}, f32[64,128]{1,0:T(8,128)S(1)}, f32[64,128]{1,0:T(8,128)S(1)}, /*index=5*/f32[64,128]{1,0:T(8,128)S(1)}) fusion(f32[64,128]{1,0:T(8,128)S(1)} %get-tuple-element.1665, f32[64,128]{1,0:T(8,128)S(1)} %get-tuple-element.1666, ...), kind=kLoop, calls=%fused_computation.314.clone.1.clone | loop fusion | flops 76496896 | bytes 786432 | tf_op jit(solution)/shard_map/while/body/eval_jaxpr/reduce_sum | solution.py:64
  318.4 8.0 %fusion.226 = (f32[64,128]{1,0:T(8,128)S(1)}, f32[64,128]{1,0:T(8,128)S(1)}, f32[64,128]{1,0:T(8,128)S(1)}) fusion(f32[64,128]{1,0:T(8,128)S(1)} %get-tuple-element.1652, f32[64,128]{1,0:T(8,128)S(1)} %get-tuple-element.1653, f32[64,128]{1,0:T(8,128)S(1)} %get-tuple-element.1654, f32[64,128]{1,0:T(8,128)S(1)} %get-tuple-element.1655, ...), kind=kLoop, calls=%fused_computation.312.clone.1.clone | loop fusion | flops 39821312 | bytes 458752 | tf_op jit(solution)/shard_map/while/body/eval_jaxpr/reduce_sum | solution.py:64
  326.4 13.8 %fusion.227 = (f32[64,128]{1,0:T(8,128)S(1)}, f32[64,128]{1,0:T(8,128)S(1)}, f32[64,128]{1,0:T(8,128)S(1)}, f32[64,128]{1,0:T(8,128)S(1)}, f32[64,128]{1,0:T(8,128)S(1)}, /*index=5*/f32[64,128]{1,0:T(8,128)S(1)}) fusion(f32[64,128]{1,0:T(8,128)S(1)} %get-tuple-element.1665, f32[64,128]{1,0:T(8,128)S(1)} %get-tuple-element.1666, ...), kind=kLoop, calls=%fused_computation.314.clone.1.clone | loop fusion | flops 76496896 | bytes 786432 | tf_op jit(solution)/shard_map/while/body/eval_jaxpr/reduce_sum | solution.py:64
  356.8 89.8 %while.74 = (s32[]{:T(128)}, f32[2,2,64,128]{3,2,1,0:T(8,128)S(1)}, s32[2]{0:T(128)S(1)}, f32[4,4,66,128]{3,2,1,0:T(8,128)S(1)}) while((s32[]{:T(128)}, f32[2,2,64,128]{3,2,1,0:T(8,128)S(1)}, s32[2]{0:T(128)S(1)}, f32[4,4,66,128]{3,2,1,0:T(8,128)S(1)}) %tuple.494), condition=%wide.region_81.82_spmd.clone, body=%wide.region_62.81_spmd.sunk.clone | while | flops 163708928 | bytes 4980931 | solution.py:91
  359.5 6.3 %multiply_reduce_fusion.42 = (f32[64,128]{1,0:T(8,128)S(1)}, f32[64,128]{1,0:T(8,128)S(1)}) fusion(f32[64,128]{1,0:T(8,128)S(1)} %get-tuple-element.1703, f32[64,128]{1,0:T(8,128)S(1)} %get-tuple-element.1704, f32[64,128]{1,0:T(8,128)S(1)} %get-tuple-element.1705, f32[64,128]{1,0:T(8,128)S(1)} %get-tuple-element.1706, ...), kind=kLoop, calls=%fused_computation.427.clone.1.clone | loop fusion | flops 18857984 | bytes 294912 | tf_op jit(solution)/shard_map/while/body/eval_jaxpr/reduce_sum | solution.py:71
  365.8 17.8 %multiply_reduce_fusion.43 = (f32[64,128]{1,0:T(8,128)S(1)}, f32[64,128]{1,0:T(8,128)S(1)}, f32[64,128]{1,0:T(8,128)S(1)}, f32[64,128]{1,0:T(8,128)S(1)}, f32[64...) fusion(f32[64,128]{1,0:T(8,128)S(1)} %get-tuple-element.1712, ...), kind=kLoop, calls=%fused_computation.407.clone.1.clone | loop fusion | flops 73334784 | bytes 884736 | tf_op jit(solution)/shard_map/while/body/eval_jaxpr/reduce_sum | solution.py:71
  383.6 17.9 %multiply_reduce_fusion.44 = (f32[64,128]{1,0:T(8,128)S(1)}, f32[64,128]{1,0:T(8,128)S(1)}, f32[64,128]{1,0:T(8,128)S(1)}, f32[64,128]{1,0:T(8,128)S(1)}, f32[64...) fusion(f32[64,128]{1,0:T(8,128)S(1)} %get-tuple-element.1734, ...), kind=kLoop, calls=%fused_computation.410.clone.1.clone | loop fusion | flops 71237632 | bytes 786432 | tf_op jit(solution)/shard_map/while/body/eval_jaxpr/reduce_sum | solution.py:71
  404.4 6.3 %multiply_reduce_fusion.42 = (f32[64,128]{1,0:T(8,128)S(1)}, f32[64,128]{1,0:T(8,128)S(1)}) fusion(f32[64,128]{1,0:T(8,128)S(1)} %get-tuple-element.1703, f32[64,128]{1,0:T(8,128)S(1)} %get-tuple-element.1704, f32[64,128]{1,0:T(8,128)S(1)} %get-tuple-element.1705, f32[64,128]{1,0:T(8,128)S(1)} %get-tuple-element.1706, ...), kind=kLoop, calls=%fused_computation.427.clone.1.clone | loop fusion | flops 18857984 | bytes 294912 | tf_op jit(solution)/shard_map/while/body/eval_jaxpr/reduce_sum | solution.py:71
  410.7 17.8 %multiply_reduce_fusion.43 = (f32[64,128]{1,0:T(8,128)S(1)}, f32[64,128]{1,0:T(8,128)S(1)}, f32[64,128]{1,0:T(8,128)S(1)}, f32[64,128]{1,0:T(8,128)S(1)}, f32[64...) fusion(f32[64,128]{1,0:T(8,128)S(1)} %get-tuple-element.1712, ...), kind=kLoop, calls=%fused_computation.407.clone.1.clone | loop fusion | flops 73334784 | bytes 884736 | tf_op jit(solution)/shard_map/while/body/eval_jaxpr/reduce_sum | solution.py:71
  428.5 17.9 %multiply_reduce_fusion.44 = (f32[64,128]{1,0:T(8,128)S(1)}, f32[64,128]{1,0:T(8,128)S(1)}, f32[64,128]{1,0:T(8,128)S(1)}, f32[64,128]{1,0:T(8,128)S(1)}, f32[64...) fusion(f32[64,128]{1,0:T(8,128)S(1)} %get-tuple-element.1734, ...), kind=kLoop, calls=%fused_computation.410.clone.1.clone | loop fusion | flops 71237632 | bytes 786432 | tf_op jit(solution)/shard_map/while/body/eval_jaxpr/reduce_sum | solution.py:71
  447.1 5.3 %copy.57 = f32[6,16384]{0,1:T(8,128)} copy(f32[6,16384]{1,0:T(8,128)S(1)} %pad_maximum_fusion.6) | data formatting | bytes 786432 | tf_op jit(solution)/shard_map/concatenate | solution.py:148
  452.4 6.2 %gather_fusion = f32[1024,6]{1,0:T(8,128)S(1)} fusion(f32[6,16384]{0,1:T(8,128)} %copy.57, s32[1024]{0:T(1024)S(1)} %broadcast_clamp_fusion), kind=kCustom, calls=%fused_computation | custom fusion | bytes 53248 | tf_op jit(solution)/shard_map/gather | solution.py:152
  (172 shorter events, 107.6 us)
Async XLA Ops:
  2.6 5.6 %collective-permute-start.1 = (f32[5,1,64,128]{3,2,1,0:T(8,128)S(1)}, f32[5,1,64,128]{3,2,1,0:T(8,128)S(1)}, u32[]{:S(2)}, u32[]{:S(2)}) collective-permute-start(f32[5,1,64,128]{3,2,1,0:T(8,128)S(1)} %get-tuple-element.770), channel_id=1, source_target_pairs={{4,0},{8,4},{12,8},{16,12},{20,16},{24,20},{28,24},{5,1},{9,5},{13... | collective-permute-start | bytes 491528 | tf_op jit(solution)/shard_map/ppermute | solution.py:24
  5.4 7.5 %collective-permute-start = (f32[5,1,64,128]{3,2,1,0:T(8,128)S(1)}, f32[5,1,64,128]{3,2,1,0:T(8,128)S(1)}, u32[]{:S(2)}, u32[]{:S(2)}) collective-permute-start(f32[5,1,64,128]{3,2,1,0:T(8,128)S(1)} %get-tuple-element.769), channel_id=1, source_target_pairs={{0,4},{4,8},{8,12},{12,16},{16,20},{20,24},{24,28},{1,5},{5,9},{9,... | collective-permute-start | bytes 491528 | tf_op jit(solution)/shard_map/ppermute | solution.py:23
  13.7 3.7 collective-permute-start.3
  16.1 5.6 %collective-permute-start.2 = (f32[5,4,1,128]{3,2,1,0:T(1,128)S(1)}, f32[5,4,1,128]{3,2,1,0:T(1,128)S(1)}, u32[]{:S(2)}, u32[]{:S(2)}) collective-permute-start(f32[5,4,1,128]{3,2,1,0:T(1,128)S(1)} %get-tuple-element.767), channel_id=1, source_target_pairs={{0,1},{1,2},{2,3},{4,5},{5,6},{6,7},{8,9},{9,10},{10,11},{12,13},{... | collective-permute-start | bytes 30728 | tf_op jit(solution)/shard_map/ppermute | solution.py:23
  22.7 95.9 %copy-start.3 = (f32[2,64,128]{2,1,0:T(8,128)S(1)}, f32[2,64,128]{2,1,0:T(8,128)}, u32[]{:S(2)}) copy-start(f32[2,64,128]{2,1,0:T(8,128)} %param.20) | copy-start | bytes 196612
  22.7 95.9 %copy-start.6 = (f32[2,64,128]{2,1,0:T(8,128)S(1)}, f32[2,64,128]{2,1,0:T(8,128)}, u32[]{:S(2)}) copy-start(f32[2,64,128]{2,1,0:T(8,128)} %param.21) | copy-start | bytes 196612
  22.7 95.9 %copy-start.7 = (s32[2,64]{1,0:T(2,128)S(1)}, s32[2,64]{1,0:T(2,128)}, u32[]{:S(2)}) copy-start(s32[2,64]{1,0:T(2,128)} %param.22) | copy-start | bytes 1540
  118.8 8.0 %collective-permute-start.9 = (f32[2,1,128]{2,1,0:T(1,128)S(1)}, f32[2,1,128]{2,1,0:T(1,128)S(1)}, u32[]{:S(2)}, u32[]{:S(2)}) collective-permute-start(f32[2,1,128]{2,1,0:T(1,128)S(1)} %get-tuple-element.802), channel_id=1, source_target_pairs={{1,0},{2,1},{3,2},{5,4},{6,5},{7,6},{9,8},{10,9},{11,10},{13,12},{... | collective-permute-start | bytes 3080 | tf_op jit(solution)/shard_map/ppermute | solution.py:24
  121.1 5.7 %collective-permute-start.8 = (f32[2,1,128]{2,1,0:T(1,128)S(1)}, f32[2,1,128]{2,1,0:T(1,128)S(1)}, u32[]{:S(2)}, u32[]{:S(2)}) collective-permute-start(f32[2,1,128]{2,1,0:T(1,128)S(1)} %get-tuple-element.801), channel_id=1, source_target_pairs={{0,1},{1,2},{2,3},{4,5},{5,6},{6,7},{8,9},{9,10},{10,11},{12,13},{... | collective-permute-start | bytes 3080 | tf_op jit(solution)/shard_map/ppermute | solution.py:23
  122.4 10.4 %collective-permute-start.5 = (f32[1,64,128]{2,1,0:T(8,128)S(1)}, f32[1,64,128]{2,1,0:T(8,128)S(1)}, u32[]{:S(2)}, u32[]{:S(2)}) collective-permute-start(f32[1,64,128]{2,1,0:T(8,128)S(1)} %get-tuple-element.800), channel_id=1, source_target_pairs={{4,0},{8,4},{12,8},{16,12},{20,16},{24,20},{28,24},{5,1},{9,5},{13... | collective-permute-start | bytes 98312 | tf_op jit(solution)/shard_map/ppermute | solution.py:24
  124.4 8.5 %collective-permute-start.4 = (f32[1,64,128]{2,1,0:T(8,128)S(1)}, f32[1,64,128]{2,1,0:T(8,128)S(1)}, u32[]{:S(2)}, u32[]{:S(2)}) collective-permute-start(f32[1,64,128]{2,1,0:T(8,128)S(1)} %get-tuple-element.799), channel_id=1, source_target_pairs={{0,4},{4,8},{8,12},{12,16},{16,20},{20,24},{24,28},{1,5},{5,9},{9,... | collective-permute-start | bytes 98312 | tf_op jit(solution)/shard_map/ppermute | solution.py:23
  126.8 11.9 %collective-permute-start.11 = (f32[1,66,128]{2,1,0:T(8,128)S(1)}, f32[1,66,128]{2,1,0:T(8,128)S(1)}, u32[]{:S(2)}, u32[]{:S(2)}) collective-permute-start(f32[1,66,128]{2,1,0:T(8,128)S(1)} %get-tuple-element.786), channel_id=1, source_target_pairs={{4,0},{8,4},{12,8},{16,12},{20,16},{24,20},{28,24},{5,1},{9,5},{13... | collective-permute-start | bytes 101384 | tf_op jit(solution)/shard_map/ppermute | solution.py:24
  130.9 7.9 %collective-permute-start.10 = (f32[1,66,128]{2,1,0:T(8,128)S(1)}, f32[1,66,128]{2,1,0:T(8,128)S(1)}, u32[]{:S(2)}, u32[]{:S(2)}) collective-permute-start(f32[1,66,128]{2,1,0:T(8,128)S(1)} %get-tuple-element.785), channel_id=1, source_target_pairs={{0,4},{4,8},{8,12},{12,16},{16,20},{20,24},{24,28},{1,5},{5,9},{9,... | collective-permute-start | bytes 101384 | tf_op jit(solution)/shard_map/ppermute | solution.py:23
  132.9 5.9 %collective-permute-start.7 = (f32[4,1,128]{2,1,0:T(1,128)S(1)}, f32[4,1,128]{2,1,0:T(1,128)S(1)}, u32[]{:S(2)}, u32[]{:S(2)}) collective-permute-start(f32[4,1,128]{2,1,0:T(1,128)S(1)} %get-tuple-element.776), channel_id=1, source_target_pairs={{1,0},{2,1},{3,2},{5,4},{6,5},{7,6},{9,8},{10,9},{11,10},{13,12},{... | collective-permute-start | bytes 6152 | tf_op jit(solution)/shard_map/ppermute | solution.py:24
  137.4 5.5 %collective-permute-start.6 = (f32[4,1,128]{2,1,0:T(1,128)S(1)}, f32[4,1,128]{2,1,0:T(1,128)S(1)}, u32[]{:S(2)}, u32[]{:S(2)}) collective-permute-start(f32[4,1,128]{2,1,0:T(1,128)S(1)} %get-tuple-element.775), channel_id=1, source_target_pairs={{0,1},{1,2},{2,3},{4,5},{5,6},{6,7},{8,9},{9,10},{10,11},{12,13},{... | collective-permute-start | bytes 6152 | tf_op jit(solution)/shard_map/ppermute | solution.py:23
  210.2 3.8 collective-permute-start.13
  212.6 5.5 %collective-permute-start.12 = (f32[2,1,128]{2,1,0:T(1,128)S(1)}, f32[2,1,128]{2,1,0:T(1,128)S(1)}, u32[]{:S(2)}, u32[]{:S(2)}) collective-permute-start(f32[2,1,128]{2,1,0:T(1,128)S(1)} %get-tuple-element.797), channel_id=1, source_target_pairs={{0,1},{1,2},{2,3},{4,5},{5,6},{6,7},{8,9},{9,10},{10,11},{12,13},{... | collective-permute-start | bytes 3080 | tf_op jit(solution)/shard_map/ppermute | solution.py:23
  218.1 4.6 collective-permute-start.15
  220.0 6.2 %collective-permute-start.14 = (f32[1,66,128]{2,1,0:T(8,128)S(1)}, f32[1,66,128]{2,1,0:T(8,128)S(1)}, u32[]{:S(2)}, u32[]{:S(2)}) collective-permute-start(f32[1,66,128]{2,1,0:T(8,128)S(1)} %get-tuple-element.783), channel_id=1, source_target_pairs={{0,4},{4,8},{8,12},{12,16},{16,20},{20,24},{24,28},{1,5},{5,9},{9,... | collective-permute-start | bytes 101384 | tf_op jit(solution)/shard_map/ppermute | solution.py:23
  275.4 3.4 collective-permute-start.17
  277.4 5.5 %collective-permute-start.16 = (f32[2,1,128]{2,1,0:T(1,128)S(1)}, f32[2,1,128]{2,1,0:T(1,128)S(1)}, u32[]{:S(2)}, u32[]{:S(2)}) collective-permute-start(f32[2,1,128]{2,1,0:T(1,128)S(1)} %get-tuple-element.795), channel_id=1, source_target_pairs={{0,1},{1,2},{2,3},{4,5},{5,6},{6,7},{8,9},{9,10},{10,11},{12,13},{... | collective-permute-start | bytes 3080 | tf_op jit(solution)/shard_map/ppermute | solution.py:23
  282.9 4.4 collective-permute-start.19
  284.9 6.2 %collective-permute-start.18 = (f32[1,66,128]{2,1,0:T(8,128)S(1)}, f32[1,66,128]{2,1,0:T(8,128)S(1)}, u32[]{:S(2)}, u32[]{:S(2)}) collective-permute-start(f32[1,66,128]{2,1,0:T(8,128)S(1)} %get-tuple-element.781), channel_id=1, source_target_pairs={{0,4},{4,8},{8,12},{12,16},{16,20},{20,24},{24,28},{1,5},{5,9},{9,... | collective-permute-start | bytes 101384 | tf_op jit(solution)/shard_map/ppermute | solution.py:23
  340.9 105.9 %copy-start.2 = (f32[2,64,128]{2,1,0:T(8,128)}, f32[2,64,128]{2,1,0:T(8,128)S(1)}, u32[]{:S(2)}) copy-start(f32[2,64,128]{2,1,0:T(8,128)S(1)} %get-tuple-element.771) | copy-start | bytes 196612
  340.9 3.5 collective-permute-start.21
  343.1 5.5 %collective-permute-start.20 = (f32[2,1,128]{2,1,0:T(1,128)S(1)}, f32[2,1,128]{2,1,0:T(1,128)S(1)}, u32[]{:S(2)}, u32[]{:S(2)}) collective-permute-start(f32[2,1,128]{2,1,0:T(1,128)S(1)} %get-tuple-element.793), channel_id=1, source_target_pairs={{0,1},{1,2},{2,3},{4,5},{5,6},{6,7},{8,9},{9,10},{10,11},{12,13},{... | collective-permute-start | bytes 3080 | tf_op jit(solution)/shard_map/ppermute | solution.py:23
  348.5 4.4 collective-permute-start.23
  350.5 6.2 %collective-permute-start.22 = (f32[1,66,128]{2,1,0:T(8,128)S(1)}, f32[1,66,128]{2,1,0:T(8,128)S(1)}, u32[]{:S(2)}, u32[]{:S(2)}) collective-permute-start(f32[1,66,128]{2,1,0:T(8,128)S(1)} %get-tuple-element.779), channel_id=1, source_target_pairs={{0,4},{4,8},{8,12},{12,16},{16,20},{20,24},{24,28},{1,5},{5,9},{9,... | collective-permute-start | bytes 101384 | tf_op jit(solution)/shard_map/ppermute | solution.py:23
  356.7 89.8 %copy-start = (f32[2,2,64,128]{3,2,1,0:T(8,128)S(1)}, f32[2,2,64,128]{3,2,1,0:T(8,128)}, u32[]{:S(2)}) copy-start(f32[2,2,64,128]{3,2,1,0:T(8,128)} %param.19) | copy-start | bytes 393220
  356.7 89.8 %copy-start.1 = (f32[2,2,64,128]{3,2,1,0:T(8,128)S(1)}, f32[2,2,64,128]{3,2,1,0:T(8,128)}, u32[]{:S(2)}) copy-start(f32[2,2,64,128]{3,2,1,0:T(8,128)} %param.18) | copy-start | bytes 393220
  458.8 5.0 %collective-permute-start.25 = (f32[6,8,1,128]{3,1,0,2:T(8,128)S(1)}, f32[6,8,1,128]{3,1,0,2:T(8,128)S(1)}, u32[]{:S(2)}, u32[]{:S(2)}) collective-permute-start(f32[6,8,1,128]{3,1,0,2:T(8,128)S(1)} %get-tuple-element.804), channel_id=1, source_target_pairs={{4,0},{8,4},{12,8},{16,12},{20,16},{24,20},{28,24},{5,1},{9,5},{13... | collective-permute-start | bytes 73736 | tf_op jit(solution)/shard_map/ppermute | solution.py:32
  460.8 6.0 %collective-permute-start.24 = (f32[6,8,1,128]{3,1,0,2:T(8,128)S(1)}, f32[6,8,1,128]{3,1,0,2:T(8,128)S(1)}, u32[]{:S(2)}, u32[]{:S(2)}) collective-permute-start(f32[6,8,1,128]{3,1,0,2:T(8,128)S(1)} %get-tuple-element.803), channel_id=1, source_target_pairs={{0,4},{4,8},{8,12},{12,16},{16,20},{20,24},{24,28},{1,5},{5,9},{9,... | collective-permute-start | bytes 73736 | tf_op jit(solution)/shard_map/ppermute | solution.py:32
  (5 other events, 179.0 us)
where the time goes:
time: 469 us; the launch traced here: 467 us
  other arithmetic  329 us (70%)
  starting transfers between devices  56 us (12%)
  waiting for transfers between devices  40.2 us (9%)
  local copies, waits for them, and re-layouts  20.8 us (4%)
  loops' own time  20 us (4%)
    reduce_sum x6, other arithmetic, density_terms(): jnp.sum(masses * kernel, -1)  89.8 us
    reduce_sum x8, other arithmetic, update_terms(): return jnp.sum(neighbor[3][:, None, :] * slope, -1)[None]  87 us
    reduce_sum x6, other arithmetic, force_terms(): jnp.sum(lifted * delta_x, -1)  84.1 us
    reduce_sum x4, other arithmetic, jacobi_terms(): jnp.sum(neighbor[2][:, None, :] * slope, -1)  61.3 us
    ppermute x12, waiting for transfers between devices, with_halo(): before = lax.ppermute(last, axis, up)  36.3 us
    ppermute x12, starting transfers between devices, with_halo(): after = lax.ppermute(initial, axis, down)  30.3 us
    ppermute x12, starting transfers between devices, with_halo(): before = lax.ppermute(last, axis, up)  21.4 us
    another operation x5, loops' own time, sweep(): totals = lax.map(one_column, jnp.arange(columns, dtype=jnp.int32))  20 us
  transfers between devices with their start and end apart: 26, of which 12 were waited for; matrix products, arithmetic and copies ran while one was open for 0% of the time, Pallas kernels for 0%

commit v1 on v0

v1 whole, which is shorter than its diff:
```python
import functools

import jax
import jax.numpy as jnp
import numpy as np
from jax import lax
from jax.experimental import pallas as pl
from jax.experimental.pallas import tpu as pltpu
from jax.sharding import PartitionSpec as P

ITERS = 3
TIME_STEP = 0.1
REST_DENSITY = 50.0
COMPRESSION = 2.0
RELAXATION = 0.5
GRAVITY = 1.0

HALO = 8
KP = 32
KD = 48
KE = 16
FAR = -64.0
SHIFTS = [(sx, sz) for sx in (-1, 0, 1) for sz in (-1, 0, 1)]
F32 = jnp.float32
BF16 = jnp.bfloat16
VMEM_LIMIT = 56 * 1024 * 1024


def split3(value):
    high = value.astype(BF16).astype(F32)
    rest = value - high
    mid = rest.astype(BF16).astype(F32)
    return [high, mid, rest - mid]


def left_six(parts):
    h, m, l = parts
    return [h, h, h, m, m, l]


def right_six(parts):
    h, m, l = parts
    return [h, m, l, h, m, h]


def position_rows(x, z):
    one, zero = jnp.ones_like(x), jnp.zeros_like(x)
    x, z = x - 0.5, z - 0.5
    xs, zs = split3(x), split3(z)
    square = x * x + z * z
    x2, z2 = [2.0 * v for v in xs], [2.0 * v for v in zs]
    ones = [one] * 3
    target = (
        left_six(x2) + x2 + ones + left_six(z2) + z2 + ones + split3(1.0 - square) + ones + [one, zero]
    )
    source = (
        right_six(xs) + ones + x2 + right_six(zs) + ones + z2 + ones + split3(-square) + [one, zero]
    )
    return target, source


def position_signs(sx, sz):
    return [1] * 6 + [sx] * 3 + [-sx] * 3 + [1] * 6 + [sz] * 3 + [-sz] * 3 + [1] * 6 + [-(sx * sx + sz * sz), 0]


def velocity_rows(x, z, vx, vz):
    one, zero = jnp.ones_like(x), jnp.zeros_like(x)
    x, z = x - 0.5, z - 0.5
    xs, zs, vxs, vzs = split3(x), split3(z), split3(vx), split3(vz)
    dots = split3(vx * x + vz * z)
    ones = [one] * 3
    pad = [zero] * 6
    minus = lambda rows: [-v for v in rows]
    target = dots + left_six(vxs) + left_six(vzs) + left_six(xs) + left_six(zs) + ones + vxs + vzs + ones + ones + pad
    source = (
        ones
        + minus(right_six(xs) + right_six(zs) + right_six(vxs) + right_six(vzs))
        + dots
        + ones
        + ones
        + vxs
        + vzs
        + pad
    )
    return target, source


def velocity_signs(sx, sz):
    return [1] * 30 + [-sx] * 3 + [-sz] * 3 + [sx] * 3 + [sz] * 3 + [0] * 6


def pressure_rows(weight, lifted, pressure):
    one, zero = jnp.ones_like(weight), jnp.zeros_like(weight)
    pad = [zero] * 7
    target = [one] * 3 + left_six(split3(pressure)) + pad
    source = split3(lifted) + [-v for v in right_six(split3(weight))] + pad
    return target, source


def sign_table(signs):
    table = np.asarray([signs(sx, sz) for sx, sz in SHIFTS], np.float32)
    return jnp.broadcast_to(jnp.asarray(table)[:, :, None], (*table.shape, 128)).astype(BF16)


def position_table(cut_first, cut_second):
    table = np.asarray([position_signs(sx, sz) for sx, sz in SHIFTS] * 2, np.float32)
    constant = np.arange(KP) == KP - 2
    sides = np.asarray([sx for sx, _ in SHIFTS] * 2)
    target = np.repeat([0, 1], 9)
    spots = lambda t, side: jnp.asarray(((target == t) & (sides == side))[:, None] & constant)
    table = jnp.where(spots(0, cut_first[1]) & cut_first[0], FAR, jnp.asarray(table))
    table = jnp.where(spots(1, cut_second[1]) & cut_second[0], FAR, table)
    return jnp.broadcast_to(table[:, :, None], (18, KP, 128)).astype(BF16)


def store_rows(rows, stage, dest, cell):
    count = len(rows)
    for index, value in enumerate(rows):
        stage[pl.ds(index, 8, stride=count), :] = value
    dest[pl.ds(cell, 8)] = stage[...].reshape(8, count, 128).astype(BF16)


def pair_tile(left, right, signs):
    return lax.dot_general(
        left, right * signs, (((0,), (0,)), ((), ())), preferred_element_type=F32
    )


def fold(total):
    return jnp.sum(total.T, axis=0, keepdims=True)


def density_kernel(
    low, high, left, own, right, posc, velc,
    out_r, out_l, out_w, out_density, out_source, out_send,
    stage_p, stage_d, vel_r, vel_l, acc,
):
    depth = own.shape[2]
    groups = depth // 8
    blocks = [(left, 0), (left, 1), (own, 0), (own, 1), (right, 0)]

    def prepare(group, carry):
        rows = pl.ds(pl.multiple_of(group * 8, 8), 8)
        for col, (ref, at) in enumerate(blocks):
            x, z, vx, vz = (ref[f, at, rows, :] for f in range(4))
            cell = pl.multiple_of(col * depth + group * 8, 8)
            target, source = position_rows(x, z)
            store_rows(source, stage_p, out_r, cell)
            if 1 <= col <= 3:
                store_rows(target, stage_p, out_l, pl.multiple_of((col - 1) * depth + group * 8, 8))
            if col >= 1:
                target, source = velocity_rows(x, z, vx, vz)
                store_rows(source, stage_d, vel_r, pl.multiple_of((col - 1) * depth + group * 8, 8))
                if 2 <= col <= 3:
                    store_rows(target, stage_d, vel_l, pl.multiple_of((col - 2) * depth + group * 8, 8))
        return carry

    lax.fori_loop(0, groups, prepare, 0)
    acc[...] = jnp.zeros_like(acc)

    def row(k, carry):
        for t in range(2):
            pos_l, vel_l_t = out_l[(t + 1) * depth + k], vel_l[t * depth + k]
            rho = jnp.zeros((128, 128), F32)
            div = jnp.zeros((128, 128), F32)
            for n, (sx, sz) in enumerate(SHIFTS):
                col = t + 1 + sx
                cell = col * depth + k + sz
                s = jnp.maximum(pair_tile(pos_l, out_r[cell + depth], posc[9 * t + n]), 0.0)
                d = pair_tile(vel_l_t, vel_r[cell], velc[n])
                ref, at = blocks[col + 1]
                q = s * s * ref[4, at, pl.ds(k + sz, 1), :]
                rho = rho + q * s
                div = div + q * d
            acc[0, t, pl.ds(k, 1), :] = fold(rho)
            acc[1, t, pl.ds(k, 1), :] = fold(div)
        return carry

    lax.fori_loop(low, high, row, 0)
    mass = own[4]
    alive = mass > 0.0
    density = jnp.where(alive, acc[0], 0.0)
    weight = jnp.where(alive, mass / jnp.where(alive, density, 1.0), 0.0)
    source = jnp.where(
        alive, (density - TIME_STEP * 6.0 * acc[1] - REST_DENSITY) / REST_DENSITY, 0.0
    )
    out_w[...] = weight
    out_density[...] = density / REST_DENSITY
    out_source[...] = source
    out_send[0:2] = weight
    out_send[2] = source[1]


def column_update(alive, pressure, source, pulled, diagonal):
    updated = (1.0 - RELAXATION) * pressure + RELAXATION * (source + 6.0 * pulled) / diagonal
    return jnp.where(alive, updated, 0.0)


def jacobi_rows(low, high, first_col, feat_r, feat_l, posc, wide_u, acc, depth):
    def row(k, carry):
        for t in range(2):
            pos_l = feat_l[(first_col + t) * depth + k]
            total = jnp.zeros((128, 128), F32)
            for n, (sx, sz) in enumerate(SHIFTS):
                col = t + 1 + sx
                cell = (first_col + col) * depth + k + sz
                s = jnp.maximum(pair_tile(pos_l, feat_r[cell], posc[9 * t + n]), 0.0)
                total = total + s * s * wide_u[col, pl.ds(k + sz, 1), :]
            acc[t, pl.ds(k, 1), :] = fold(total)
        return carry

    lax.fori_loop(low, high, row, 0)


def sweep1_kernel(
    low, high, feat_r, feat_l, left, own, recv, weight_own, source_own, posc,
    out_p, out_diag, out_send, wide_w, wide_u, acc,
):
    depth = weight_own.shape[1]
    start_l = jnp.where(left[4] > 0.0, left[5], 0.0)
    start_o = jnp.where(own[4] > 0.0, own[5], 0.0)
    wide_w[0:2] = recv[0:2]
    wide_w[2:4] = weight_own[...]
    wide_u[0:2] = recv[0:2] * start_l
    wide_u[2:4] = weight_own[...] * start_o
    acc[...] = jnp.zeros_like(acc)

    def row(k, carry):
        for t in range(2):
            pos_l = feat_l[t * depth + k]
            total_w = jnp.zeros((128, 128), F32)
            total_u = jnp.zeros((128, 128), F32)
            for n, (sx, sz) in enumerate(SHIFTS):
                col = t + 1 + sx
                s = jnp.maximum(pair_tile(pos_l, feat_r[col * depth + k + sz], posc[9 * t + n]), 0.0)
                q = s * s
                total_w = total_w + q * wide_w[col, pl.ds(k + sz, 1), :]
                total_u = total_u + q * wide_u[col, pl.ds(k + sz, 1), :]
            acc[0, t, pl.ds(k, 1), :] = fold(total_w)
            acc[1, t, pl.ds(k, 1), :] = fold(total_u)
        return carry

    lax.fori_loop(low, high, row, 0)
    diagonal = COMPRESSION + 6.0 * acc[0]
    out_diag[...] = diagonal
    below = column_update(left[4, 1] > 0.0, start_l[1], recv[2], acc[1, 0], diagonal[0])
    here = column_update(own[4, 0] > 0.0, start_o[0], source_own[0], acc[1, 1], diagonal[1])
    out_p[0] = below
    out_p[1] = here
    out_send[0] = below
    out_send[1] = here
    out_send[2] = weight_own[0]
    out_send[3] = diagonal[0]


def sweep2_kernel(
    low, high, feat_r, feat_l, own, recv1, recv2, weight_own, source_own, diag, p1, posc,
    out_p, wide_u, acc,
):
    depth = weight_own.shape[1]
    wide_u[0] = recv1[1] * p1[0]
    wide_u[1] = weight_own[0] * p1[1]
    wide_u[2] = weight_own[1] * recv2[0]
    wide_u[3] = recv2[2] * recv2[1]
    acc[...] = jnp.zeros_like(acc)
    jacobi_rows(low, high, 1, feat_r, feat_l, posc, wide_u, acc, depth)
    out_p[0] = column_update(own[4, 0] > 0.0, p1[1], source_own[0], acc[0], diag[1])
    out_p[1] = column_update(own[4, 1] > 0.0, recv2[0], source_own[1], acc[1], recv2[3])


def sweep3_kernel(
    low, high, feat_r, feat_l, left, own, recv1, recv3, weight_own, source_own, diag, p2, posc,
    out_p, wide_u, acc,
):
    depth = weight_own.shape[1]
    wide_u[0:2] = recv1[0:2] * recv3[...]
    wide_u[2:4] = weight_own[...] * p2[...]
    acc[...] = jnp.zeros_like(acc)
    jacobi_rows(low, high, 0, feat_r, feat_l, posc, wide_u, acc, depth)
    out_p[0] = column_update(left[4, 1] > 0.0, recv3[1], recv1[2], acc[0], diag[0])
    out_p[1] = column_update(own[4, 0] > 0.0, p2[0], source_own[0], acc[1], diag[1])


def force_kernel(
    low, high, feat_r, feat_l, own, recv1, recv2, recv4, left, right, weight_own, p3, posc,
    out_pressure, out_acc, out_velocity, out_offsets,
    wide_p, wide_w, wide_x, wide_z, pres_r, pres_l, stage, acc,
):
    depth = weight_own.shape[1]
    wide_p[0:2] = p3[...]
    wide_p[2:4] = recv4[...]
    wide_w[0] = recv1[1]
    wide_w[1:3] = weight_own[...]
    wide_w[3] = recv2[2]
    for field, wide in ((0, wide_x), (1, wide_z)):
        wide[0] = left[field, 1] - 0.5
        wide[1:3] = own[field] - 0.5
        wide[3] = right[field, 0] - 0.5

    def prepare(group, carry):
        rows = pl.ds(pl.multiple_of(group * 8, 8), 8)
        for col in range(4):
            pressure, weight = wide_p[col, rows, :], wide_w[col, rows, :]
            target, source = pressure_rows(weight, weight * pressure, pressure)
            store_rows(source, stage, pres_r, pl.multiple_of(col * depth + group * 8, 8))
            if 1 <= col <= 2:
                store_rows(target, stage, pres_l, pl.multiple_of((col - 1) * depth + group * 8, 8))
        return carry

    lax.fori_loop(0, depth // 8, prepare, 0)

    def row(k, carry):
        for t in range(2):
            pos_l, pres_l_t = feat_l[(t + 1) * depth + k], pres_l[t * depth + k]
            plain = jnp.zeros((128, 128), F32)
            by_x = jnp.zeros((128, 128), F32)
            by_z = jnp.zeros((128, 128), F32)
            for n, (sx, sz) in enumerate(SHIFTS):
                col = t + 1 + sx
                s = jnp.maximum(pair_tile(pos_l, feat_r[(col + 1) * depth + k + sz], posc[9 * t + n]), 0.0)
                e = lax.dot_general(
                    pres_l_t, pres_r[col * depth + k + sz], (((0,), (0,)), ((), ())),
                    preferred_element_type=F32,
                )
                g = s * s * e
                plain = plain + g
                by_x = by_x + g * (wide_x[col, pl.ds(k + sz, 1), :] + float(sx))
                by_z = by_z + g * (wide_z[col, pl.ds(k + sz, 1), :] + float(sz))
            acc[0, t, pl.ds(k, 1), :] = fold(plain)
            acc[1, t, pl.ds(k, 1), :] = fold(by_x)
            acc[2, t, pl.ds(k, 1), :] = fold(by_z)
        return carry

    lax.fori_loop(low, high, row, 0)
    inner = slice(low, high)
    alive = own[4, :, inner] > 0.0
    out_pressure[0] = p3[1, inner]
    out_pressure[1] = recv4[0, inner]
    for axis, wide, pull in ((0, wide_x, 0.0), (1, wide_z, GRAVITY)):
        force = 6.0 * (wide[1:3, inner] * acc[0, :, inner] - acc[axis + 1, :, inner])
        force = jnp.where(alive, force, 0.0)
        velocity = jnp.where(alive, own[axis + 2, :, inner] + TIME_STEP * (force - pull), 0.0)
        out_acc[axis] = force
        out_velocity[axis] = velocity
        out_offsets[axis] = jnp.where(alive, own[axis, :, inner] + TIME_STEP * velocity, 0.0)


def local_call(kernel, out_shapes, scratch, *operands):
    vmem = pl.BlockSpec(memory_space=pltpu.VMEM)
    return pl.pallas_call(
        kernel,
        out_shape=[jax.ShapeDtypeStruct(shape, dtype) for shape, dtype in out_shapes],
        in_specs=[vmem] * len(operands),
        out_specs=[vmem] * len(out_shapes),
        scratch_shapes=[pltpu.VMEM(shape, dtype) for shape, dtype in scratch],
        compiler_params=pltpu.CompilerParams(vmem_limit_bytes=VMEM_LIMIT),
    )(*operands)


def from_behind(block, axis, distance):
    devices = range(lax.axis_size(axis))
    route = [(i - distance, i) for i in devices if i - distance in devices]
    return lax.ppermute(block, axis, route)


def around(block, axis, distance):
    peers = lax.axis_size(axis)
    return lax.ppermute(block, axis, [(i, (i + distance) % peers) for i in range(peers)])


def per_device(
    offsets, velocity, particle_mass, pressure_start, counts, leaving_slot, leaving_count, leaving_side
):
    cells, slots = counts.shape[1], offsets.shape[-1]
    alive = jnp.arange(slots, dtype=jnp.int32)[None, None, :] < counts[:, :, None]
    live_mass = jnp.where(alive, particle_mass, 0.0)
    base = jnp.concatenate([offsets, velocity, live_mass[None], pressure_start[None]], 0)
    above = from_behind(base[:, :, cells - HALO :], "slab", 1)
    below = from_behind(base[:, :, :HALO], "slab", -1)
    own = jnp.concatenate([above, base, below], 2)
    left = around(own, "col", 1)
    right = around(own[:5, :1], "col", -1)
    depth = cells + 2 * HALO
    first = lax.axis_index("col") == 0
    last = lax.axis_index("col") == lax.axis_size("col") - 1
    here = position_table((first, -1), (last, 1))
    back = position_table((first, 1), (first, -1))
    velc = sign_table(velocity_signs)
    plane = (2, depth, slots)

    def rows(level):
        reach = ITERS + 2 - level
        return HALO - reach, HALO + cells + reach

    feat_r, feat_l, weight, density_ratio, source, send1 = local_call(
        functools.partial(density_kernel, *rows(1)),
        [
            ((5 * depth, KP, slots), BF16),
            ((3 * depth, KP, slots), BF16),
            (plane, F32),
            (plane, F32),
            (plane, F32),
            ((3, depth, slots), F32),
        ],
        [
            ((8 * KP, slots), F32),
            ((8 * KD, slots), F32),
            ((4 * depth, KD, slots), BF16),
            ((2 * depth, KD, slots), BF16),
            ((2, 2, depth, slots), F32),
        ],
        left, own, right, here, velc,
    )
    recv1 = around(send1, "col", 1)
    p1, diag, send2 = local_call(
        functools.partial(sweep1_kernel, *rows(2)),
        [(plane, F32), (plane, F32), ((4, depth, slots), F32)],
        [((4, depth, slots), F32), ((4, depth, slots), F32), ((2, 2, depth, slots), F32)],
        feat_r, feat_l, left, own, recv1, weight, source, back,
    )
    recv2 = around(send2, "col", -1)
    (p2,) = local_call(
        functools.partial(sweep2_kernel, *rows(3)),
        [(plane, F32)],
        [((4, depth, slots), F32), (plane, F32)],
        feat_r, feat_l, own, recv1, recv2, weight, source, diag, p1, here,
    )
    recv3 = around(p2, "col", 1)
    (p3,) = local_call(
        functools.partial(sweep3_kernel, *rows(4)),
        [(plane, F32)],
        [((4, depth, slots), F32), (plane, F32)],
        feat_r, feat_l, left, own, recv1, recv3, weight, source, diag, p2, back,
    )
    recv4 = around(p3, "col", -1)
    inner = (2, cells, slots)
    pressure, acceleration, velocity_new, offsets_new = local_call(
        functools.partial(force_kernel, *rows(5)),
        [(inner, F32), ((2, *inner), F32), ((2, *inner), F32), ((2, *inner), F32)],
        [((4, depth, slots), F32)] * 4
        + [
            ((4 * depth, KE, slots), BF16),
            ((2 * depth, KE, slots), BF16),
            ((8 * KE, slots), F32),
            ((3, *plane), F32),
        ],
        feat_r, feat_l, own, recv1, recv2, recv4, left, right, weight, p3, here,
    )
    density_ratio = density_ratio[:, HALO : HALO + cells]
    state = jnp.concatenate([offsets_new, velocity_new, pressure[None], live_mass[None]], 0).reshape(6, -1)
    block_rows = leaving_slot.shape[0]
    blocks = state[:, leaving_slot.reshape(-1)].reshape(6, block_rows, 1, slots)
    filled = jnp.arange(slots, dtype=jnp.int32)[None, None, :] < leaving_count[:, :, None]
    upward = jnp.where(filled & (leaving_side[:, :, None] == 1), blocks, 0.0)
    downward = jnp.where(filled & (leaving_side[:, :, None] == 0), blocks, 0.0)
    arrived = jnp.stack([from_behind(upward, "col", 1), from_behind(downward, "col", -1)])
    return (density_ratio, pressure, acceleration, velocity_new, offsets_new, arrived)


def solution(mesh):
    return jax.shard_map(
        per_device,
        mesh=mesh,
        in_specs=(
            P(None, "col", "slab", None),
            P(None, "col", "slab", None),
            P("col", "slab", None),
            P("col", "slab", None),
            P("col", "slab"),
            P("col", "slab", None),
            P("col", "slab"),
            P("col", "slab"),
        ),
        out_specs=(
            P("col", "slab", None),
            P("col", "slab", None),
            P(None, "col", "slab", None),
            P(None, "col", "slab", None),
            P(None, "col", "slab", None),
            P(None, None, "col", "slab", None),
        ),
        check_vma=False,
    )
```

time: 469 us -> 278 us (0.59)
  other arithmetic: 329 us -> 7.11 us
  Pallas kernels: 0 us -> 208 us
  starting transfers between devices: 56 us -> 12.7 us
  loops' own time: 20 us -> 0 us
  waiting for transfers between devices: 40.2 us -> 30.3 us
    reduce_sum x24 -> x0, other arithmetic: 322 us -> none  [the longest x6 89.8 us: density_terms(): jnp.sum(masses * kernel, -1)]
    pallas_call x0 -> x5, Pallas kernels: none -> 208 us  [local_call(): pl.pallas_call(kernel, out_shape=[jax.ShapeDtypeStruct(shape, dtype) for...]
    ppermute x24 -> x6, starting transfers between devices: 51.7 us -> 2.65 us  [around(): lax.ppermute(block, axis, [(i, (i + distance) % peers) for i in range(pee...]
    another operation x5 -> x0, loops' own time: 20 us -> none  [sweep(): totals = lax.map(one_column, jnp.arange(columns, dtype=jnp.int32))]
    ppermute x24 -> x6, waiting for transfers between devices: 37.2 us -> 22.1 us  [around(): lax.ppermute(block, axis, [(i, (i + distance) % peers) for i in range(pee...]
    dynamic_slice x10 -> x0, local copies, waits for them, and re-layouts: 5.86 us -> none  [sweep(): totals = lax.map(one_column, jnp.arange(columns, dtype=jnp.int32))]
    ppermute x2 -> x4, starting transfers between devices: 4.33 us -> 10.1 us  [from_behind(): return lax.ppermute(block, axis, route)]
    ppermute x2 -> x4, waiting for transfers between devices: 2.94 us -> 8.15 us  [from_behind(): return lax.ppermute(block, axis, route)]
  transfers between devices with their start and end apart: 26 -> 10, of which waited for: 12 -> 9; matrix products, arithmetic and copies ran while one was open for 0% -> 1% of each run, Pallas kernels for 0% -> 0%
where the time goes in v1:
time: 278 us
  Pallas kernels  208 us (75%)
  waiting for transfers between devices  30.3 us (11%)
  local copies, waits for them, and re-layouts  18.6 us (7%)
  starting transfers between devices  12.7 us (5%)
  other arithmetic  7.11 us (3%)
    pallas_call x5, Pallas kernels, local_call(): pl.pallas_call(kernel, out_shape=[jax.ShapeDtypeStruct(shape, dtype) for...  208 us
    ppermute x6, waiting for transfers between devices, around(): lax.ppermute(block, axis, [(i, (i + distance) % peers) for i in range(pee...  22.1 us
    ppermute x4, starting transfers between devices, from_behind(): return lax.ppermute(block, axis, route)  10.1 us
    ppermute x4, waiting for transfers between devices, from_behind(): return lax.ppermute(block, axis, route)  8.15 us
    concatenate x2, local copies, waits for them, and re-layouts, per_device(): jnp.concatenate([offsets_new, velocity_new, pressure[None], live_mass[Non...  6.5 us
    gather x1, local copies, waits for them, and re-layouts, per_device(): blocks = state[:, leaving_slot.reshape(-1)].reshape(6, block_rows, 1, slots)  6.19 us
  transfers between devices with their start and end apart: 10, of which 9 were waited for; matrix products, arithmetic and copies ran while one was open for 1% of the time, Pallas kernels for 0%

profile of v1, /device:TPU:28, one launch (start us, length us, event | category | flops | bytes accessed | tf_op | source)
XLA Modules:
  0.0 277.8 jit_solution(3542953846135171546)
XLA Ops:
  0.6 0.9 fusion.3
  1.6 0.8 pad_maximum_fusion.5
  2.4 2.4 collective-permute-start.1
  4.8 1.3 collective-permute-start
  6.5 4.3 %collective-permute-done = f32[6,2,8,128]{3,2,1,0:T(8,128)S(1)} collective-permute-done((f32[6,2,8,128]{3,2,1,0:T(8,128)S(1)}, f32[6,2,8,128]{3,2,1,0:T(8,128)S(1)}, u32[]{:S(2)}, u32[]{:S(2)}) %collective-permute-start) | collective-permute-done | bytes 49184 | tf_op jit(solution)/shard_map/ppermute | solution.py:363
  10.7 1.0 pad_maximum_fusion.1.own
  11.9 1.0 fusion
  12.9 2.6 collective-permute-start.3
  15.5 0.8 select_convert_fusion
  16.3 4.8 %collective-permute-done.3.right = f32[5,1,80,128]{3,2,1,0:T(8,128)S(1)} collective-permute-done((f32[5,1,80,128]{3,2,1,0:T(8,128)S(1)}, f32[5,1,80,128]{3,2,1,0:T(8,128)S(1)}, u32[]{:S(2)}, u32[]{:S(2)}) %collective-permute-start.3) | collective-permute-done | bytes 204832 | tf_op jit(solution)/shard_map/ppermute | solution.py:368
  21.0 2.2 collective-permute-done.2.left
  23.2 0.9 broadcast_in_dim.61.posc
  24.1 1.5 broadcast_in_dim.62.velc
  25.5 56.2 %shard_map.190 = (bf16[400,32,128]{2,1,0:T(8,128)(2,1)}, bf16[240,32,128]{2,1,0:T(8,128)(2,1)}, f32[2,80,128]{2,1,0:T(8,128)}, f32[2,80,128]{2,1,0:T(8,128)}, f3...) custom-call(f32[6,2,80,128]{3,2,1,0:T(8,128)} %copy-done.1, f32[6,2,80,128]{3,2,1,0:T(8,128)} %copy-done, ...), custom_call_target="tpu_custom_call" | custom-call | tf_op jit(solution)/shard_map/pallas_call | solution.py:350
  81.8 0.7 compare_select_fusion
  82.5 4.7 %collective-permute-done.4.recv.recv1 = f32[3,80,128]{2,1,0:T(8,128)S(1)} collective-permute-done((f32[3,80,128]{2,1,0:T(8,128)}, f32[3,80,128]{2,1,0:T(8,128)S(1)}, u32[]{:S(2)}, u32[]{:S(2)}) %collective-permute-start.4) | collective-permute-done | bytes 122912 | tf_op jit(solution)/shard_map/ppermute | solution.py:368
  87.2 0.8 broadcast_in_dim.63.posc
  88.0 39.5 %shard_map.191 = (f32[2,80,128]{2,1,0:T(8,128)}, f32[2,80,128]{2,1,0:T(8,128)}, f32[4,80,128]{2,1,0:T(8,128)}) custom-call(bf16[400,32,128]{2,1,0:T(8,128)(2,1)} %get-tuple-element.20.feat_r, bf16[240,32,128]{2,1,0:T(8,128)(2,1)} %get-tuple-element.21.feat_l, f32[6,2,80,128]{3,2,1,0:T(8,128)} %copy-done.1, f32[6,2,80,128]{3,2,1,0:T(8,128)} %copy-done, ...), custom_call_target="tpu_custom_call" | custom-call | tf_op jit(solution)/shard_map/pallas_call | solution.py:350
  127.5 3.1 %collective-permute-done.5.recv2 = f32[4,80,128]{2,1,0:T(8,128)S(1)} collective-permute-done((f32[4,80,128]{2,1,0:T(8,128)}, f32[4,80,128]{2,1,0:T(8,128)S(1)}, u32[]{:S(2)}, u32[]{:S(2)}) %collective-permute-start.5) | collective-permute-done | bytes 163872 | tf_op jit(solution)/shard_map/ppermute | solution.py:368
  130.7 0.7 copy-done.4
  131.4 33.2 %shard_map.192.p2 = f32[2,80,128]{2,1,0:T(8,128)} custom-call(bf16[400,32,128]{2,1,0:T(8,128)(2,1)} %get-tuple-element.20.feat_r, bf16[240,32,128]{2,1,0:T(8,128)(2,1)} %get-tuple-element.21.feat_l, f32[6,2,80,128]{3,2,1,0:T(8,128)} %copy-done, f32[3,80,128]{2,1,0:T(8,128)} %copy-done.2, f32[4,80,128]{2,1,0:T(8,128)} %copy-done.4, ...), custom_call_target="tpu_custom_call" | custom-call | tf_op jit(solution)/shard_map/pallas_call | solution.py:350
  164.6 5.0 %collective-permute-done.6.recv3 = f32[2,80,128]{2,1,0:T(8,128)S(1)} collective-permute-done((f32[2,80,128]{2,1,0:T(8,128)}, f32[2,80,128]{2,1,0:T(8,128)S(1)}, u32[]{:S(2)}, u32[]{:S(2)}) %collective-permute-start.6) | collective-permute-done | bytes 81952 | tf_op jit(solution)/shard_map/ppermute | solution.py:368
  170.3 32.5 %shard_map.193.p3 = f32[2,80,128]{2,1,0:T(8,128)} custom-call(bf16[400,32,128]{2,1,0:T(8,128)(2,1)} %get-tuple-element.20.feat_r, bf16[240,32,128]{2,1,0:T(8,128)(2,1)} %get-tuple-element.21.feat_l, f32[6,2,80,128]{3,2,1,0:T(8,128)} %copy-done.1, f32[6,2,80,128]{3,2,1,0:T(8,128)} %copy-done, f32[3,80,128]{2,1,0:T(8,128)} %copy-done.2, ...), custom_call_target="tpu_custom_call" | custom-call | tf_op jit(solution)/shard_map/pallas_call | solution.py:350
  202.9 2.3 collective-permute-done.7.recv4
  205.8 46.8 %shard_map.194 = (f32[2,64,128]{2,1,0:T(8,128)}, f32[2,2,64,128]{3,2,1,0:T(8,128)}, f32[2,2,64,128]{3,2,1,0:T(8,128)}, f32[2,2,64,128]{3,2,1,0:T(8,128)}) custom-call(bf16[400,32,128]{2,1,0:T(8,128)(2,1)} %get-tuple-element.20.feat_r, bf16[240,32,128]{2,1,0:T(8,128)(2,1)} %get-tuple-element.21.feat_l, f32[6,2,80,128]{3,2,1,0:T(8,128)} %copy-done, ...), custom_call_target="tpu_custom_call" | custom-call | tf_op jit(solution)/shard_map/pallas_call | solution.py:350
  252.5 1.2 copy_bitcast_fusion
  253.7 1.1 pad_maximum_fusion
  254.8 5.3 %copy.28 = f32[6,16384]{0,1:T(8,128)} copy(f32[6,16384]{1,0:T(8,128)S(1)} %pad_maximum_fusion) | data formatting | bytes 786432 | tf_op jit(solution)/shard_map/concatenate | solution.py:450
  260.1 6.2 %gather_fusion = f32[1024,6]{1,0:T(8,128)S(1)} fusion(f32[6,16384]{0,1:T(8,128)} %copy.28, s32[1024]{0:T(1024)S(1)} %broadcast_clamp_fusion), kind=kCustom, calls=%fused_computation | custom fusion | bytes 53248 | tf_op jit(solution)/shard_map/gather | solution.py:452
  266.5 4.5 %collective-permute-start.9 = (f32[6,8,1,128]{3,1,0,2:T(8,128)S(1)}, f32[6,8,1,128]{3,1,0,2:T(8,128)S(1)}, u32[]{:S(2)}, u32[]{:S(2)}) collective-permute-start(f32[6,8,1,128]{3,1,0,2:T(8,128)S(1)} %get-tuple-element.35), channel_id=1, source_target_pairs={{4,0},{8,4},{12,8},{16,12},{20,16},{24,20},{28,24},{5,1},{9,5},{13... | collective-permute-start | bytes 73736 | tf_op jit(solution)/shard_map/ppermute | solution.py:363
  271.0 1.9 collective-permute-start.8
  273.6 3.5 %collective-permute-done.8 = f32[6,8,1,128]{3,1,0,2:T(8,128)S(1)} collective-permute-done((f32[6,8,1,128]{3,1,0,2:T(8,128)S(1)}, f32[6,8,1,128]{3,1,0,2:T(8,128)S(1)}, u32[]{:S(2)}, u32[]{:S(2)}) %collective-permute-start.8) | collective-permute-done | bytes 24608 | tf_op jit(solution)/shard_map/ppermute | solution.py:363
  (34 shorter events, 3.4 us)
Async XLA Ops:
  2.4 162.2 %copy-start.9 = (s32[8,1]{0,1:T(1,128)S(1)}, s32[8,1]{0,1:T(1,128)}, u32[]{:S(2)}) copy-start(s32[8,1]{0,1:T(1,128)} %param.22) | copy-start | bytes 100
  2.4 4.1 %collective-permute-start.1 = (f32[6,2,8,128]{3,2,1,0:T(8,128)S(1)}, f32[6,2,8,128]{3,2,1,0:T(8,128)S(1)}, u32[]{:S(2)}, u32[]{:S(2)}) collective-permute-start(f32[6,2,8,128]{3,2,1,0:T(8,128)S(1)} %get-tuple-element.33), channel_id=1, source_target_pairs={{1,0},{2,1},{3,2},{5,4},{6,5},{7,6},{9,8},{10,9},{11,10},{13,12},{... | collective-permute-start | bytes 147464 | tf_op jit(solution)/shard_map/ppermute | solution.py:363
  4.8 6.0 %collective-permute-start = (f32[6,2,8,128]{3,2,1,0:T(8,128)S(1)}, f32[6,2,8,128]{3,2,1,0:T(8,128)S(1)}, u32[]{:S(2)}, u32[]{:S(2)}) collective-permute-start(f32[6,2,8,128]{3,2,1,0:T(8,128)S(1)} %get-tuple-element.32), channel_id=1, source_target_pairs={{0,1},{1,2},{2,3},{4,5},{5,6},{6,7},{8,9},{9,10},{10,11},{12,13},{... | collective-permute-start | bytes 147464 | tf_op jit(solution)/shard_map/ppermute | solution.py:363
  11.8 13.7 %copy-start = (f32[6,2,80,128]{3,2,1,0:T(8,128)}, f32[6,2,80,128]{3,2,1,0:T(8,128)S(1)}, u32[]{:S(2)}) copy-start(f32[6,2,80,128]{3,2,1,0:T(8,128)S(1)} %pad_maximum_fusion.1.own) | copy-start | bytes 1474564
  11.8 11.4 %collective-permute-start.2 = (f32[6,2,80,128]{3,2,1,0:T(8,128)S(1)}, f32[6,2,80,128]{3,2,1,0:T(8,128)S(1)}, u32[]{:S(2)}, u32[]{:S(2)}) collective-permute-start(f32[6,2,80,128]{3,2,1,0:T(8,128)S(1)} %pad_maximum_fusion.1.own), channel_id=1, source_target_pairs={{0,4},{4,8},{8,12},{12,16},{16,20},{20,24},{24,28},{28,0},{1,5},{5... | collective-permute-start | bytes 1474568 | tf_op jit(solution)/shard_map/ppermute | solution.py:368
  12.9 8.1 %collective-permute-start.3 = (f32[5,1,80,128]{3,2,1,0:T(8,128)S(1)}, f32[5,1,80,128]{3,2,1,0:T(8,128)S(1)}, u32[]{:S(2)}, u32[]{:S(2)}) collective-permute-start(f32[5,1,80,128]{3,2,1,0:T(8,128)S(1)} %slice.18), channel_id=1, source_target_pairs={{0,28},{4,0},{8,4},{12,8},{16,12},{20,16},{24,20},{28,24},{1,29},{... | collective-permute-start | bytes 614408 | tf_op jit(solution)/shard_map/ppermute | solution.py:368
  21.0 4.5 %copy-start.3 = (f32[5,1,80,128]{3,2,1,0:T(8,128)}, f32[5,1,80,128]{3,2,1,0:T(8,128)S(1)}, u32[]{:S(2)}) copy-start(f32[5,1,80,128]{3,2,1,0:T(8,128)S(1)} %collective-permute-done.3.right) | copy-start | bytes 614404
  23.2 2.3 copy-start.1
  81.8 5.4 %collective-permute-start.4 = (f32[3,80,128]{2,1,0:T(8,128)}, f32[3,80,128]{2,1,0:T(8,128)S(1)}, u32[]{:S(2)}, u32[]{:S(2)}) collective-permute-start(f32[3,80,128]{2,1,0:T(8,128)} %get-tuple-element.22), channel_id=1, source_target_pairs={{0,4},{4,8},{8,12},{12,16},{16,20},{20,24},{24,28},{28,0},{1,5},{5... | collective-permute-start | bytes 368648 | tf_op jit(solution)/shard_map/ppermute | solution.py:368
  87.2 0.8 copy-start.2
  127.5 75.3 %copy-start.8 = (s32[8,1]{0,1:T(1,128)S(1)}, s32[8,1]{0,1:T(1,128)}, u32[]{:S(2)}) copy-start(s32[8,1]{0,1:T(1,128)} %param.21) | copy-start | bytes 100
  127.5 3.2 %collective-permute-start.5 = (f32[4,80,128]{2,1,0:T(8,128)}, f32[4,80,128]{2,1,0:T(8,128)S(1)}, u32[]{:S(2)}, u32[]{:S(2)}) collective-permute-start(f32[4,80,128]{2,1,0:T(8,128)} %get-tuple-element.25), channel_id=1, source_target_pairs={{0,28},{4,0},{8,4},{12,8},{16,12},{20,16},{24,20},{28,24},{1,29},{... | collective-permute-start | bytes 491528 | tf_op jit(solution)/shard_map/ppermute | solution.py:368
  130.7 0.7 copy-start.4
  164.6 5.0 %collective-permute-start.6 = (f32[2,80,128]{2,1,0:T(8,128)}, f32[2,80,128]{2,1,0:T(8,128)S(1)}, u32[]{:S(2)}, u32[]{:S(2)}) collective-permute-start(f32[2,80,128]{2,1,0:T(8,128)} %shard_map.192.p2), channel_id=1, source_target_pairs={{0,4},{4,8},{8,12},{12,16},{16,20},{20,24},{24,28},{28,0},{1,5},{5... | collective-permute-start | bytes 245768 | tf_op jit(solution)/shard_map/ppermute | solution.py:368
  169.7 0.6 copy-start.6
  202.8 2.4 collective-permute-start.7
  202.9 70.1 %copy-start.7 = (f32[2,80,128]{2,1,0:T(8,128)S(1)}, f32[2,80,128]{2,1,0:T(8,128)}, u32[]{:S(2)}) copy-start(f32[2,80,128]{2,1,0:T(8,128)} %get-tuple-element.19) | copy-start | bytes 245764
  205.2 0.6 copy-start.5
  266.5 7.1 %collective-permute-start.9 = (f32[6,8,1,128]{3,1,0,2:T(8,128)S(1)}, f32[6,8,1,128]{3,1,0,2:T(8,128)S(1)}, u32[]{:S(2)}, u32[]{:S(2)}) collective-permute-start(f32[6,8,1,128]{3,1,0,2:T(8,128)S(1)} %get-tuple-element.35), channel_id=1, source_target_pairs={{4,0},{8,4},{12,8},{16,12},{20,16},{24,20},{28,24},{5,1},{9,5},{13... | collective-permute-start | bytes 73736 | tf_op jit(solution)/shard_map/ppermute | solution.py:363
  271.0 6.0 %collective-permute-start.8 = (f32[6,8,1,128]{3,1,0,2:T(8,128)S(1)}, f32[6,8,1,128]{3,1,0,2:T(8,128)S(1)}, u32[]{:S(2)}, u32[]{:S(2)}) collective-permute-start(f32[6,8,1,128]{3,1,0,2:T(8,128)S(1)} %get-tuple-element.34), channel_id=1, source_target_pairs={{0,4},{4,8},{8,12},{12,16},{16,20},{20,24},{24,28},{1,5},{5,9},{9,... | collective-permute-start | bytes 73736 | tf_op jit(solution)/shard_map/ppermute | solution.py:363

commit v2 on v1

--- a/solution.py
+++ b/solution.py
@@ -16,6 +16,7 @@
 GRAVITY = 1.0
 
 HALO = 8
+UNROLL = 2
 KP = 32
 KD = 48
 KE = 16
@@ -120,14 +121,30 @@
     dest[pl.ds(cell, 8)] = stage[...].reshape(8, count, 128).astype(BF16)
 
 
-def pair_tile(left, right, signs):
-    return lax.dot_general(
-        left, right * signs, (((0,), (0,)), ((), ())), preferred_element_type=F32
-    )
+def upright(rows):
+    return rows.astype(F32).T.astype(BF16)
+
+
+def tiles(left, sources):
+    product = jnp.dot(left, jnp.concatenate(sources, axis=1), preferred_element_type=F32)
+    return [product[:, 128 * i : 128 * (i + 1)] for i in range(3)]
+
+
+def signed(feat, cell, table, first):
+    return [feat[cell + sz] * table[first + sz + 1] for sz in (-1, 0, 1)]
 
 
 def fold(total):
     return jnp.sum(total.T, axis=0, keepdims=True)
+
+
+def each_row(low, high, row):
+    def step(i, carry):
+        for u in range(UNROLL):
+            row(low + i * UNROLL + u)
+        return carry
+
+    lax.fori_loop(0, (high - low) // UNROLL, step, 0)
 
 
 def density_kernel(
@@ -158,25 +175,25 @@
     lax.fori_loop(0, groups, prepare, 0)
     acc[...] = jnp.zeros_like(acc)
 
-    def row(k, carry):
+    def row(k):
         for t in range(2):
-            pos_l, vel_l_t = out_l[(t + 1) * depth + k], vel_l[t * depth + k]
+            pos_l, vel_l_t = upright(out_l[(t + 1) * depth + k]), upright(vel_l[t * depth + k])
             rho = jnp.zeros((128, 128), F32)
             div = jnp.zeros((128, 128), F32)
-            for n, (sx, sz) in enumerate(SHIFTS):
-                col = t + 1 + sx
-                cell = col * depth + k + sz
-                s = jnp.maximum(pair_tile(pos_l, out_r[cell + depth], posc[9 * t + n]), 0.0)
-                d = pair_tile(vel_l_t, vel_r[cell], velc[n])
-                ref, at = blocks[col + 1]
-                q = s * s * ref[4, at, pl.ds(k + sz, 1), :]
-                rho = rho + q * s
-                div = div + q * d
+            for sx in range(3):
+                cell = (t + sx) * depth + k
+                reach = tiles(pos_l, signed(out_r, cell + depth, posc, 9 * t + 3 * sx))
+                closing = tiles(vel_l_t, signed(vel_r, cell, velc, 3 * sx))
+                ref, at = blocks[t + sx + 1]
+                for sz in range(3):
+                    s = jnp.maximum(reach[sz], 0.0)
+                    q = s * s * ref[4, at, pl.ds(k + sz - 1, 1), :]
+                    rho = rho + q * s
+                    div = div + q * closing[sz]
             acc[0, t, pl.ds(k, 1), :] = fold(rho)
             acc[1, t, pl.ds(k, 1), :] = fold(div)
-        return carry
-
-    lax.fori_loop(low, high, row, 0)
+
+    each_row(low, high, row)
     mass = own[4]
     alive = mass > 0.0
     density = jnp.where(alive, acc[0], 0.0)
@@ -197,19 +214,19 @@
 
 
 def jacobi_rows(low, high, first_col, feat_r, feat_l, posc, wide_u, acc, depth):
-    def row(k, carry):
+    def row(k):
         for t in range(2):
-            pos_l = feat_l[(first_col + t) * depth + k]
+            pos_l = upright(feat_l[(first_col + t) * depth + k])
             total = jnp.zeros((128, 128), F32)
-            for n, (sx, sz) in enumerate(SHIFTS):
-                col = t + 1 + sx
-                cell = (first_col + col) * depth + k + sz
-                s = jnp.maximum(pair_tile(pos_l, feat_r[cell], posc[9 * t + n]), 0.0)
-                total = total + s * s * wide_u[col, pl.ds(k + sz, 1), :]
+            for sx in range(3):
+                cell = (first_col + t + sx) * depth + k
+                reach = tiles(pos_l, signed(feat_r, cell, posc, 9 * t + 3 * sx))
+                for sz in range(3):
+                    s = jnp.maximum(reach[sz], 0.0)
+                    total = total + s * s * wide_u[t + sx, pl.ds(k + sz - 1, 1), :]
             acc[t, pl.ds(k, 1), :] = fold(total)
-        return carry
-
-    lax.fori_loop(low, high, row, 0)
+
+    each_row(low, high, row)
 
 
 def sweep1_kernel(
@@ -225,22 +242,23 @@
     wide_u[2:4] = weight_own[...] * start_o
     acc[...] = jnp.zeros_like(acc)
 
-    def row(k, carry):
+    def row(k):
         for t in range(2):
-            pos_l = feat_l[t * depth + k]
+            pos_l = upright(feat_l[t * depth + k])
             total_w = jnp.zeros((128, 128), F32)
             total_u = jnp.zeros((128, 128), F32)
-            for n, (sx, sz) in enumerate(SHIFTS):
-                col = t + 1 + sx
-                s = jnp.maximum(pair_tile(pos_l, feat_r[col * depth + k + sz], posc[9 * t + n]), 0.0)
-                q = s * s
-                total_w = total_w + q * wide_w[col, pl.ds(k + sz, 1), :]
-                total_u = total_u + q * wide_u[col, pl.ds(k + sz, 1), :]
+            for sx in range(3):
+                col = t + sx
+                reach = tiles(pos_l, signed(feat_r, col * depth + k, posc, 9 * t + 3 * sx))
+                for sz in range(3):
+                    s = jnp.maximum(reach[sz], 0.0)
+                    q = s * s
+                    total_w = total_w + q * wide_w[col, pl.ds(k + sz - 1, 1), :]
+                    total_u = total_u + q * wide_u[col, pl.ds(k + sz - 1, 1), :]
             acc[0, t, pl.ds(k, 1), :] = fold(total_w)
             acc[1, t, pl.ds(k, 1), :] = fold(total_u)
-        return carry
-
-    lax.fori_loop(low, high, row, 0)
+
+    each_row(low, high, row)
     diagonal = COMPRESSION + 6.0 * acc[0]
     out_diag[...] = diagonal
     below = column_update(left[4, 1] > 0.0, start_l[1], recv[2], acc[1, 0], diagonal[0])
@@ -309,30 +327,30 @@
 
     lax.fori_loop(0, depth // 8, prepare, 0)
 
-    def row(k, carry):
+    def row(k):
         for t in range(2):
-            pos_l, pres_l_t = feat_l[(t + 1) * depth + k], pres_l[t * depth + k]
+            pos_l, pres_l_t = upright(feat_l[(t + 1) * depth + k]), upright(pres_l[t * depth + k])
             plain = jnp.zeros((128, 128), F32)
             by_x = jnp.zeros((128, 128), F32)
             by_z = jnp.zeros((128, 128), F32)
-            for n, (sx, sz) in enumerate(SHIFTS):
-                col = t + 1 + sx
-                s = jnp.maximum(pair_tile(pos_l, feat_r[(col + 1) * depth + k + sz], posc[9 * t + n]), 0.0)
-                e = lax.dot_general(
-                    pres_l_t, pres_r[col * depth + k + sz], (((0,), (0,)), ((), ())),
-                    preferred_element_type=F32,
-                )
-                g = s * s * e
-                plain = plain + g
-                by_x = by_x + g * (wide_x[col, pl.ds(k + sz, 1), :] + float(sx))
-                by_z = by_z + g * (wide_z[col, pl.ds(k + sz, 1), :] + float(sz))
+            for sx in range(3):
+                col = t + sx
+                cell = col * depth + k
+                reach = tiles(pos_l, signed(feat_r, cell + depth, posc, 9 * t + 3 * sx))
+                lift = tiles(pres_l_t, [pres_r[cell + sz] for sz in (-1, 0, 1)])
+                for sz in range(3):
+                    s = jnp.maximum(reach[sz], 0.0)
+                    g = s * s * lift[sz]
+                    at = pl.ds(k + sz - 1, 1)
+                    plain = plain + g
+                    by_x = by_x + g * (wide_x[col, at, :] + float(sx - 1))
+                    by_z = by_z + g * (wide_z[col, at, :] + float(sz - 1))
             acc[0, t, pl.ds(k, 1), :] = fold(plain)
             acc[1, t, pl.ds(k, 1), :] = fold(by_x)
             acc[2, t, pl.ds(k, 1), :] = fold(by_z)
-        return carry
-
-    lax.fori_loop(low, high, row, 0)
-    inner = slice(low, high)
+
+    each_row(low, high, row)
+    inner = slice(HALO, depth - HALO)
     alive = own[4, :, inner] > 0.0
     out_pressure[0] = p3[1, inner]
     out_pressure[1] = recv4[0, inner]
@@ -390,7 +408,10 @@
 
     def rows(level):
         reach = ITERS + 2 - level
-        return HALO - reach, HALO + cells + reach
+        low = HALO - reach
+        steps = -(-(cells + 2 * reach) // UNROLL)
+        assert low + steps * UNROLL < depth
+        return low, low + steps * UNROLL
 
     feat_r, feat_l, weight, density_ratio, source, send1 = local_call(
         functools.partial(density_kernel, *rows(1)),

time: 278 us -> 235 us (0.85)
  Pallas kernels: 208 us -> 165 us
    pallas_call x5, Pallas kernels: 208 us -> 165 us  [local_call(): pl.pallas_call(kernel, out_shape=[jax.ShapeDtypeStruct(shape, dtype) for...]
where the time goes in v2:
time: 235 us; the launch traced here: 234 us
  Pallas kernels  165 us (70%)
  waiting for transfers between devices  30.2 us (13%)
  local copies, waits for them, and re-layouts  18.6 us (8%)
  starting transfers between devices  12.7 us (5%)
  other arithmetic  7.11 us (3%)
    pallas_call x5, Pallas kernels, local_call(): pl.pallas_call(kernel, out_shape=[jax.ShapeDtypeStruct(shape, dtype) for...  165 us
    ppermute x6, waiting for transfers between devices, around(): lax.ppermute(block, axis, [(i, (i + distance) % peers) for i in range(pee...  22.1 us
    ppermute x4, starting transfers between devices, from_behind(): return lax.ppermute(block, axis, route)  10.1 us
    ppermute x4, waiting for transfers between devices, from_behind(): return lax.ppermute(block, axis, route)  8.15 us
    concatenate x2, local copies, waits for them, and re-layouts, per_device(): jnp.concatenate([offsets_new, velocity_new, pressure[None], live_mass[Non...  6.5 us
    gather x1, local copies, waits for them, and re-layouts, per_device(): blocks = state[:, leaving_slot.reshape(-1)].reshape(6, block_rows, 1, slots)  6.18 us
  transfers between devices with their start and end apart: 10, of which 9 were waited for; matrix products, arithmetic and copies ran while one was open for 1% of the time, Pallas kernels for 0%

profile of v2, /device:TPU:28, one launch (start us, length us, event | category | flops | bytes accessed | tf_op | source)
XLA Modules:
  0.0 234.5 jit_solution(5095439596624882966)
XLA Ops:
  0.6 0.9 fusion.3
  1.6 0.8 pad_maximum_fusion.5
  2.4 2.4 %collective-permute-start.1 = (f32[6,2,8,128]{3,2,1,0:T(8,128)S(1)}, f32[6,2,8,128]{3,2,1,0:T(8,128)S(1)}, u32[]{:S(2)}, u32[]{:S(2)}) collective-permute-start(f32[6,2,8,128]{3,2,1,0:T(8,128)S(1)} %get-tuple-element.33), channel_id=1, source_target_pairs={{1,0},{2,1},{3,2},{5,4},{6,5},{7,6},{9,8},{10,9},{11,10},{13,12},{... | collective-permute-start | bytes 147464 | tf_op jit(solution)/shard_map/ppermute | solution.py:381
  4.8 1.3 collective-permute-start
  6.5 4.3 %collective-permute-done = f32[6,2,8,128]{3,2,1,0:T(8,128)S(1)} collective-permute-done((f32[6,2,8,128]{3,2,1,0:T(8,128)S(1)}, f32[6,2,8,128]{3,2,1,0:T(8,128)S(1)}, u32[]{:S(2)}, u32[]{:S(2)}) %collective-permute-start) | collective-permute-done | bytes 49184 | tf_op jit(solution)/shard_map/ppermute | solution.py:381
  10.7 1.0 pad_maximum_fusion.1.own
  11.9 1.0 fusion
  12.9 2.6 %collective-permute-start.3 = (f32[5,1,80,128]{3,2,1,0:T(8,128)S(1)}, f32[5,1,80,128]{3,2,1,0:T(8,128)S(1)}, u32[]{:S(2)}, u32[]{:S(2)}) collective-permute-start(f32[5,1,80,128]{3,2,1,0:T(8,128)S(1)} %slice.18), channel_id=1, source_target_pairs={{0,28},{4,0},{8,4},{12,8},{16,12},{20,16},{24,20},{28,24},{1,29},{... | collective-permute-start | bytes 614408 | tf_op jit(solution)/shard_map/ppermute | solution.py:386
  15.5 0.8 select_convert_fusion
  16.3 4.8 %collective-permute-done.3.right = f32[5,1,80,128]{3,2,1,0:T(8,128)S(1)} collective-permute-done((f32[5,1,80,128]{3,2,1,0:T(8,128)S(1)}, f32[5,1,80,128]{3,2,1,0:T(8,128)S(1)}, u32[]{:S(2)}, u32[]{:S(2)}) %collective-permute-start.3) | collective-permute-done | bytes 204832 | tf_op jit(solution)/shard_map/ppermute | solution.py:386
  21.0 2.2 collective-permute-done.2.left
  23.2 0.9 broadcast_in_dim.61.posc
  24.1 1.5 broadcast_in_dim.62.velc
  25.5 47.5 %shard_map.190 = (bf16[400,32,128]{2,1,0:T(8,128)(2,1)}, bf16[240,32,128]{2,1,0:T(8,128)(2,1)}, f32[2,80,128]{2,1,0:T(8,128)}, f32[2,80,128]{2,1,0:T(8,128)}, f3...) custom-call(f32[6,2,80,128]{3,2,1,0:T(8,128)} %copy-done.1, f32[6,2,80,128]{3,2,1,0:T(8,128)} %copy-done, ...), custom_call_target="tpu_custom_call" | custom-call | tf_op jit(solution)/shard_map/pallas_call | solution.py:368
  73.1 0.7 compare_select_fusion
  73.8 4.7 %collective-permute-done.4.recv.recv1 = f32[3,80,128]{2,1,0:T(8,128)S(1)} collective-permute-done((f32[3,80,128]{2,1,0:T(8,128)}, f32[3,80,128]{2,1,0:T(8,128)S(1)}, u32[]{:S(2)}, u32[]{:S(2)}) %collective-permute-start.4) | collective-permute-done | bytes 122912 | tf_op jit(solution)/shard_map/ppermute | solution.py:386
  78.5 0.8 broadcast_in_dim.63.posc
  79.3 31.0 %shard_map.191 = (f32[2,80,128]{2,1,0:T(8,128)}, f32[2,80,128]{2,1,0:T(8,128)}, f32[4,80,128]{2,1,0:T(8,128)}) custom-call(bf16[400,32,128]{2,1,0:T(8,128)(2,1)} %get-tuple-element.20.feat_r, bf16[240,32,128]{2,1,0:T(8,128)(2,1)} %get-tuple-element.21.feat_l, f32[6,2,80,128]{3,2,1,0:T(8,128)} %copy-done.1, f32[6,2,80,128]{3,2,1,0:T(8,128)} %copy-done, ...), custom_call_target="tpu_custom_call" | custom-call | tf_op jit(solution)/shard_map/pallas_call | solution.py:368
  110.3 3.1 %collective-permute-done.5.recv2 = f32[4,80,128]{2,1,0:T(8,128)S(1)} collective-permute-done((f32[4,80,128]{2,1,0:T(8,128)}, f32[4,80,128]{2,1,0:T(8,128)S(1)}, u32[]{:S(2)}, u32[]{:S(2)}) %collective-permute-start.5) | collective-permute-done | bytes 163872 | tf_op jit(solution)/shard_map/ppermute | solution.py:386
  113.4 0.7 copy-done.4
  114.1 24.3 %shard_map.192.p2 = f32[2,80,128]{2,1,0:T(8,128)} custom-call(bf16[400,32,128]{2,1,0:T(8,128)(2,1)} %get-tuple-element.20.feat_r, bf16[240,32,128]{2,1,0:T(8,128)(2,1)} %get-tuple-element.21.feat_l, f32[6,2,80,128]{3,2,1,0:T(8,128)} %copy-done, f32[3,80,128]{2,1,0:T(8,128)} %copy-done.2, f32[4,80,128]{2,1,0:T(8,128)} %copy-done.4, ...), custom_call_target="tpu_custom_call" | custom-call | tf_op jit(solution)/shard_map/pallas_call | solution.py:368
  138.5 5.0 %collective-permute-done.6.recv3 = f32[2,80,128]{2,1,0:T(8,128)S(1)} collective-permute-done((f32[2,80,128]{2,1,0:T(8,128)}, f32[2,80,128]{2,1,0:T(8,128)S(1)}, u32[]{:S(2)}, u32[]{:S(2)}) %collective-permute-start.6) | collective-permute-done | bytes 81952 | tf_op jit(solution)/shard_map/ppermute | solution.py:386
  144.1 23.8 %shard_map.193.p3 = f32[2,80,128]{2,1,0:T(8,128)} custom-call(bf16[400,32,128]{2,1,0:T(8,128)(2,1)} %get-tuple-element.20.feat_r, bf16[240,32,128]{2,1,0:T(8,128)(2,1)} %get-tuple-element.21.feat_l, f32[6,2,80,128]{3,2,1,0:T(8,128)} %copy-done.1, f32[6,2,80,128]{3,2,1,0:T(8,128)} %copy-done, f32[3,80,128]{2,1,0:T(8,128)} %copy-done.2, ...), custom_call_target="tpu_custom_call" | custom-call | tf_op jit(solution)/shard_map/pallas_call | solution.py:368
  168.0 2.3 collective-permute-done.7.recv4
  170.9 38.3 %shard_map.194 = (f32[2,64,128]{2,1,0:T(8,128)}, f32[2,2,64,128]{3,2,1,0:T(8,128)}, f32[2,2,64,128]{3,2,1,0:T(8,128)}, f32[2,2,64,128]{3,2,1,0:T(8,128)}) custom-call(bf16[400,32,128]{2,1,0:T(8,128)(2,1)} %get-tuple-element.20.feat_r, bf16[240,32,128]{2,1,0:T(8,128)(2,1)} %get-tuple-element.21.feat_l, f32[6,2,80,128]{3,2,1,0:T(8,128)} %copy-done, ...), custom_call_target="tpu_custom_call" | custom-call | tf_op jit(solution)/shard_map/pallas_call | solution.py:368
  209.3 1.2 copy_bitcast_fusion
  210.4 1.1 pad_maximum_fusion
  211.5 5.3 %copy.28 = f32[6,16384]{0,1:T(8,128)} copy(f32[6,16384]{1,0:T(8,128)S(1)} %pad_maximum_fusion) | data formatting | bytes 786432 | tf_op jit(solution)/shard_map/concatenate | solution.py:471
  216.9 6.2 %gather_fusion = f32[1024,6]{1,0:T(8,128)S(1)} fusion(f32[6,16384]{0,1:T(8,128)} %copy.28, s32[1024]{0:T(1024)S(1)} %broadcast_clamp_fusion), kind=kCustom, calls=%fused_computation | custom fusion | bytes 53248 | tf_op jit(solution)/shard_map/gather | solution.py:473
  223.3 4.5 %collective-permute-start.9 = (f32[6,8,1,128]{3,1,0,2:T(8,128)S(1)}, f32[6,8,1,128]{3,1,0,2:T(8,128)S(1)}, u32[]{:S(2)}, u32[]{:S(2)}) collective-permute-start(f32[6,8,1,128]{3,1,0,2:T(8,128)S(1)} %get-tuple-element.35), channel_id=1, source_target_pairs={{4,0},{8,4},{12,8},{16,12},{20,16},{24,20},{28,24},{5,1},{9,5},{13... | collective-permute-start | bytes 73736 | tf_op jit(solution)/shard_map/ppermute | solution.py:381
  227.8 1.9 collective-permute-start.8
  230.4 3.5 %collective-permute-done.8 = f32[6,8,1,128]{3,1,0,2:T(8,128)S(1)} collective-permute-done((f32[6,8,1,128]{3,1,0,2:T(8,128)S(1)}, f32[6,8,1,128]{3,1,0,2:T(8,128)S(1)}, u32[]{:S(2)}, u32[]{:S(2)}) %collective-permute-start.8) | collective-permute-done | bytes 24608 | tf_op jit(solution)/shard_map/ppermute | solution.py:381
  (34 shorter events, 3.4 us)
Async XLA Ops:
  2.4 136.1 %copy-start.9 = (s32[8,1]{0,1:T(1,128)S(1)}, s32[8,1]{0,1:T(1,128)}, u32[]{:S(2)}) copy-start(s32[8,1]{0,1:T(1,128)} %param.22) | copy-start | bytes 100
  2.4 4.1 %collective-permute-start.1 = (f32[6,2,8,128]{3,2,1,0:T(8,128)S(1)}, f32[6,2,8,128]{3,2,1,0:T(8,128)S(1)}, u32[]{:S(2)}, u32[]{:S(2)}) collective-permute-start(f32[6,2,8,128]{3,2,1,0:T(8,128)S(1)} %get-tuple-element.33), channel_id=1, source_target_pairs={{1,0},{2,1},{3,2},{5,4},{6,5},{7,6},{9,8},{10,9},{11,10},{13,12},{... | collective-permute-start | bytes 147464 | tf_op jit(solution)/shard_map/ppermute | solution.py:381
  4.8 6.0 %collective-permute-start = (f32[6,2,8,128]{3,2,1,0:T(8,128)S(1)}, f32[6,2,8,128]{3,2,1,0:T(8,128)S(1)}, u32[]{:S(2)}, u32[]{:S(2)}) collective-permute-start(f32[6,2,8,128]{3,2,1,0:T(8,128)S(1)} %get-tuple-element.32), channel_id=1, source_target_pairs={{0,1},{1,2},{2,3},{4,5},{5,6},{6,7},{8,9},{9,10},{10,11},{12,13},{... | collective-permute-start | bytes 147464 | tf_op jit(solution)/shard_map/ppermute | solution.py:381
  11.8 13.7 %copy-start = (f32[6,2,80,128]{3,2,1,0:T(8,128)}, f32[6,2,80,128]{3,2,1,0:T(8,128)S(1)}, u32[]{:S(2)}) copy-start(f32[6,2,80,128]{3,2,1,0:T(8,128)S(1)} %pad_maximum_fusion.1.own) | copy-start | bytes 1474564
  11.8 11.4 %collective-permute-start.2 = (f32[6,2,80,128]{3,2,1,0:T(8,128)S(1)}, f32[6,2,80,128]{3,2,1,0:T(8,128)S(1)}, u32[]{:S(2)}, u32[]{:S(2)}) collective-permute-start(f32[6,2,80,128]{3,2,1,0:T(8,128)S(1)} %pad_maximum_fusion.1.own), channel_id=1, source_target_pairs={{0,4},{4,8},{8,12},{12,16},{16,20},{20,24},{24,28},{28,0},{1,5},{5... | collective-permute-start | bytes 1474568 | tf_op jit(solution)/shard_map/ppermute | solution.py:386
  12.9 8.1 %collective-permute-start.3 = (f32[5,1,80,128]{3,2,1,0:T(8,128)S(1)}, f32[5,1,80,128]{3,2,1,0:T(8,128)S(1)}, u32[]{:S(2)}, u32[]{:S(2)}) collective-permute-start(f32[5,1,80,128]{3,2,1,0:T(8,128)S(1)} %slice.18), channel_id=1, source_target_pairs={{0,28},{4,0},{8,4},{12,8},{16,12},{20,16},{24,20},{28,24},{1,29},{... | collective-permute-start | bytes 614408 | tf_op jit(solution)/shard_map/ppermute | solution.py:386
  21.0 4.5 %copy-start.3 = (f32[5,1,80,128]{3,2,1,0:T(8,128)}, f32[5,1,80,128]{3,2,1,0:T(8,128)S(1)}, u32[]{:S(2)}) copy-start(f32[5,1,80,128]{3,2,1,0:T(8,128)S(1)} %collective-permute-done.3.right) | copy-start | bytes 614404
  23.2 2.3 copy-start.1
  73.1 5.4 %collective-permute-start.4 = (f32[3,80,128]{2,1,0:T(8,128)}, f32[3,80,128]{2,1,0:T(8,128)S(1)}, u32[]{:S(2)}, u32[]{:S(2)}) collective-permute-start(f32[3,80,128]{2,1,0:T(8,128)} %get-tuple-element.22), channel_id=1, source_target_pairs={{0,4},{4,8},{8,12},{12,16},{16,20},{20,24},{24,28},{28,0},{1,5},{5... | collective-permute-start | bytes 368648 | tf_op jit(solution)/shard_map/ppermute | solution.py:386
  78.5 0.8 copy-start.2
  110.3 57.7 %copy-start.8 = (s32[8,1]{0,1:T(1,128)S(1)}, s32[8,1]{0,1:T(1,128)}, u32[]{:S(2)}) copy-start(s32[8,1]{0,1:T(1,128)} %param.21) | copy-start | bytes 100
  110.3 3.2 %collective-permute-start.5 = (f32[4,80,128]{2,1,0:T(8,128)}, f32[4,80,128]{2,1,0:T(8,128)S(1)}, u32[]{:S(2)}, u32[]{:S(2)}) collective-permute-start(f32[4,80,128]{2,1,0:T(8,128)} %get-tuple-element.25), channel_id=1, source_target_pairs={{0,28},{4,0},{8,4},{12,8},{16,12},{20,16},{24,20},{28,24},{1,29},{... | collective-permute-start | bytes 491528 | tf_op jit(solution)/shard_map/ppermute | solution.py:386
  113.4 0.7 copy-start.4
  138.5 5.0 %collective-permute-start.6 = (f32[2,80,128]{2,1,0:T(8,128)}, f32[2,80,128]{2,1,0:T(8,128)S(1)}, u32[]{:S(2)}, u32[]{:S(2)}) collective-permute-start(f32[2,80,128]{2,1,0:T(8,128)} %shard_map.192.p2), channel_id=1, source_target_pairs={{0,4},{4,8},{8,12},{12,16},{16,20},{20,24},{24,28},{28,0},{1,5},{5... | collective-permute-start | bytes 245768 | tf_op jit(solution)/shard_map/ppermute | solution.py:386
  143.5 0.6 copy-start.6
  167.9 2.4 %collective-permute-start.7 = (f32[2,80,128]{2,1,0:T(8,128)}, f32[2,80,128]{2,1,0:T(8,128)S(1)}, u32[]{:S(2)}, u32[]{:S(2)}) collective-permute-start(f32[2,80,128]{2,1,0:T(8,128)} %shard_map.193.p3), channel_id=1, source_target_pairs={{0,28},{4,0},{8,4},{12,8},{16,12},{20,16},{24,20},{28,24},{1,29},{... | collective-permute-start | bytes 245768 | tf_op jit(solution)/shard_map/ppermute | solution.py:386
  168.0 61.7 %copy-start.7 = (f32[2,80,128]{2,1,0:T(8,128)S(1)}, f32[2,80,128]{2,1,0:T(8,128)}, u32[]{:S(2)}) copy-start(f32[2,80,128]{2,1,0:T(8,128)} %get-tuple-element.19) | copy-start | bytes 245764
  170.3 0.6 copy-start.5
  223.3 7.1 %collective-permute-start.9 = (f32[6,8,1,128]{3,1,0,2:T(8,128)S(1)}, f32[6,8,1,128]{3,1,0,2:T(8,128)S(1)}, u32[]{:S(2)}, u32[]{:S(2)}) collective-permute-start(f32[6,8,1,128]{3,1,0,2:T(8,128)S(1)} %get-tuple-element.35), channel_id=1, source_target_pairs={{4,0},{8,4},{12,8},{16,12},{20,16},{24,20},{28,24},{5,1},{9,5},{13... | collective-permute-start | bytes 73736 | tf_op jit(solution)/shard_map/ppermute | solution.py:381
  227.8 6.0 %collective-permute-start.8 = (f32[6,8,1,128]{3,1,0,2:T(8,128)S(1)}, f32[6,8,1,128]{3,1,0,2:T(8,128)S(1)}, u32[]{:S(2)}, u32[]{:S(2)}) collective-permute-start(f32[6,8,1,128]{3,1,0,2:T(8,128)S(1)} %get-tuple-element.34), channel_id=1, source_target_pairs={{0,4},{4,8},{8,12},{12,16},{16,20},{20,24},{24,28},{1,5},{5,9},{9,... | collective-permute-start | bytes 73736 | tf_op jit(solution)/shard_map/ppermute | solution.py:381

commit v3 on v1

--- a/solution.py
+++ b/solution.py
@@ -16,6 +16,7 @@
 GRAVITY = 1.0
 
 HALO = 8
+CLASSES = ((32, 16), (64, 8), (96, 6), (128, 6))
 KP = 32
 KD = 48
 KE = 16
@@ -120,20 +121,40 @@
     dest[pl.ds(cell, 8)] = stage[...].reshape(8, count, 128).astype(BF16)
 
 
-def pair_tile(left, right, signs):
-    return lax.dot_general(
-        left, right * signs, (((0,), (0,)), ((), ())), preferred_element_type=F32
-    )
+def upright(rows, slots):
+    return rows.astype(F32).T[:slots].astype(BF16)
+
+
+def tiles(left, sources):
+    product = jnp.dot(left, jnp.concatenate(sources, axis=1), preferred_element_type=F32)
+    return [product[:, 128 * i : 128 * (i + 1)] for i in range(3)]
+
+
+def signed(feat, cell, table, first):
+    return [feat[cell + sz] * table[first + sz + 1] for sz in (-1, 0, 1)]
 
 
 def fold(total):
     return jnp.sum(total.T, axis=0, keepdims=True)
 
 
+def each_target(level, order, bounds, target):
+    for index, (slots, cells) in enumerate(CLASSES):
+        start = bounds[level, index]
+        steps = (bounds[level, index + 1] - start + cells - 1) // cells
+
+        def step(i, carry, slots=slots, cells=cells, start=start):
+            for u in range(cells):
+                target(order[level, start + i * cells + u], slots)
+            return carry
+
+        lax.fori_loop(0, steps, step, 0)
+
+
 def density_kernel(
-    low, high, left, own, right, posc, velc,
+    level, order, bounds, left, own, right, posc, velc,
     out_r, out_l, out_w, out_density, out_source, out_send,
-    stage_p, stage_d, vel_r, vel_l, acc,
+    stage_p, stage_d, vel_r, vel_l, wide_m, acc,
 ):
     depth = own.shape[2]
     groups = depth // 8
@@ -158,31 +179,37 @@
     lax.fori_loop(0, groups, prepare, 0)
     acc[...] = jnp.zeros_like(acc)
 
-    def row(k, carry):
-        for t in range(2):
-            pos_l, vel_l_t = out_l[(t + 1) * depth + k], vel_l[t * depth + k]
-            rho = jnp.zeros((128, 128), F32)
-            div = jnp.zeros((128, 128), F32)
-            for n, (sx, sz) in enumerate(SHIFTS):
-                col = t + 1 + sx
-                cell = col * depth + k + sz
-                s = jnp.maximum(pair_tile(pos_l, out_r[cell + depth], posc[9 * t + n]), 0.0)
-                d = pair_tile(vel_l_t, vel_r[cell], velc[n])
-                ref, at = blocks[col + 1]
-                q = s * s * ref[4, at, pl.ds(k + sz, 1), :]
+    wide_m[0:depth] = left[4, 1]
+    wide_m[depth : 2 * depth] = own[4, 0]
+    wide_m[2 * depth : 3 * depth] = own[4, 1]
+    wide_m[3 * depth : 4 * depth] = right[4, 0]
+
+    def target(cell, slots):
+        sign = 9 * (cell >= depth).astype(jnp.int32)
+        pos_l, vel_l_t = upright(out_l[cell + depth], slots), upright(vel_l[cell], slots)
+        rho = jnp.zeros((slots, 128), F32)
+        div = jnp.zeros((slots, 128), F32)
+        for sx in range(3):
+            source = cell + sx * depth
+            reach = tiles(pos_l, signed(out_r, source + depth, posc, sign + 3 * sx))
+            closing = tiles(vel_l_t, signed(vel_r, source, velc, 3 * sx))
+            for sz in range(3):
+                s = jnp.maximum(reach[sz], 0.0)
+                q = s * s * wide_m[pl.ds(source + sz - 1, 1), :]
                 rho = rho + q * s
-                div = div + q * d
-            acc[0, t, pl.ds(k, 1), :] = fold(rho)
-            acc[1, t, pl.ds(k, 1), :] = fold(div)
-        return carry
-
-    lax.fori_loop(low, high, row, 0)
+                div = div + q * closing[sz]
+        acc[0, pl.ds(cell, 1), 0:slots] = fold(rho)
+        acc[1, pl.ds(cell, 1), 0:slots] = fold(div)
+
+    each_target(level, order, bounds, target)
+    density = acc[0].reshape(2, depth, 128)
+    div = -6.0 * acc[1].reshape(2, depth, 128)
     mass = own[4]
     alive = mass > 0.0
-    density = jnp.where(alive, acc[0], 0.0)
+    density = jnp.where(alive, density, 0.0)
     weight = jnp.where(alive, mass / jnp.where(alive, density, 1.0), 0.0)
     source = jnp.where(
-        alive, (density - TIME_STEP * 6.0 * acc[1] - REST_DENSITY) / REST_DENSITY, 0.0
+        alive, (density + TIME_STEP * div - REST_DENSITY) / REST_DENSITY, 0.0
     )
     out_w[...] = weight
     out_density[...] = density / REST_DENSITY
@@ -196,55 +223,60 @@
     return jnp.where(alive, updated, 0.0)
 
 
-def jacobi_rows(low, high, first_col, feat_r, feat_l, posc, wide_u, acc, depth):
-    def row(k, carry):
-        for t in range(2):
-            pos_l = feat_l[(first_col + t) * depth + k]
-            total = jnp.zeros((128, 128), F32)
-            for n, (sx, sz) in enumerate(SHIFTS):
-                col = t + 1 + sx
-                cell = (first_col + col) * depth + k + sz
-                s = jnp.maximum(pair_tile(pos_l, feat_r[cell], posc[9 * t + n]), 0.0)
-                total = total + s * s * wide_u[col, pl.ds(k + sz, 1), :]
-            acc[t, pl.ds(k, 1), :] = fold(total)
-        return carry
-
-    lax.fori_loop(low, high, row, 0)
+def jacobi_sums(level, order, bounds, first_col, feat_r, feat_l, posc, wide_u, acc, depth):
+    def target(cell, slots):
+        sign = 9 * (cell >= depth).astype(jnp.int32)
+        at = cell + first_col * depth
+        pos_l = upright(feat_l[at], slots)
+        total = jnp.zeros((slots, 128), F32)
+        for sx in range(3):
+            reach = tiles(pos_l, signed(feat_r, at + sx * depth, posc, sign + 3 * sx))
+            for sz in range(3):
+                s = jnp.maximum(reach[sz], 0.0)
+                total = total + s * s * wide_u[pl.ds(cell + sx * depth + sz - 1, 1), :]
+        acc[pl.ds(cell, 1), 0:slots] = fold(total)
+
+    acc[...] = jnp.zeros_like(acc)
+    each_target(level, order, bounds, target)
+    return acc[...].reshape(2, depth, 128)
 
 
 def sweep1_kernel(
-    low, high, feat_r, feat_l, left, own, recv, weight_own, source_own, posc,
+    level, order, bounds, feat_r, feat_l, left, own, recv, weight_own, source_own, posc,
     out_p, out_diag, out_send, wide_w, wide_u, acc,
 ):
     depth = weight_own.shape[1]
     start_l = jnp.where(left[4] > 0.0, left[5], 0.0)
     start_o = jnp.where(own[4] > 0.0, own[5], 0.0)
-    wide_w[0:2] = recv[0:2]
-    wide_w[2:4] = weight_own[...]
-    wide_u[0:2] = recv[0:2] * start_l
-    wide_u[2:4] = weight_own[...] * start_o
+    for col in range(4):
+        rows = slice(col * depth, (col + 1) * depth)
+        weight = recv[col] if col < 2 else weight_own[col - 2]
+        wide_w[rows] = weight
+        wide_u[rows] = weight * (start_l if col < 2 else start_o)[col % 2]
     acc[...] = jnp.zeros_like(acc)
 
-    def row(k, carry):
-        for t in range(2):
-            pos_l = feat_l[t * depth + k]
-            total_w = jnp.zeros((128, 128), F32)
-            total_u = jnp.zeros((128, 128), F32)
-            for n, (sx, sz) in enumerate(SHIFTS):
-                col = t + 1 + sx
-                s = jnp.maximum(pair_tile(pos_l, feat_r[col * depth + k + sz], posc[9 * t + n]), 0.0)
+    def target(cell, slots):
+        sign = 9 * (cell >= depth).astype(jnp.int32)
+        pos_l = upright(feat_l[cell], slots)
+        total_w = jnp.zeros((slots, 128), F32)
+        total_u = jnp.zeros((slots, 128), F32)
+        for sx in range(3):
+            source = cell + sx * depth
+            reach = tiles(pos_l, signed(feat_r, source, posc, sign + 3 * sx))
+            for sz in range(3):
+                s = jnp.maximum(reach[sz], 0.0)
                 q = s * s
-                total_w = total_w + q * wide_w[col, pl.ds(k + sz, 1), :]
-                total_u = total_u + q * wide_u[col, pl.ds(k + sz, 1), :]
-            acc[0, t, pl.ds(k, 1), :] = fold(total_w)
-            acc[1, t, pl.ds(k, 1), :] = fold(total_u)
-        return carry
-
-    lax.fori_loop(low, high, row, 0)
-    diagonal = COMPRESSION + 6.0 * acc[0]
+                total_w = total_w + q * wide_w[pl.ds(source + sz - 1, 1), :]
+                total_u = total_u + q * wide_u[pl.ds(source + sz - 1, 1), :]
+        acc[0, pl.ds(cell, 1), 0:slots] = fold(total_w)
+        acc[1, pl.ds(cell, 1), 0:slots] = fold(total_u)
+
+    each_target(level, order, bounds, target)
+    diagonal = COMPRESSION + 6.0 * acc[0].reshape(2, depth, 128)
+    pulled = acc[1].reshape(2, depth, 128)
     out_diag[...] = diagonal
-    below = column_update(left[4, 1] > 0.0, start_l[1], recv[2], acc[1, 0], diagonal[0])
-    here = column_update(own[4, 0] > 0.0, start_o[0], source_own[0], acc[1, 1], diagonal[1])
+    below = column_update(left[4, 1] > 0.0, start_l[1], recv[2], pulled[0], diagonal[0])
+    here = column_update(own[4, 0] > 0.0, start_o[0], source_own[0], pulled[1], diagonal[1])
     out_p[0] = below
     out_p[1] = here
     out_send[0] = below
@@ -254,35 +286,33 @@
 
 
 def sweep2_kernel(
-    low, high, feat_r, feat_l, own, recv1, recv2, weight_own, source_own, diag, p1, posc,
+    level, order, bounds, feat_r, feat_l, own, recv1, recv2, weight_own, source_own, diag, p1, posc,
     out_p, wide_u, acc,
 ):
     depth = weight_own.shape[1]
-    wide_u[0] = recv1[1] * p1[0]
-    wide_u[1] = weight_own[0] * p1[1]
-    wide_u[2] = weight_own[1] * recv2[0]
-    wide_u[3] = recv2[2] * recv2[1]
-    acc[...] = jnp.zeros_like(acc)
-    jacobi_rows(low, high, 1, feat_r, feat_l, posc, wide_u, acc, depth)
-    out_p[0] = column_update(own[4, 0] > 0.0, p1[1], source_own[0], acc[0], diag[1])
-    out_p[1] = column_update(own[4, 1] > 0.0, recv2[0], source_own[1], acc[1], recv2[3])
+    wide_u[0:depth] = recv1[1] * p1[0]
+    wide_u[depth : 2 * depth] = weight_own[0] * p1[1]
+    wide_u[2 * depth : 3 * depth] = weight_own[1] * recv2[0]
+    wide_u[3 * depth : 4 * depth] = recv2[2] * recv2[1]
+    pulled = jacobi_sums(level, order, bounds, 1, feat_r, feat_l, posc, wide_u, acc, depth)
+    out_p[0] = column_update(own[4, 0] > 0.0, p1[1], source_own[0], pulled[0], diag[1])
+    out_p[1] = column_update(own[4, 1] > 0.0, recv2[0], source_own[1], pulled[1], recv2[3])
 
 
 def sweep3_kernel(
-    low, high, feat_r, feat_l, left, own, recv1, recv3, weight_own, source_own, diag, p2, posc,
+    level, order, bounds, feat_r, feat_l, left, own, recv1, recv3, weight_own, source_own, diag, p2, posc,
     out_p, wide_u, acc,
 ):
     depth = weight_own.shape[1]
-    wide_u[0:2] = recv1[0:2] * recv3[...]
-    wide_u[2:4] = weight_own[...] * p2[...]
-    acc[...] = jnp.zeros_like(acc)
-    jacobi_rows(low, high, 0, feat_r, feat_l, posc, wide_u, acc, depth)
-    out_p[0] = column_update(left[4, 1] > 0.0, recv3[1], recv1[2], acc[0], diag[0])
-    out_p[1] = column_update(own[4, 0] > 0.0, p2[0], source_own[0], acc[1], diag[1])
+    wide_u[0 : 2 * depth] = (recv1[0:2] * recv3[...]).reshape(2 * depth, 128)
+    wide_u[2 * depth : 4 * depth] = (weight_own[...] * p2[...]).reshape(2 * depth, 128)
+    pulled = jacobi_sums(level, order, bounds, 0, feat_r, feat_l, posc, wide_u, acc, depth)
+    out_p[0] = column_update(left[4, 1] > 0.0, recv3[1], recv1[2], pulled[0], diag[0])
+    out_p[1] = column_update(own[4, 0] > 0.0, p2[0], source_own[0], pulled[1], diag[1])
 
 
 def force_kernel(
-    low, high, feat_r, feat_l, own, recv1, recv2, recv4, left, right, weight_own, p3, posc,
+    level, order, bounds, feat_r, feat_l, own, recv1, recv2, recv4, left, right, weight_own, p3, posc,
     out_pressure, out_acc, out_velocity, out_offsets,
     wide_p, wide_w, wide_x, wide_z, pres_r, pres_l, stage, acc,
 ):
@@ -293,9 +323,9 @@
     wide_w[1:3] = weight_own[...]
     wide_w[3] = recv2[2]
     for field, wide in ((0, wide_x), (1, wide_z)):
-        wide[0] = left[field, 1] - 0.5
-        wide[1:3] = own[field] - 0.5
-        wide[3] = right[field, 0] - 0.5
+        wide[0:depth] = left[field, 1] - 0.5
+        wide[depth : 3 * depth] = own[field].reshape(2 * depth, 128) - 0.5
+        wide[3 * depth : 4 * depth] = right[field, 0] - 0.5
 
     def prepare(group, carry):
         rows = pl.ds(pl.multiple_of(group * 8, 8), 8)
@@ -309,35 +339,37 @@
 
     lax.fori_loop(0, depth // 8, prepare, 0)
 
-    def row(k, carry):
-        for t in range(2):
-            pos_l, pres_l_t = feat_l[(t + 1) * depth + k], pres_l[t * depth + k]
-            plain = jnp.zeros((128, 128), F32)
-            by_x = jnp.zeros((128, 128), F32)
-            by_z = jnp.zeros((128, 128), F32)
-            for n, (sx, sz) in enumerate(SHIFTS):
-                col = t + 1 + sx
-                s = jnp.maximum(pair_tile(pos_l, feat_r[(col + 1) * depth + k + sz], posc[9 * t + n]), 0.0)
-                e = lax.dot_general(
-                    pres_l_t, pres_r[col * depth + k + sz], (((0,), (0,)), ((), ())),
-                    preferred_element_type=F32,
-                )
-                g = s * s * e
+    def target(cell, slots):
+        sign = 9 * (cell >= depth).astype(jnp.int32)
+        pos_l, pres_l_t = upright(feat_l[cell + depth], slots), upright(pres_l[cell], slots)
+        plain = jnp.zeros((slots, 128), F32)
+        by_x = jnp.zeros((slots, 128), F32)
+        by_z = jnp.zeros((slots, 128), F32)
+        for sx in range(3):
+            source = cell + sx * depth
+            reach = tiles(pos_l, signed(feat_r, source + depth, posc, sign + 3 * sx))
+            lift = tiles(pres_l_t, [pres_r[source + sz] for sz in (-1, 0, 1)])
+            for sz in range(3):
+                s = jnp.maximum(reach[sz], 0.0)
+                g = s * s * lift[sz]
+                at = pl.ds(source + sz - 1, 1)
                 plain = plain + g
-                by_x = by_x + g * (wide_x[col, pl.ds(k + sz, 1), :] + float(sx))
-                by_z = by_z + g * (wide_z[col, pl.ds(k + sz, 1), :] + float(sz))
-            acc[0, t, pl.ds(k, 1), :] = fold(plain)
-            acc[1, t, pl.ds(k, 1), :] = fold(by_x)
-            acc[2, t, pl.ds(k, 1), :] = fold(by_z)
-        return carry
-
-    lax.fori_loop(low, high, row, 0)
-    inner = slice(low, high)
+                by_x = by_x + g * (wide_x[at, :] + float(sx - 1))
+                by_z = by_z + g * (wide_z[at, :] + float(sz - 1))
+        acc[0, pl.ds(cell, 1), 0:slots] = fold(plain)
+        acc[1, pl.ds(cell, 1), 0:slots] = fold(by_x)
+        acc[2, pl.ds(cell, 1), 0:slots] = fold(by_z)
+
+    acc[...] = jnp.zeros_like(acc)
+    each_target(level, order, bounds, target)
+    sums = acc[...].reshape(3, 2, depth, 128)
+    inner = slice(HALO, depth - HALO)
     alive = own[4, :, inner] > 0.0
     out_pressure[0] = p3[1, inner]
     out_pressure[1] = recv4[0, inner]
     for axis, wide, pull in ((0, wide_x, 0.0), (1, wide_z, GRAVITY)):
-        force = 6.0 * (wide[1:3, inner] * acc[0, :, inner] - acc[axis + 1, :, inner])
+        here = wide[depth : 3 * depth].reshape(2, depth, 128)
+        force = 6.0 * (here[:, inner] * sums[0, :, inner] - sums[axis + 1, :, inner])
         force = jnp.where(alive, force, 0.0)
         velocity = jnp.where(alive, own[axis + 2, :, inner] + TIME_STEP * (force - pull), 0.0)
         out_acc[axis] = force
@@ -345,16 +377,37 @@
         out_offsets[axis] = jnp.where(alive, own[axis, :, inner] + TIME_STEP * velocity, 0.0)
 
 
-def local_call(kernel, out_shapes, scratch, *operands):
+def target_lists(count, cells):
+    depth = count.shape[1]
+    number = jnp.arange(2 * depth, dtype=jnp.int32)
+    kinds = []
+    for level in range(1, ITERS + 3):
+        window = count[1:3] if level % 2 else count[0:2]
+        kind = sum((window > slots).astype(jnp.int32) for slots, _ in CLASSES[:-1])
+        reach = ITERS + 2 - level
+        row = jnp.arange(depth, dtype=jnp.int32)[None]
+        kind = jnp.where((row >= HALO - reach) & (row < HALO + cells + reach), kind, len(CLASSES))
+        kinds.append(kind.reshape(-1))
+    kinds = jnp.stack(kinds)
+    key = kinds * (2 * depth) + number
+    rank = jnp.sum((key[:, None, :] < key[:, :, None]).astype(jnp.int32), 2)
+    bounds = jnp.stack([jnp.sum((kinds < c).astype(jnp.int32), 1) for c in range(len(CLASSES) + 1)], 1)
+    place = jnp.arange(2 * depth + max(c for _, c in CLASSES), dtype=jnp.int32)
+    order = jnp.sum(jnp.where(rank[:, None, :] == place[None, :, None], number, 0), 2)
+    return jnp.where(place < bounds[:, -1:], order, HALO), bounds
+
+
+def local_call(kernel, out_shapes, scratch, order, bounds, *operands):
     vmem = pl.BlockSpec(memory_space=pltpu.VMEM)
+    smem = pl.BlockSpec(memory_space=pltpu.SMEM)
     return pl.pallas_call(
         kernel,
         out_shape=[jax.ShapeDtypeStruct(shape, dtype) for shape, dtype in out_shapes],
-        in_specs=[vmem] * len(operands),
+        in_specs=[smem] * 2 + [vmem] * len(operands),
         out_specs=[vmem] * len(out_shapes),
         scratch_shapes=[pltpu.VMEM(shape, dtype) for shape, dtype in scratch],
         compiler_params=pltpu.CompilerParams(vmem_limit_bytes=VMEM_LIMIT),
-    )(*operands)
+    )(order, bounds, *operands)
 
 
 def from_behind(block, axis, distance):
@@ -388,12 +441,13 @@
     velc = sign_table(velocity_signs)
     plane = (2, depth, slots)
 
-    def rows(level):
-        reach = ITERS + 2 - level
-        return HALO - reach, HALO + cells + reach
+    live = jnp.stack([left[4, 1], own[4, 0], own[4, 1]]) > 0.0
+    lists = target_lists(jnp.sum(live.astype(jnp.int32), -1), cells)
+    long = (4 * depth, slots)
+    sums = (2 * depth, slots)
 
     feat_r, feat_l, weight, density_ratio, source, send1 = local_call(
-        functools.partial(density_kernel, *rows(1)),
+        functools.partial(density_kernel, 0),
         [
             ((5 * depth, KP, slots), BF16),
             ((3 * depth, KP, slots), BF16),
@@ -407,44 +461,46 @@
             ((8 * KD, slots), F32),
             ((4 * depth, KD, slots), BF16),
             ((2 * depth, KD, slots), BF16),
-            ((2, 2, depth, slots), F32),
+            (long, F32),
+            ((2, *sums), F32),
         ],
-        left, own, right, here, velc,
+        *lists, left, own, right, here, velc,
     )
     recv1 = around(send1, "col", 1)
     p1, diag, send2 = local_call(
-        functools.partial(sweep1_kernel, *rows(2)),
+        functools.partial(sweep1_kernel, 1),
         [(plane, F32), (plane, F32), ((4, depth, slots), F32)],
-        [((4, depth, slots), F32), ((4, depth, slots), F32), ((2, 2, depth, slots), F32)],
-        feat_r, feat_l, left, own, recv1, weight, source, back,
+        [(long, F32), (long, F32), ((2, *sums), F32)],
+        *lists, feat_r, feat_l, left, own, recv1, weight, source, back,
     )
     recv2 = around(send2, "col", -1)
     (p2,) = local_call(
-        functools.partial(sweep2_kernel, *rows(3)),
+        functools.partial(sweep2_kernel, 2),
         [(plane, F32)],
-        [((4, depth, slots), F32), (plane, F32)],
-        feat_r, feat_l, own, recv1, recv2, weight, source, diag, p1, here,
+        [(long, F32), (sums, F32)],
+        *lists, feat_r, feat_l, own, recv1, recv2, weight, source, diag, p1, here,
     )
     recv3 = around(p2, "col", 1)
     (p3,) = local_call(
-        functools.partial(sweep3_kernel, *rows(4)),
+        functools.partial(sweep3_kernel, 3),
         [(plane, F32)],
-        [((4, depth, slots), F32), (plane, F32)],
-        feat_r, feat_l, left, own, recv1, recv3, weight, source, diag, p2, back,
+        [(long, F32), (sums, F32)],
+        *lists, feat_r, feat_l, left, own, recv1, recv3, weight, source, diag, p2, back,
     )
     recv4 = around(p3, "col", -1)
     inner = (2, cells, slots)
     pressure, acceleration, velocity_new, offsets_new = local_call(
-        functools.partial(force_kernel, *rows(5)),
+        functools.partial(force_kernel, 4),
         [(inner, F32), ((2, *inner), F32), ((2, *inner), F32), ((2, *inner), F32)],
-        [((4, depth, slots), F32)] * 4
+        [((4, depth, slots), F32)] * 2
+        + [(long, F32)] * 2
         + [
             ((4 * depth, KE, slots), BF16),
             ((2 * depth, KE, slots), BF16),
             ((8 * KE, slots), F32),
-            ((3, *plane), F32),
+            ((3, *sums), F32),
         ],
-        feat_r, feat_l, own, recv1, recv2, recv4, left, right, weight, p3, here,
+        *lists, feat_r, feat_l, own, recv1, recv2, recv4, left, right, weight, p3, here,
     )
     density_ratio = density_ratio[:, HALO : HALO + cells]
     state = jnp.concatenate([offsets_new, velocity_new, pressure[None], live_mass[None]], 0).reshape(6, -1)

time: 278 us -> 203 us (0.73); the launches traced: 278 us -> 200 us
  Pallas kernels: 208 us -> 124 us
    pallas_call x5, Pallas kernels: 208 us -> 124 us  [local_call(): pl.pallas_call(kernel, out_shape=[jax.ShapeDtypeStruct(shape, dtype) for...]
    concatenate x2 -> x1, local copies, waits for them, and re-layouts: 6.5 us -> 5.29 us  [per_device(): jnp.concatenate([offsets_new, velocity_new, pressure[None], live_mass[Non...]
  transfers between devices with their start and end apart: 10 -> 10, of which waited for: 9 -> 7; matrix products, arithmetic and copies ran while one was open for 1% -> 3% of each run, Pallas kernels for 0% -> 0%
where the time goes in v3:
time: 203 us; the launch traced here: 200 us
  Pallas kernels  124 us (61%)
  waiting for transfers between devices  31.2 us (15%)
  local copies, waits for them, and re-layouts  20.9 us (10%)
  starting transfers between devices  13.6 us (7%)
  other arithmetic  8.73 us (4%)
    pallas_call x5, Pallas kernels, local_call(): pl.pallas_call(kernel, out_shape=[jax.ShapeDtypeStruct(shape, dtype) for...  124 us
    ppermute x6, waiting for transfers between devices, around(): lax.ppermute(block, axis, [(i, (i + distance) % peers) for i in range(pee...  23.9 us
    ppermute x4, starting transfers between devices, from_behind(): return lax.ppermute(block, axis, route)  10.1 us
    ppermute x4, waiting for transfers between devices, from_behind(): return lax.ppermute(block, axis, route)  7.34 us
    gather x1, local copies, waits for them, and re-layouts, per_device(): blocks = state[:, leaving_slot.reshape(-1)].reshape(6, block_rows, 1, slots)  6.18 us
    concatenate x1, local copies, waits for them, and re-layouts, per_device(): jnp.concatenate([offsets_new, velocity_new, pressure[None], live_mass[Non...  5.29 us
  transfers between devices with their start and end apart: 10, of which 7 were waited for; matrix products, arithmetic and copies ran while one was open for 3% of the time, Pallas kernels for 0%

profile of v3, /device:TPU:28, one launch (start us, length us, event | category | flops | bytes accessed | tf_op | source)
XLA Modules:
  0.0 199.9 jit_solution(469041438867167982)
XLA Ops:
  0.6 0.9 fusion.8
  1.6 0.8 pad_maximum_fusion.5
  2.4 2.4 %collective-permute-start.1 = (f32[6,2,8,128]{3,2,1,0:T(8,128)S(1)}, f32[6,2,8,128]{3,2,1,0:T(8,128)S(1)}, u32[]{:S(2)}, u32[]{:S(2)}) collective-permute-start(f32[6,2,8,128]{3,2,1,0:T(8,128)S(1)} %get-tuple-element.40), channel_id=1, source_target_pairs={{1,0},{2,1},{3,2},{5,4},{6,5},{7,6},{9,8},{10,9},{11,10},{13,12},{... | collective-permute-start | bytes 147464 | tf_op jit(solution)/shard_map/ppermute | solution.py:416
  4.7 1.3 collective-permute-start
  6.1 0.8 select_convert_fusion
  6.9 3.9 %collective-permute-done = f32[6,2,8,128]{3,2,1,0:T(8,128)S(1)} collective-permute-done((f32[6,2,8,128]{3,2,1,0:T(8,128)S(1)}, f32[6,2,8,128]{3,2,1,0:T(8,128)S(1)}, u32[]{:S(2)}, u32[]{:S(2)}) %collective-permute-start) | collective-permute-done | bytes 49184 | tf_op jit(solution)/shard_map/ppermute | solution.py:416
  10.7 1.0 pad_maximum_fusion.1.own
  11.9 1.0 fusion
  12.9 2.6 %collective-permute-start.3 = (f32[5,1,80,128]{3,2,1,0:T(8,128)S(1)}, f32[5,1,80,128]{3,2,1,0:T(8,128)S(1)}, u32[]{:S(2)}, u32[]{:S(2)}) collective-permute-start(f32[5,1,80,128]{3,2,1,0:T(8,128)S(1)} %slice.44), channel_id=1, source_target_pairs={{0,28},{4,0},{8,4},{12,8},{16,12},{20,16},{24,20},{28,24},{1,29},{... | collective-permute-start | bytes 614408 | tf_op jit(solution)/shard_map/ppermute | solution.py:421
  15.5 7.7 %collective-permute-done.2.left = f32[6,2,80,128]{3,2,1,0:T(8,128)S(1)} collective-permute-done((f32[6,2,80,128]{3,2,1,0:T(8,128)S(1)}, f32[6,2,80,128]{3,2,1,0:T(8,128)S(1)}, u32[]{:S(2)}, u32[]{:S(2)}) %collective-permute-start.2) | collective-permute-done | bytes 491552 | tf_op jit(solution)/shard_map/ppermute | solution.py:421
  26.4 0.8 broadcast_in_dim.129.posc
  27.2 1.5 broadcast_in_dim.130.velc
  28.7 37.9 %shard_map.190 = (bf16[400,32,128]{2,1,0:T(8,128)(2,1)}, bf16[240,32,128]{2,1,0:T(8,128)(2,1)}, f32[2,80,128]{2,1,0:T(8,128)}, f32[2,80,128]{2,1,0:T(8,128)}, f3...) custom-call(s32[5,176]{1,0:T(8,128)} %fusion.1.order, s32[5,5]{1,0:T(8,128)} %stack.40.bounds, f32[6,2,80,128]{3,2,1,0:T(8,128)} %copy-done.1, ...), custom_call_target="tpu_custom_call" | custom-call | tf_op jit(solution)/shard_map/pallas_call | solution.py:403
  66.6 0.7 compare_select_fusion
  67.3 4.7 %collective-permute-done.4.recv.recv1 = f32[3,80,128]{2,1,0:T(8,128)S(1)} collective-permute-done((f32[3,80,128]{2,1,0:T(8,128)}, f32[3,80,128]{2,1,0:T(8,128)S(1)}, u32[]{:S(2)}, u32[]{:S(2)}) %collective-permute-start.4) | collective-permute-done | bytes 122912 | tf_op jit(solution)/shard_map/ppermute | solution.py:421
  72.0 0.8 broadcast_in_dim.131.posc
  72.8 23.4 %shard_map.191 = (f32[2,80,128]{2,1,0:T(8,128)}, f32[2,80,128]{2,1,0:T(8,128)}, f32[4,80,128]{2,1,0:T(8,128)}) custom-call(s32[5,176]{1,0:T(8,128)} %fusion.1.order, s32[5,5]{1,0:T(8,128)} %stack.40.bounds, bf16[400,32,128]{2,1,0:T(8,128)(2,1)} %get-tuple-element.20.feat_r, bf16[240,32,128]{2,1,0:T(8,128)(2,1)} %get-tuple-element.21.feat_l, ...), custom_call_target="tpu_custom_call" | custom-call | tf_op jit(solution)/shard_map/pallas_call | solution.py:403
  96.2 3.1 %collective-permute-done.5.recv2 = f32[4,80,128]{2,1,0:T(8,128)S(1)} collective-permute-done((f32[4,80,128]{2,1,0:T(8,128)}, f32[4,80,128]{2,1,0:T(8,128)S(1)}, u32[]{:S(2)}, u32[]{:S(2)}) %collective-permute-start.5) | collective-permute-done | bytes 163872 | tf_op jit(solution)/shard_map/ppermute | solution.py:421
  99.3 0.7 copy-done.4
  100.0 16.8 %shard_map.192.p2 = f32[2,80,128]{2,1,0:T(8,128)} custom-call(s32[5,176]{1,0:T(8,128)} %fusion.1.order, s32[5,5]{1,0:T(8,128)} %stack.40.bounds, bf16[400,32,128]{2,1,0:T(8,128)(2,1)} %get-tuple-element.20.feat_r, bf16[240,32,128]{2,1,0:T(8,128)(2,1)} %get-tuple-element.21.feat_l, f32[6,2,80,128]{3,2,1,0:T(8,128)} %copy-done, f32[3,80,128]{2,1,0:T(8,128)} %copy-done.2, ...), custom_call_target="tpu_custom_call" | custom-call | tf_op jit(solution)/shard_map/pallas_call | solution.py:403
  117.3 6.1 %collective-permute-done.6.recv3 = f32[2,80,128]{2,1,0:T(8,128)S(1)} collective-permute-done((f32[2,80,128]{2,1,0:T(8,128)}, f32[2,80,128]{2,1,0:T(8,128)S(1)}, u32[]{:S(2)}, u32[]{:S(2)}) %collective-permute-start.6) | collective-permute-done | bytes 81952 | tf_op jit(solution)/shard_map/ppermute | solution.py:421
  124.0 16.7 %shard_map.193.p3 = f32[2,80,128]{2,1,0:T(8,128)} custom-call(s32[5,176]{1,0:T(8,128)} %fusion.1.order, s32[5,5]{1,0:T(8,128)} %stack.40.bounds, bf16[400,32,128]{2,1,0:T(8,128)(2,1)} %get-tuple-element.20.feat_r, bf16[240,32,128]{2,1,0:T(8,128)(2,1)} %get-tuple-element.21.feat_l, f32[6,2,80,128]{3,2,1,0:T(8,128)} %copy-done.1, f32[6,2,80,128]{3,2,1,0:T(8,128)} %copy-done, ...), custom_call_target="tpu_custom_call" | custom-call | tf_op jit(solution)/shard_map/pallas_call | solution.py:403
  141.2 2.3 %collective-permute-done.7.recv4 = f32[2,80,128]{2,1,0:T(8,128)S(1)} collective-permute-done((f32[2,80,128]{2,1,0:T(8,128)}, f32[2,80,128]{2,1,0:T(8,128)S(1)}, u32[]{:S(2)}, u32[]{:S(2)}) %collective-permute-start.7) | collective-permute-done | bytes 81952 | tf_op jit(solution)/shard_map/ppermute | solution.py:421
  144.1 29.7 %shard_map.194 = (f32[2,64,128]{2,1,0:T(8,128)}, f32[2,2,64,128]{3,2,1,0:T(8,128)}, f32[2,2,64,128]{3,2,1,0:T(8,128)}, f32[2,2,64,128]{3,2,1,0:T(8,128)}) custom-call(s32[5,176]{1,0:T(8,128)} %fusion.1.order, s32[5,5]{1,0:T(8,128)} %stack.40.bounds, bf16[400,32,128]{2,1,0:T(8,128)(2,1)} %get-tuple-element.20.feat_r, ...), custom_call_target="tpu_custom_call" | custom-call | tf_op jit(solution)/shard_map/pallas_call | solution.py:403
  173.8 1.0 copy.55
  174.8 1.0 copy.56
  175.9 1.1 pad_maximum_fusion
  176.9 5.3 %copy.47 = f32[6,16384]{0,1:T(8,128)} copy(f32[6,16384]{1,0:T(8,128)S(1)} %pad_maximum_fusion) | data formatting | bytes 786432 | tf_op jit(solution)/shard_map/concatenate | solution.py:506
  182.2 6.2 %gather_fusion = f32[1024,6]{1,0:T(8,128)S(1)} fusion(f32[6,16384]{0,1:T(8,128)} %copy.47, s32[1024]{0:T(1024)S(1)} %broadcast_clamp_fusion), kind=kCustom, calls=%fused_computation | custom fusion | bytes 53248 | tf_op jit(solution)/shard_map/gather | solution.py:508
  188.6 4.5 %collective-permute-start.9 = (f32[6,8,1,128]{3,1,0,2:T(8,128)S(1)}, f32[6,8,1,128]{3,1,0,2:T(8,128)S(1)}, u32[]{:S(2)}, u32[]{:S(2)}) collective-permute-start(f32[6,8,1,128]{3,1,0,2:T(8,128)S(1)} %get-tuple-element.42), channel_id=1, source_target_pairs={{4,0},{8,4},{12,8},{16,12},{20,16},{24,20},{28,24},{5,1},{9,5},{13... | collective-permute-start | bytes 73736 | tf_op jit(solution)/shard_map/ppermute | solution.py:416
  193.1 1.9 collective-permute-start.8
  195.7 3.5 %collective-permute-done.8 = f32[6,8,1,128]{3,1,0,2:T(8,128)S(1)} collective-permute-done((f32[6,8,1,128]{3,1,0,2:T(8,128)S(1)}, f32[6,8,1,128]{3,1,0,2:T(8,128)S(1)}, u32[]{:S(2)}, u32[]{:S(2)}) %collective-permute-start.8) | collective-permute-done | bytes 24608 | tf_op jit(solution)/shard_map/ppermute | solution.py:416
  (58 shorter events, 7.1 us)
Async XLA Ops:
  2.4 4.5 %collective-permute-start.1 = (f32[6,2,8,128]{3,2,1,0:T(8,128)S(1)}, f32[6,2,8,128]{3,2,1,0:T(8,128)S(1)}, u32[]{:S(2)}, u32[]{:S(2)}) collective-permute-start(f32[6,2,8,128]{3,2,1,0:T(8,128)S(1)} %get-tuple-element.40), channel_id=1, source_target_pairs={{1,0},{2,1},{3,2},{5,4},{6,5},{7,6},{9,8},{10,9},{11,10},{13,12},{... | collective-permute-start | bytes 147464 | tf_op jit(solution)/shard_map/ppermute | solution.py:416
  4.7 6.0 %collective-permute-start = (f32[6,2,8,128]{3,2,1,0:T(8,128)S(1)}, f32[6,2,8,128]{3,2,1,0:T(8,128)S(1)}, u32[]{:S(2)}, u32[]{:S(2)}) collective-permute-start(f32[6,2,8,128]{3,2,1,0:T(8,128)S(1)} %get-tuple-element.39), channel_id=1, source_target_pairs={{0,1},{1,2},{2,3},{4,5},{5,6},{6,7},{8,9},{9,10},{10,11},{12,13},{... | collective-permute-start | bytes 147464 | tf_op jit(solution)/shard_map/ppermute | solution.py:416
  11.8 16.9 %copy-start = (f32[6,2,80,128]{3,2,1,0:T(8,128)}, f32[6,2,80,128]{3,2,1,0:T(8,128)S(1)}, u32[]{:S(2)}) copy-start(f32[6,2,80,128]{3,2,1,0:T(8,128)S(1)} %pad_maximum_fusion.1.own) | copy-start | bytes 1474564
  11.8 105.5 %copy-start.9 = (s32[8,1]{0,1:T(1,128)S(1)}, s32[8,1]{0,1:T(1,128)}, u32[]{:S(2)}) copy-start(s32[8,1]{0,1:T(1,128)} %param.22) | copy-start | bytes 100
  11.8 11.4 %collective-permute-start.2 = (f32[6,2,80,128]{3,2,1,0:T(8,128)S(1)}, f32[6,2,80,128]{3,2,1,0:T(8,128)S(1)}, u32[]{:S(2)}, u32[]{:S(2)}) collective-permute-start(f32[6,2,80,128]{3,2,1,0:T(8,128)S(1)} %pad_maximum_fusion.1.own), channel_id=1, source_target_pairs={{0,4},{4,8},{8,12},{12,16},{16,20},{20,24},{24,28},{28,0},{1,5},{5... | collective-permute-start | bytes 1474568 | tf_op jit(solution)/shard_map/ppermute | solution.py:421
  12.9 13.5 %collective-permute-start.3 = (f32[5,1,80,128]{3,2,1,0:T(8,128)S(1)}, f32[5,1,80,128]{3,2,1,0:T(8,128)S(1)}, u32[]{:S(2)}, u32[]{:S(2)}) collective-permute-start(f32[5,1,80,128]{3,2,1,0:T(8,128)S(1)} %slice.44), channel_id=1, source_target_pairs={{0,28},{4,0},{8,4},{12,8},{16,12},{20,16},{24,20},{28,24},{1,29},{... | collective-permute-start | bytes 614408 | tf_op jit(solution)/shard_map/ppermute | solution.py:421
  23.2 5.5 %copy-start.1 = (f32[6,2,80,128]{3,2,1,0:T(8,128)}, f32[6,2,80,128]{3,2,1,0:T(8,128)S(1)}, u32[]{:S(2)}) copy-start(f32[6,2,80,128]{3,2,1,0:T(8,128)S(1)} %collective-permute-done.2.left) | copy-start | bytes 1474564
  26.4 2.3 %copy-start.3 = (f32[5,1,80,128]{3,2,1,0:T(8,128)}, f32[5,1,80,128]{3,2,1,0:T(8,128)S(1)}, u32[]{:S(2)}) copy-start(f32[5,1,80,128]{3,2,1,0:T(8,128)S(1)} %collective-permute-done.3.right) | copy-start | bytes 614404
  66.6 5.4 %collective-permute-start.4 = (f32[3,80,128]{2,1,0:T(8,128)}, f32[3,80,128]{2,1,0:T(8,128)S(1)}, u32[]{:S(2)}, u32[]{:S(2)}) collective-permute-start(f32[3,80,128]{2,1,0:T(8,128)} %get-tuple-element.22), channel_id=1, source_target_pairs={{0,4},{4,8},{8,12},{12,16},{16,20},{20,24},{24,28},{28,0},{1,5},{5... | collective-permute-start | bytes 368648 | tf_op jit(solution)/shard_map/ppermute | solution.py:421
  72.0 0.8 copy-start.2
  96.2 44.9 %copy-start.8 = (s32[8,1]{0,1:T(1,128)S(1)}, s32[8,1]{0,1:T(1,128)}, u32[]{:S(2)}) copy-start(s32[8,1]{0,1:T(1,128)} %param.21) | copy-start | bytes 100
  96.2 3.2 %collective-permute-start.5 = (f32[4,80,128]{2,1,0:T(8,128)}, f32[4,80,128]{2,1,0:T(8,128)S(1)}, u32[]{:S(2)}, u32[]{:S(2)}) collective-permute-start(f32[4,80,128]{2,1,0:T(8,128)} %get-tuple-element.25), channel_id=1, source_target_pairs={{0,28},{4,0},{8,4},{12,8},{16,12},{20,16},{24,20},{28,24},{1,29},{... | collective-permute-start | bytes 491528 | tf_op jit(solution)/shard_map/ppermute | solution.py:421
  99.3 0.7 copy-start.4
  116.8 6.6 %collective-permute-start.6 = (f32[2,80,128]{2,1,0:T(8,128)}, f32[2,80,128]{2,1,0:T(8,128)S(1)}, u32[]{:S(2)}, u32[]{:S(2)}) collective-permute-start(f32[2,80,128]{2,1,0:T(8,128)} %shard_map.192.p2), channel_id=1, source_target_pairs={{0,4},{4,8},{8,12},{12,16},{16,20},{20,24},{24,28},{28,0},{1,5},{5... | collective-permute-start | bytes 245768 | tf_op jit(solution)/shard_map/ppermute | solution.py:421
  123.4 0.6 copy-start.6
  140.7 2.8 %collective-permute-start.7 = (f32[2,80,128]{2,1,0:T(8,128)}, f32[2,80,128]{2,1,0:T(8,128)S(1)}, u32[]{:S(2)}, u32[]{:S(2)}) collective-permute-start(f32[2,80,128]{2,1,0:T(8,128)} %shard_map.193.p3), channel_id=1, source_target_pairs={{0,28},{4,0},{8,4},{12,8},{16,12},{20,16},{24,20},{28,24},{1,29},{... | collective-permute-start | bytes 245768 | tf_op jit(solution)/shard_map/ppermute | solution.py:421
  141.1 53.9 %copy-start.7 = (f32[2,80,128]{2,1,0:T(8,128)S(1)}, f32[2,80,128]{2,1,0:T(8,128)}, u32[]{:S(2)}) copy-start(f32[2,80,128]{2,1,0:T(8,128)} %get-tuple-element.19) | copy-start | bytes 245764
  143.4 0.6 copy-start.5
  188.6 7.1 %collective-permute-start.9 = (f32[6,8,1,128]{3,1,0,2:T(8,128)S(1)}, f32[6,8,1,128]{3,1,0,2:T(8,128)S(1)}, u32[]{:S(2)}, u32[]{:S(2)}) collective-permute-start(f32[6,8,1,128]{3,1,0,2:T(8,128)S(1)} %get-tuple-element.42), channel_id=1, source_target_pairs={{4,0},{8,4},{12,8},{16,12},{20,16},{24,20},{28,24},{5,1},{9,5},{13... | collective-permute-start | bytes 73736 | tf_op jit(solution)/shard_map/ppermute | solution.py:416
  193.1 6.0 %collective-permute-start.8 = (f32[6,8,1,128]{3,1,0,2:T(8,128)S(1)}, f32[6,8,1,128]{3,1,0,2:T(8,128)S(1)}, u32[]{:S(2)}, u32[]{:S(2)}) collective-permute-start(f32[6,8,1,128]{3,1,0,2:T(8,128)S(1)} %get-tuple-element.41), channel_id=1, source_target_pairs={{0,4},{4,8},{8,12},{12,16},{16,20},{20,24},{24,28},{1,5},{5,9},{9,... | collective-permute-start | bytes 73736 | tf_op jit(solution)/shard_map/ppermute | solution.py:416

commit v4 on v3

--- a/solution.py
+++ b/solution.py
@@ -17,6 +17,8 @@
 
 HALO = 8
 CLASSES = ((32, 16), (64, 8), (96, 6), (128, 6))
+CHUNKS = ((0, 1), (2, 3), (4, 5), (6, 7), (8,))
+AHEAD = 2
 KP = 32
 KD = 48
 KE = 16
@@ -125,13 +127,16 @@
     return rows.astype(F32).T[:slots].astype(BF16)
 
 
-def tiles(left, sources):
-    product = jnp.dot(left, jnp.concatenate(sources, axis=1), preferred_element_type=F32)
-    return [product[:, 128 * i : 128 * (i + 1)] for i in range(3)]
-
-
-def signed(feat, cell, table, first):
-    return [feat[cell + sz] * table[first + sz + 1] for sz in (-1, 0, 1)]
+def sources_of(feat, cell, depth, chunk, table=None, first=0):
+    parts = []
+    for n in chunk:
+        part = feat[cell + (n // 3) * depth + n % 3 - 1]
+        parts.append(part if table is None else part * table[first + n])
+    return jnp.concatenate(parts, axis=1) if len(parts) > 1 else parts[0]
+
+
+def product(left, right):
+    return jnp.dot(left, right, preferred_element_type=F32)
 
 
 def fold(total):
@@ -144,11 +149,25 @@
         steps = (bounds[level, index + 1] - start + cells - 1) // cells
 
         def step(i, carry, slots=slots, cells=cells, start=start):
+            waiting = []
             for u in range(cells):
-                target(order[level, start + i * cells + u], slots)
+                issue, consume, finish = target(order[level, start + i * cells + u], slots)
+                for chunk in CHUNKS:
+                    waiting.append((consume, chunk, issue(chunk), finish))
+                    if len(waiting) > AHEAD:
+                        take(waiting.pop(0))
+            for entry in waiting:
+                take(entry)
             return carry
 
         lax.fori_loop(0, steps, step, 0)
+
+
+def take(entry):
+    consume, chunk, products, finish = entry
+    consume(chunk, products)
+    if chunk is CHUNKS[-1]:
+        finish()
 
 
 def density_kernel(
@@ -187,19 +206,27 @@
     def target(cell, slots):
         sign = 9 * (cell >= depth).astype(jnp.int32)
         pos_l, vel_l_t = upright(out_l[cell + depth], slots), upright(vel_l[cell], slots)
-        rho = jnp.zeros((slots, 128), F32)
-        div = jnp.zeros((slots, 128), F32)
-        for sx in range(3):
-            source = cell + sx * depth
-            reach = tiles(pos_l, signed(out_r, source + depth, posc, sign + 3 * sx))
-            closing = tiles(vel_l_t, signed(vel_r, source, velc, 3 * sx))
-            for sz in range(3):
-                s = jnp.maximum(reach[sz], 0.0)
-                q = s * s * wide_m[pl.ds(source + sz - 1, 1), :]
-                rho = rho + q * s
-                div = div + q * closing[sz]
-        acc[0, pl.ds(cell, 1), 0:slots] = fold(rho)
-        acc[1, pl.ds(cell, 1), 0:slots] = fold(div)
+        sums = [jnp.zeros((slots, 128), F32)] * 2
+
+        def issue(chunk):
+            return (
+                product(pos_l, sources_of(out_r, cell + depth, depth, chunk, posc, sign)),
+                product(vel_l_t, sources_of(vel_r, cell, depth, chunk, velc)),
+            )
+
+        def consume(chunk, products):
+            for i, n in enumerate(chunk):
+                lanes = slice(128 * i, 128 * (i + 1))
+                s = jnp.maximum(products[0][:, lanes], 0.0)
+                q = s * s * wide_m[pl.ds(cell + (n // 3) * depth + n % 3 - 1, 1), :]
+                sums[0] = sums[0] + q * s
+                sums[1] = sums[1] + q * products[1][:, lanes]
+
+        def finish():
+            for i in range(2):
+                acc[i, pl.ds(cell, 1), 0:slots] = fold(sums[i])
+
+        return issue, consume, finish
 
     each_target(level, order, bounds, target)
     density = acc[0].reshape(2, depth, 128)
@@ -228,13 +255,21 @@
         sign = 9 * (cell >= depth).astype(jnp.int32)
         at = cell + first_col * depth
         pos_l = upright(feat_l[at], slots)
-        total = jnp.zeros((slots, 128), F32)
-        for sx in range(3):
-            reach = tiles(pos_l, signed(feat_r, at + sx * depth, posc, sign + 3 * sx))
-            for sz in range(3):
-                s = jnp.maximum(reach[sz], 0.0)
-                total = total + s * s * wide_u[pl.ds(cell + sx * depth + sz - 1, 1), :]
-        acc[pl.ds(cell, 1), 0:slots] = fold(total)
+        sums = [jnp.zeros((slots, 128), F32)]
+
+        def issue(chunk):
+            return product(pos_l, sources_of(feat_r, at, depth, chunk, posc, sign))
+
+        def consume(chunk, products):
+            for i, n in enumerate(chunk):
+                s = jnp.maximum(products[:, 128 * i : 128 * (i + 1)], 0.0)
+                lifted = wide_u[pl.ds(cell + (n // 3) * depth + n % 3 - 1, 1), :]
+                sums[0] = sums[0] + s * s * lifted
+
+        def finish():
+            acc[pl.ds(cell, 1), 0:slots] = fold(sums[0])
+
+        return issue, consume, finish
 
     acc[...] = jnp.zeros_like(acc)
     each_target(level, order, bounds, target)
@@ -258,18 +293,24 @@
     def target(cell, slots):
         sign = 9 * (cell >= depth).astype(jnp.int32)
         pos_l = upright(feat_l[cell], slots)
-        total_w = jnp.zeros((slots, 128), F32)
-        total_u = jnp.zeros((slots, 128), F32)
-        for sx in range(3):
-            source = cell + sx * depth
-            reach = tiles(pos_l, signed(feat_r, source, posc, sign + 3 * sx))
-            for sz in range(3):
-                s = jnp.maximum(reach[sz], 0.0)
+        sums = [jnp.zeros((slots, 128), F32)] * 2
+
+        def issue(chunk):
+            return product(pos_l, sources_of(feat_r, cell, depth, chunk, posc, sign))
+
+        def consume(chunk, products):
+            for i, n in enumerate(chunk):
+                s = jnp.maximum(products[:, 128 * i : 128 * (i + 1)], 0.0)
                 q = s * s
-                total_w = total_w + q * wide_w[pl.ds(source + sz - 1, 1), :]
-                total_u = total_u + q * wide_u[pl.ds(source + sz - 1, 1), :]
-        acc[0, pl.ds(cell, 1), 0:slots] = fold(total_w)
-        acc[1, pl.ds(cell, 1), 0:slots] = fold(total_u)
+                at = pl.ds(cell + (n // 3) * depth + n % 3 - 1, 1)
+                sums[0] = sums[0] + q * wide_w[at, :]
+                sums[1] = sums[1] + q * wide_u[at, :]
+
+        def finish():
+            for i in range(2):
+                acc[i, pl.ds(cell, 1), 0:slots] = fold(sums[i])
+
+        return issue, consume, finish
 
     each_target(level, order, bounds, target)
     diagonal = COMPRESSION + 6.0 * acc[0].reshape(2, depth, 128)
@@ -342,23 +383,29 @@
     def target(cell, slots):
         sign = 9 * (cell >= depth).astype(jnp.int32)
         pos_l, pres_l_t = upright(feat_l[cell + depth], slots), upright(pres_l[cell], slots)
-        plain = jnp.zeros((slots, 128), F32)
-        by_x = jnp.zeros((slots, 128), F32)
-        by_z = jnp.zeros((slots, 128), F32)
-        for sx in range(3):
-            source = cell + sx * depth
-            reach = tiles(pos_l, signed(feat_r, source + depth, posc, sign + 3 * sx))
-            lift = tiles(pres_l_t, [pres_r[source + sz] for sz in (-1, 0, 1)])
-            for sz in range(3):
-                s = jnp.maximum(reach[sz], 0.0)
-                g = s * s * lift[sz]
-                at = pl.ds(source + sz - 1, 1)
-                plain = plain + g
-                by_x = by_x + g * (wide_x[at, :] + float(sx - 1))
-                by_z = by_z + g * (wide_z[at, :] + float(sz - 1))
-        acc[0, pl.ds(cell, 1), 0:slots] = fold(plain)
-        acc[1, pl.ds(cell, 1), 0:slots] = fold(by_x)
-        acc[2, pl.ds(cell, 1), 0:slots] = fold(by_z)
+        sums = [jnp.zeros((slots, 128), F32)] * 3
+
+        def issue(chunk):
+            return (
+                product(pos_l, sources_of(feat_r, cell + depth, depth, chunk, posc, sign)),
+                product(pres_l_t, sources_of(pres_r, cell, depth, chunk)),
+            )
+
+        def consume(chunk, products):
+            for i, n in enumerate(chunk):
+                lanes = slice(128 * i, 128 * (i + 1))
+                s = jnp.maximum(products[0][:, lanes], 0.0)
+                g = s * s * products[1][:, lanes]
+                at = pl.ds(cell + (n // 3) * depth + n % 3 - 1, 1)
+                sums[0] = sums[0] + g
+                sums[1] = sums[1] + g * (wide_x[at, :] + float(n // 3 - 1))
+                sums[2] = sums[2] + g * (wide_z[at, :] + float(n % 3 - 1))
+
+        def finish():
+            for i in range(3):
+                acc[i, pl.ds(cell, 1), 0:slots] = fold(sums[i])
+
+        return issue, consume, finish
 
     acc[...] = jnp.zeros_like(acc)
     each_target(level, order, bounds, target)
@@ -375,6 +422,33 @@
         out_acc[axis] = force
         out_velocity[axis] = velocity
         out_offsets[axis] = jnp.where(alive, own[axis, :, inner] + TIME_STEP * velocity, 0.0)
+
+
+def leaving_kernel(
+    slot, count, side, offsets, velocity, pressure, mass, out_up, out_down, hot
+):
+    blocks, slots = slot.shape
+    fields = [offsets[0], offsets[1], velocity[0], velocity[1], pressure[...], mass[...]]
+    fields = [f.reshape(-1, slots) for f in fields]
+    cells = fields[0].shape[0]
+    number = lax.broadcasted_iota(jnp.int32, (cells, slots), 0)
+    place = lax.broadcasted_iota(jnp.int32, (slots, slots), 0)
+    for b in range(blocks):
+        one_hot = (number == slot[b : b + 1, :] // slots).astype(F32).astype(BF16)
+        for part in range(3):
+            hot[part * cells : (part + 1) * cells, b * slots : (b + 1) * slots] = one_hot
+    filled = lax.broadcasted_iota(jnp.int32, (blocks, slots), 1) < count[...]
+    up = side[...] == 1
+    for index, field in enumerate(fields):
+        parts = jnp.concatenate([v.astype(BF16) for v in split3(field.T)], axis=1)
+        rows = []
+        for b in range(blocks):
+            picked = product(parts, hot[:, b * slots : (b + 1) * slots])
+            here = place == slot[b : b + 1, :] % slots
+            rows.append(jnp.sum(jnp.where(here, picked, 0.0), axis=0, keepdims=True))
+        block = jnp.where(filled, jnp.concatenate(rows, axis=0), 0.0)
+        out_up[index] = jnp.where(up, block, 0.0)
+        out_down[index] = jnp.where(up, 0.0, block)
 
 
 def target_lists(count, cells):
@@ -397,17 +471,17 @@
     return jnp.where(place < bounds[:, -1:], order, HALO), bounds
 
 
-def local_call(kernel, out_shapes, scratch, order, bounds, *operands):
+def local_call(kernel, out_shapes, scratch, scalars, *operands):
     vmem = pl.BlockSpec(memory_space=pltpu.VMEM)
     smem = pl.BlockSpec(memory_space=pltpu.SMEM)
     return pl.pallas_call(
         kernel,
         out_shape=[jax.ShapeDtypeStruct(shape, dtype) for shape, dtype in out_shapes],
-        in_specs=[smem] * 2 + [vmem] * len(operands),
+        in_specs=[smem] * len(scalars) + [vmem] * len(operands),
         out_specs=[vmem] * len(out_shapes),
         scratch_shapes=[pltpu.VMEM(shape, dtype) for shape, dtype in scratch],
         compiler_params=pltpu.CompilerParams(vmem_limit_bytes=VMEM_LIMIT),
-    )(order, bounds, *operands)
+    )(*scalars, *operands)
 
 
 def from_behind(block, axis, distance):
@@ -464,28 +538,28 @@
             (long, F32),
             ((2, *sums), F32),
         ],
-        *lists, left, own, right, here, velc,
+        lists, left, own, right, here, velc,
     )
     recv1 = around(send1, "col", 1)
     p1, diag, send2 = local_call(
         functools.partial(sweep1_kernel, 1),
         [(plane, F32), (plane, F32), ((4, depth, slots), F32)],
         [(long, F32), (long, F32), ((2, *sums), F32)],
-        *lists, feat_r, feat_l, left, own, recv1, weight, source, back,
+        lists, feat_r, feat_l, left, own, recv1, weight, source, back,
     )
     recv2 = around(send2, "col", -1)
     (p2,) = local_call(
         functools.partial(sweep2_kernel, 2),
         [(plane, F32)],
         [(long, F32), (sums, F32)],
-        *lists, feat_r, feat_l, own, recv1, recv2, weight, source, diag, p1, here,
+        lists, feat_r, feat_l, own, recv1, recv2, weight, source, diag, p1, here,
     )
     recv3 = around(p2, "col", 1)
     (p3,) = local_call(
         functools.partial(sweep3_kernel, 3),
         [(plane, F32)],
         [(long, F32), (sums, F32)],
-        *lists, feat_r, feat_l, left, own, recv1, recv3, weight, source, diag, p2, back,
+        lists, feat_r, feat_l, left, own, recv1, recv3, weight, source, diag, p2, back,
     )
     recv4 = around(p3, "col", -1)
     inner = (2, cells, slots)
@@ -500,16 +574,19 @@
             ((8 * KE, slots), F32),
             ((3, *sums), F32),
         ],
-        *lists, feat_r, feat_l, own, recv1, recv2, recv4, left, right, weight, p3, here,
+        lists, feat_r, feat_l, own, recv1, recv2, recv4, left, right, weight, p3, here,
     )
     density_ratio = density_ratio[:, HALO : HALO + cells]
-    state = jnp.concatenate([offsets_new, velocity_new, pressure[None], live_mass[None]], 0).reshape(6, -1)
-    block_rows = leaving_slot.shape[0]
-    blocks = state[:, leaving_slot.reshape(-1)].reshape(6, block_rows, 1, slots)
-    filled = jnp.arange(slots, dtype=jnp.int32)[None, None, :] < leaving_count[:, :, None]
-    upward = jnp.where(filled & (leaving_side[:, :, None] == 1), blocks, 0.0)
-    downward = jnp.where(filled & (leaving_side[:, :, None] == 0), blocks, 0.0)
-    arrived = jnp.stack([from_behind(upward, "col", 1), from_behind(downward, "col", -1)])
+    blocks = leaving_slot.shape[0]
+    packed = ((6, blocks, slots), F32)
+    upward, downward = local_call(
+        leaving_kernel,
+        [packed, packed],
+        [((3 * counts.size, blocks * slots), BF16)],
+        (),
+        leaving_slot[:, 0], leaving_count, leaving_side, offsets_new, velocity_new, pressure, live_mass,
+    )
+    arrived = jnp.stack([from_behind(upward, "col", 1), from_behind(downward, "col", -1)])[:, :, :, None]
     return (density_ratio, pressure, acceleration, velocity_new, offsets_new, arrived)
 
 

time: 203 us -> 191 us (0.941)
  local copies, waits for them, and re-layouts: 20.9 us -> 8.61 us
  Pallas kernels: 124 us -> 130 us
  other arithmetic: 8.73 us -> 6.61 us
    gather x1 -> x0, local copies, waits for them, and re-layouts: 6.18 us -> none  [per_device(): blocks = state[:, leaving_slot.reshape(-1)].reshape(6, block_rows, 1, slots)]
    pallas_call x5 -> x6, Pallas kernels: 124 us -> 130 us  [local_call(): pl.pallas_call(kernel, out_shape=[jax.ShapeDtypeStruct(shape, dtype) for...]
    concatenate x1 -> x0, local copies, waits for them, and re-layouts: 5.29 us -> none  [per_device(): jnp.concatenate([offsets_new, velocity_new, pressure[None], live_mass[Non...]
    ppermute x6, waiting for transfers between devices: 23.9 us -> 21.4 us  [around(): lax.ppermute(block, axis, [(i, (i + distance) % peers) for i in range(pee...]
  transfers between devices with their start and end apart: 10 -> 10, of which waited for: 7 -> 8; matrix products, arithmetic and copies ran while one was open for 3% -> 4% of each run, Pallas kernels for 0% -> 0%
where the time goes in v4:
time: 191 us; the launch traced here: 189 us
  Pallas kernels  130 us (68%)
  waiting for transfers between devices  29.8 us (16%)
  starting transfers between devices  13 us (7%)
  local copies, waits for them, and re-layouts  8.61 us (5%)
  other arithmetic  6.61 us (3%)
    pallas_call x6, Pallas kernels, local_call(): pl.pallas_call(kernel, out_shape=[jax.ShapeDtypeStruct(shape, dtype) for...  130 us
    ppermute x6, waiting for transfers between devices, around(): lax.ppermute(block, axis, [(i, (i + distance) % peers) for i in range(pee...  21.4 us
    ppermute x4, starting transfers between devices, from_behind(): return lax.ppermute(block, axis, route)  9.42 us
    ppermute x4, waiting for transfers between devices, from_behind(): return lax.ppermute(block, axis, route)  8.34 us
  transfers between devices with their start and end apart: 10, of which 8 were waited for; matrix products, arithmetic and copies ran while one was open for 4% of the time, Pallas kernels for 0%

profile of v4, /device:TPU:28, one launch (start us, length us, event | category | flops | bytes accessed | tf_op | source)
XLA Modules:
  0.0 189.0 jit_solution(15576388989414575066)
XLA Ops:
  0.6 0.9 fusion.6
  1.6 0.8 pad_maximum_fusion.4
  2.4 2.4 %collective-permute-start.1 = (f32[6,2,8,128]{3,2,1,0:T(8,128)S(1)}, f32[6,2,8,128]{3,2,1,0:T(8,128)S(1)}, u32[]{:S(2)}, u32[]{:S(2)}) collective-permute-start(f32[6,2,8,128]{3,2,1,0:T(8,128)S(1)} %get-tuple-element.56), channel_id=1, source_target_pairs={{1,0},{2,1},{3,2},{5,4},{6,5},{7,6},{9,8},{10,9},{11,10},{13,12},{... | collective-permute-start | bytes 147464 | tf_op jit(solution)/shard_map/ppermute | solution.py:490
  4.7 1.3 collective-permute-start
  6.5 4.3 %collective-permute-done = f32[6,2,8,128]{3,2,1,0:T(8,128)S(1)} collective-permute-done((f32[6,2,8,128]{3,2,1,0:T(8,128)S(1)}, f32[6,2,8,128]{3,2,1,0:T(8,128)S(1)}, u32[]{:S(2)}, u32[]{:S(2)}) %collective-permute-start) | collective-permute-done | bytes 49184 | tf_op jit(solution)/shard_map/ppermute | solution.py:490
  10.7 1.0 pad_maximum_fusion.own
  11.9 0.9 select_convert_fusion
  12.8 2.6 %collective-permute-start.3 = (f32[5,1,80,128]{3,2,1,0:T(8,128)S(1)}, f32[5,1,80,128]{3,2,1,0:T(8,128)S(1)}, u32[]{:S(2)}, u32[]{:S(2)}) collective-permute-start(f32[5,1,80,128]{3,2,1,0:T(8,128)S(1)} %slice.42), channel_id=1, source_target_pairs={{0,28},{4,0},{8,4},{12,8},{16,12},{20,16},{24,20},{28,24},{1,29},{... | collective-permute-start | bytes 614408 | tf_op jit(solution)/shard_map/ppermute | solution.py:495
  15.3 7.8 %collective-permute-done.2.left = f32[6,2,80,128]{3,2,1,0:T(8,128)S(1)} collective-permute-done((f32[6,2,80,128]{3,2,1,0:T(8,128)S(1)}, f32[6,2,80,128]{3,2,1,0:T(8,128)S(1)}, u32[]{:S(2)}, u32[]{:S(2)}) %collective-permute-start.2) | collective-permute-done | bytes 491552 | tf_op jit(solution)/shard_map/ppermute | solution.py:495
  25.1 0.7 stack.40.bounds
  25.7 0.7 fusion.1.order
  26.4 0.8 broadcast_in_dim.113.posc
  27.2 1.5 broadcast_in_dim.114.velc
  28.7 37.4 %shard_map.190 = (bf16[400,32,128]{2,1,0:T(8,128)(2,1)}, bf16[240,32,128]{2,1,0:T(8,128)(2,1)}, f32[2,80,128]{2,1,0:T(8,128)}, f32[2,80,128]{2,1,0:T(8,128)}, f3...) custom-call(s32[5,176]{1,0:T(8,128)} %fusion.1.order, s32[5,5]{1,0:T(8,128)} %stack.40.bounds, f32[6,2,80,128]{3,2,1,0:T(8,128)} %copy-done.1, ...), custom_call_target="tpu_custom_call" | custom-call | tf_op jit(solution)/shard_map/pallas_call | solution.py:477
  66.1 5.4 %collective-permute-done.4.recv.recv1 = f32[3,80,128]{2,1,0:T(8,128)S(1)} collective-permute-done((f32[3,80,128]{2,1,0:T(8,128)}, f32[3,80,128]{2,1,0:T(8,128)S(1)}, u32[]{:S(2)}, u32[]{:S(2)}) %collective-permute-start.4) | collective-permute-done | bytes 122912 | tf_op jit(solution)/shard_map/ppermute | solution.py:495
  71.5 0.8 broadcast_in_dim.115.posc
  72.3 24.3 %shard_map.191 = (f32[2,80,128]{2,1,0:T(8,128)}, f32[2,80,128]{2,1,0:T(8,128)}, f32[4,80,128]{2,1,0:T(8,128)}) custom-call(s32[5,176]{1,0:T(8,128)} %fusion.1.order, s32[5,5]{1,0:T(8,128)} %stack.40.bounds, bf16[400,32,128]{2,1,0:T(8,128)(2,1)} %get-tuple-element.22.feat_r, bf16[240,32,128]{2,1,0:T(8,128)(2,1)} %get-tuple-element.23.feat_l, ...), custom_call_target="tpu_custom_call" | custom-call | tf_op jit(solution)/shard_map/pallas_call | solution.py:477
  96.8 3.2 %collective-permute-done.5.recv2 = f32[4,80,128]{2,1,0:T(8,128)S(1)} collective-permute-done((f32[4,80,128]{2,1,0:T(8,128)}, f32[4,80,128]{2,1,0:T(8,128)S(1)}, u32[]{:S(2)}, u32[]{:S(2)}) %collective-permute-start.5) | collective-permute-done | bytes 163872 | tf_op jit(solution)/shard_map/ppermute | solution.py:495
  100.0 0.7 copy-done.4
  100.6 17.6 %shard_map.192.p2 = f32[2,80,128]{2,1,0:T(8,128)} custom-call(s32[5,176]{1,0:T(8,128)} %fusion.1.order, s32[5,5]{1,0:T(8,128)} %stack.40.bounds, bf16[400,32,128]{2,1,0:T(8,128)(2,1)} %get-tuple-element.22.feat_r, bf16[240,32,128]{2,1,0:T(8,128)(2,1)} %get-tuple-element.23.feat_l, f32[6,2,80,128]{3,2,1,0:T(8,128)} %copy-done, f32[3,80,128]{2,1,0:T(8,128)} %copy-done.2, ...), custom_call_target="tpu_custom_call" | custom-call | tf_op jit(solution)/shard_map/pallas_call | solution.py:477
  118.3 0.8 collective-permute-start.6
  119.1 4.7 %collective-permute-done.6.recv3 = f32[2,80,128]{2,1,0:T(8,128)S(1)} collective-permute-done((f32[2,80,128]{2,1,0:T(8,128)}, f32[2,80,128]{2,1,0:T(8,128)S(1)}, u32[]{:S(2)}, u32[]{:S(2)}) %collective-permute-start.6) | collective-permute-done | bytes 81952 | tf_op jit(solution)/shard_map/ppermute | solution.py:495
  124.5 17.5 %shard_map.193.p3 = f32[2,80,128]{2,1,0:T(8,128)} custom-call(s32[5,176]{1,0:T(8,128)} %fusion.1.order, s32[5,5]{1,0:T(8,128)} %stack.40.bounds, bf16[400,32,128]{2,1,0:T(8,128)(2,1)} %get-tuple-element.22.feat_r, bf16[240,32,128]{2,1,0:T(8,128)(2,1)} %get-tuple-element.23.feat_l, f32[6,2,80,128]{3,2,1,0:T(8,128)} %copy-done.1, f32[6,2,80,128]{3,2,1,0:T(8,128)} %copy-done, ...), custom_call_target="tpu_custom_call" | custom-call | tf_op jit(solution)/shard_map/pallas_call | solution.py:477
  141.9 0.7 fusion.mass
  142.7 0.7 copy.34.count
  143.3 0.7 copy.35.side
  144.3 0.6 copy-done.6
  145.0 30.1 %shard_map.194 = (f32[2,64,128]{2,1,0:T(8,128)}, f32[2,2,64,128]{3,2,1,0:T(8,128)}, f32[2,2,64,128]{3,2,1,0:T(8,128)}, f32[2,2,64,128]{3,2,1,0:T(8,128)}) custom-call(s32[5,176]{1,0:T(8,128)} %fusion.1.order, s32[5,5]{1,0:T(8,128)} %stack.40.bounds, bf16[400,32,128]{2,1,0:T(8,128)(2,1)} %get-tuple-element.22.feat_r, ...), custom_call_target="tpu_custom_call" | custom-call | tf_op jit(solution)/shard_map/pallas_call | solution.py:477
  175.1 3.2 %shard_map.195 = (f32[6,8,128]{2,1,0:T(8,128)}, f32[6,8,128]{2,1,0:T(8,128)}) custom-call(s32[8,128]{1,0:T(8,128)} %bitcast.26, s32[8,1]{1,0:T(8,128)} %copy.34.count, s32[8,1]{1,0:T(8,128)} %copy.35.side, f32[2,2,64,128]{3,2,1,0:T(8,128)} %get-tuple-element.46.offsets, f32[2,2,64,128]{3,2,1,0:T(8,128)} %get-tuple-element.45.velocity, ...), custom_call_target="tpu_custom_call" | custom-call | tf_op jit(solution)/shard_map/pallas_call | solution.py:477
  178.3 3.8 %collective-permute-start.9 = (f32[6,8,128]{2,1,0:T(8,128)}, f32[6,8,128]{2,1,0:T(8,128)S(1)}, u32[]{:S(2)}, u32[]{:S(2)}) collective-permute-start(f32[6,8,128]{2,1,0:T(8,128)} %get-tuple-element.35), channel_id=1, source_target_pairs={{4,0},{8,4},{12,8},{16,12},{20,16},{24,20},{28,24},{5,1},{9,5},{13... | collective-permute-start | bytes 73736 | tf_op jit(solution)/shard_map/ppermute | solution.py:490
  182.1 1.9 %collective-permute-start.8 = (f32[6,8,128]{2,1,0:T(8,128)}, f32[6,8,128]{2,1,0:T(8,128)S(1)}, u32[]{:S(2)}, u32[]{:S(2)}) collective-permute-start(f32[6,8,128]{2,1,0:T(8,128)} %get-tuple-element.34), channel_id=1, source_target_pairs={{0,4},{4,8},{8,12},{12,16},{16,20},{20,24},{24,28},{1,5},{5,9},{9,... | collective-permute-start | bytes 73736 | tf_op jit(solution)/shard_map/ppermute | solution.py:490
  184.7 3.7 %collective-permute-done.8 = f32[6,8,128]{2,1,0:T(8,128)S(1)} collective-permute-done((f32[6,8,128]{2,1,0:T(8,128)}, f32[6,8,128]{2,1,0:T(8,128)S(1)}, u32[]{:S(2)}, u32[]{:S(2)}) %collective-permute-start.8) | collective-permute-done | bytes 24608 | tf_op jit(solution)/shard_map/ppermute | solution.py:490
  (54 shorter events, 4.7 us)
Async XLA Ops:
  2.4 4.1 %collective-permute-start.1 = (f32[6,2,8,128]{3,2,1,0:T(8,128)S(1)}, f32[6,2,8,128]{3,2,1,0:T(8,128)S(1)}, u32[]{:S(2)}, u32[]{:S(2)}) collective-permute-start(f32[6,2,8,128]{3,2,1,0:T(8,128)S(1)} %get-tuple-element.56), channel_id=1, source_target_pairs={{1,0},{2,1},{3,2},{5,4},{6,5},{7,6},{9,8},{10,9},{11,10},{13,12},{... | collective-permute-start | bytes 147464 | tf_op jit(solution)/shard_map/ppermute | solution.py:490
  4.7 6.0 %collective-permute-start = (f32[6,2,8,128]{3,2,1,0:T(8,128)S(1)}, f32[6,2,8,128]{3,2,1,0:T(8,128)S(1)}, u32[]{:S(2)}, u32[]{:S(2)}) collective-permute-start(f32[6,2,8,128]{3,2,1,0:T(8,128)S(1)} %get-tuple-element.55), channel_id=1, source_target_pairs={{0,1},{1,2},{2,3},{4,5},{5,6},{6,7},{8,9},{9,10},{10,11},{12,13},{... | collective-permute-start | bytes 147464 | tf_op jit(solution)/shard_map/ppermute | solution.py:490
  11.8 16.9 %copy-start = (f32[6,2,80,128]{3,2,1,0:T(8,128)}, f32[6,2,80,128]{3,2,1,0:T(8,128)S(1)}, u32[]{:S(2)}) copy-start(f32[6,2,80,128]{3,2,1,0:T(8,128)S(1)} %pad_maximum_fusion.own) | copy-start | bytes 1474564
  11.8 11.4 %collective-permute-start.2 = (f32[6,2,80,128]{3,2,1,0:T(8,128)S(1)}, f32[6,2,80,128]{3,2,1,0:T(8,128)S(1)}, u32[]{:S(2)}, u32[]{:S(2)}) collective-permute-start(f32[6,2,80,128]{3,2,1,0:T(8,128)S(1)} %pad_maximum_fusion.own), channel_id=1, source_target_pairs={{0,4},{4,8},{8,12},{12,16},{16,20},{20,24},{24,28},{28,0},{1,5},{5... | collective-permute-start | bytes 1474568 | tf_op jit(solution)/shard_map/ppermute | solution.py:495
  12.8 13.6 %collective-permute-start.3 = (f32[5,1,80,128]{3,2,1,0:T(8,128)S(1)}, f32[5,1,80,128]{3,2,1,0:T(8,128)S(1)}, u32[]{:S(2)}, u32[]{:S(2)}) collective-permute-start(f32[5,1,80,128]{3,2,1,0:T(8,128)S(1)} %slice.42), channel_id=1, source_target_pairs={{0,28},{4,0},{8,4},{12,8},{16,12},{20,16},{24,20},{28,24},{1,29},{... | collective-permute-start | bytes 614408 | tf_op jit(solution)/shard_map/ppermute | solution.py:495
  23.2 5.5 %copy-start.1 = (f32[6,2,80,128]{3,2,1,0:T(8,128)}, f32[6,2,80,128]{3,2,1,0:T(8,128)S(1)}, u32[]{:S(2)}) copy-start(f32[6,2,80,128]{3,2,1,0:T(8,128)S(1)} %collective-permute-done.2.left) | copy-start | bytes 1474564
  26.4 2.3 %copy-start.3 = (f32[5,1,80,128]{3,2,1,0:T(8,128)}, f32[5,1,80,128]{3,2,1,0:T(8,128)S(1)}, u32[]{:S(2)}) copy-start(f32[5,1,80,128]{3,2,1,0:T(8,128)S(1)} %collective-permute-done.3.right) | copy-start | bytes 614404
  66.1 5.4 %collective-permute-start.4 = (f32[3,80,128]{2,1,0:T(8,128)}, f32[3,80,128]{2,1,0:T(8,128)S(1)}, u32[]{:S(2)}, u32[]{:S(2)}) collective-permute-start(f32[3,80,128]{2,1,0:T(8,128)} %get-tuple-element.24), channel_id=1, source_target_pairs={{0,4},{4,8},{8,12},{12,16},{16,20},{20,24},{24,28},{28,0},{1,5},{5... | collective-permute-start | bytes 368648 | tf_op jit(solution)/shard_map/ppermute | solution.py:495
  71.5 0.8 copy-start.2
  96.6 3.3 %collective-permute-start.5 = (f32[4,80,128]{2,1,0:T(8,128)}, f32[4,80,128]{2,1,0:T(8,128)S(1)}, u32[]{:S(2)}, u32[]{:S(2)}) collective-permute-start(f32[4,80,128]{2,1,0:T(8,128)} %get-tuple-element.27), channel_id=1, source_target_pairs={{0,28},{4,0},{8,4},{12,8},{16,12},{20,16},{24,20},{28,24},{1,29},{... | collective-permute-start | bytes 491528 | tf_op jit(solution)/shard_map/ppermute | solution.py:495
  100.0 0.7 copy-start.4
  118.3 23.7 %copy-start.5 = (f32[2,64,128]{2,1,0:T(8,128)S(1)}, f32[2,64,128]{2,1,0:T(8,128)}, u32[]{:S(2)}) copy-start(f32[2,64,128]{2,1,0:T(8,128)} %param.17) | copy-start | bytes 196612
  118.3 23.7 %copy-start.9 = (s32[2,64]{1,0:T(2,128)S(1)}, s32[2,64]{1,0:T(2,128)}, u32[]{:S(2)}) copy-start(s32[2,64]{1,0:T(2,128)} %param.19) | copy-start | bytes 1540
  118.3 24.4 %copy-start.10 = (s32[8,1]{0,1:T(1,128)S(1)}, s32[8,1]{0,1:T(1,128)}, u32[]{:S(2)}) copy-start(s32[8,1]{0,1:T(1,128)} %param.21) | copy-start | bytes 100
  118.3 25.0 %copy-start.11 = (s32[8,1]{0,1:T(1,128)S(1)}, s32[8,1]{0,1:T(1,128)}, u32[]{:S(2)}) copy-start(s32[8,1]{0,1:T(1,128)} %param.22) | copy-start | bytes 100
  118.3 5.5 %collective-permute-start.6 = (f32[2,80,128]{2,1,0:T(8,128)}, f32[2,80,128]{2,1,0:T(8,128)S(1)}, u32[]{:S(2)}, u32[]{:S(2)}) collective-permute-start(f32[2,80,128]{2,1,0:T(8,128)} %shard_map.192.p2), channel_id=1, source_target_pairs={{0,4},{4,8},{8,12},{12,16},{16,20},{20,24},{24,28},{28,0},{1,5},{5... | collective-permute-start | bytes 245768 | tf_op jit(solution)/shard_map/ppermute | solution.py:495
  123.8 0.6 copy-start.7
  141.9 2.4 %collective-permute-start.7 = (f32[2,80,128]{2,1,0:T(8,128)}, f32[2,80,128]{2,1,0:T(8,128)S(1)}, u32[]{:S(2)}, u32[]{:S(2)}) collective-permute-start(f32[2,80,128]{2,1,0:T(8,128)} %shard_map.193.p3), channel_id=1, source_target_pairs={{0,28},{4,0},{8,4},{12,8},{16,12},{20,16},{24,20},{28,24},{1,29},{... | collective-permute-start | bytes 245768 | tf_op jit(solution)/shard_map/ppermute | solution.py:495
  144.0 40.1 %copy-start.8 = (f32[2,80,128]{2,1,0:T(8,128)S(1)}, f32[2,80,128]{2,1,0:T(8,128)}, u32[]{:S(2)}) copy-start(f32[2,80,128]{2,1,0:T(8,128)} %get-tuple-element.21) | copy-start | bytes 245764
  144.3 0.6 copy-start.6
  178.3 6.4 %collective-permute-start.9 = (f32[6,8,128]{2,1,0:T(8,128)}, f32[6,8,128]{2,1,0:T(8,128)S(1)}, u32[]{:S(2)}, u32[]{:S(2)}) collective-permute-start(f32[6,8,128]{2,1,0:T(8,128)} %get-tuple-element.35), channel_id=1, source_target_pairs={{4,0},{8,4},{12,8},{16,12},{20,16},{24,20},{28,24},{5,1},{9,5},{13... | collective-permute-start | bytes 73736 | tf_op jit(solution)/shard_map/ppermute | solution.py:490
  182.1 6.3 %collective-permute-start.8 = (f32[6,8,128]{2,1,0:T(8,128)}, f32[6,8,128]{2,1,0:T(8,128)S(1)}, u32[]{:S(2)}, u32[]{:S(2)}) collective-permute-start(f32[6,8,128]{2,1,0:T(8,128)} %get-tuple-element.34), channel_id=1, source_target_pairs={{0,4},{4,8},{8,12},{12,16},{16,20},{20,24},{24,28},{1,5},{5,9},{9,... | collective-permute-start | bytes 73736 | tf_op jit(solution)/shard_map/ppermute | solution.py:490

commit v5 on v4

--- a/solution.py
+++ b/solution.py
@@ -123,16 +123,23 @@
     dest[pl.ds(cell, 8)] = stage[...].reshape(8, count, 128).astype(BF16)
 
 
-def upright(rows, slots):
-    return rows.astype(F32).T[:slots].astype(BF16)
-
-
-def sources_of(feat, cell, depth, chunk, table=None, first=0):
+def upright(rows):
+    rows = [r.astype(F32) for r in rows]
+    spare = 128 - sum(r.shape[0] for r in rows)
+    if spare:
+        rows.append(jnp.zeros((spare, 128), F32))
+    return jnp.concatenate(rows, axis=0).T.astype(BF16)
+
+
+def sources_of(feat, cell, depth, chunk, offset, table=None, first=0):
     parts = []
+    count = feat.shape[1]
     for n in chunk:
         part = feat[cell + (n // 3) * depth + n % 3 - 1]
         parts.append(part if table is None else part * table[first + n])
-    return jnp.concatenate(parts, axis=1) if len(parts) > 1 else parts[0]
+    part = jnp.concatenate(parts, axis=1) if len(parts) > 1 else parts[0]
+    blank = lambda rows: [jnp.zeros((rows, part.shape[1]), BF16)] if rows else []
+    return jnp.concatenate(blank(offset) + [part] + blank(128 - offset - count), axis=0)
 
 
 def product(left, right):
@@ -140,10 +147,17 @@
 
 
 def fold(total):
-    return jnp.sum(total.T, axis=0, keepdims=True)
-
-
-def each_target(level, order, bounds, target):
+    slots = total.shape[0]
+    parts = jnp.concatenate([v.astype(BF16) for v in split3(total)], axis=1)
+    spread = product(parts, jnp.ones((3 * 128, 128), BF16))
+    here = lax.broadcasted_iota(jnp.int32, (slots, 128), 0) == lax.broadcasted_iota(
+        jnp.int32, (slots, 128), 1
+    )
+    return jnp.sum(jnp.where(here, spread, 0.0), axis=0, keepdims=True)
+
+
+def each_target(level, order, bounds, each, features, target):
+    share = 128 // each
     for index, (slots, cells) in enumerate(CLASSES):
         start = bounds[level, index]
         steps = (bounds[level, index + 1] - start + cells - 1) // cells
@@ -151,7 +165,11 @@
         def step(i, carry, slots=slots, cells=cells, start=start):
             waiting = []
             for u in range(cells):
-                issue, consume, finish = target(order[level, start + i * cells + u], slots)
+                if u % share == 0:
+                    group = [order[level, start + i * cells + v] for v in range(u, min(u + share, cells))]
+                    turned = upright([r for cell in group for r in features(cell)])[:slots]
+                offset = (u % share) * each
+                issue, consume, finish = target(group[u % share], slots, turned, offset)
                 for chunk in CHUNKS:
                     waiting.append((consume, chunk, issue(chunk), finish))
                     if len(waiting) > AHEAD:
@@ -203,15 +221,17 @@
     wide_m[2 * depth : 3 * depth] = own[4, 1]
     wide_m[3 * depth : 4 * depth] = right[4, 0]
 
-    def target(cell, slots):
+    def features(cell):
+        return [out_l[cell + depth], vel_l[cell]]
+
+    def target(cell, slots, turned, offset):
         sign = 9 * (cell >= depth).astype(jnp.int32)
-        pos_l, vel_l_t = upright(out_l[cell + depth], slots), upright(vel_l[cell], slots)
         sums = [jnp.zeros((slots, 128), F32)] * 2
 
         def issue(chunk):
             return (
-                product(pos_l, sources_of(out_r, cell + depth, depth, chunk, posc, sign)),
-                product(vel_l_t, sources_of(vel_r, cell, depth, chunk, velc)),
+                product(turned, sources_of(out_r, cell + depth, depth, chunk, offset, posc, sign)),
+                product(turned, sources_of(vel_r, cell, depth, chunk, offset + KP, velc)),
             )
 
         def consume(chunk, products):
@@ -224,11 +244,11 @@
 
         def finish():
             for i in range(2):
-                acc[i, pl.ds(cell, 1), 0:slots] = fold(sums[i])
+                acc[i, pl.ds(cell, 1), :] = fold(sums[i])
 
         return issue, consume, finish
 
-    each_target(level, order, bounds, target)
+    each_target(level, order, bounds, KP + KD, features, target)
     density = acc[0].reshape(2, depth, 128)
     div = -6.0 * acc[1].reshape(2, depth, 128)
     mass = own[4]
@@ -251,14 +271,16 @@
 
 
 def jacobi_sums(level, order, bounds, first_col, feat_r, feat_l, posc, wide_u, acc, depth):
-    def target(cell, slots):
+    def features(cell):
+        return [feat_l[cell + first_col * depth]]
+
+    def target(cell, slots, turned, offset):
         sign = 9 * (cell >= depth).astype(jnp.int32)
         at = cell + first_col * depth
-        pos_l = upright(feat_l[at], slots)
         sums = [jnp.zeros((slots, 128), F32)]
 
         def issue(chunk):
-            return product(pos_l, sources_of(feat_r, at, depth, chunk, posc, sign))
+            return product(turned, sources_of(feat_r, at, depth, chunk, offset, posc, sign))
 
         def consume(chunk, products):
             for i, n in enumerate(chunk):
@@ -267,12 +289,12 @@
                 sums[0] = sums[0] + s * s * lifted
 
         def finish():
-            acc[pl.ds(cell, 1), 0:slots] = fold(sums[0])
+            acc[pl.ds(cell, 1), :] = fold(sums[0])
 
         return issue, consume, finish
 
     acc[...] = jnp.zeros_like(acc)
-    each_target(level, order, bounds, target)
+    each_target(level, order, bounds, KP, features, target)
     return acc[...].reshape(2, depth, 128)
 
 
@@ -290,13 +312,15 @@
         wide_u[rows] = weight * (start_l if col < 2 else start_o)[col % 2]
     acc[...] = jnp.zeros_like(acc)
 
-    def target(cell, slots):
+    def features(cell):
+        return [feat_l[cell]]
+
+    def target(cell, slots, turned, offset):
         sign = 9 * (cell >= depth).astype(jnp.int32)
-        pos_l = upright(feat_l[cell], slots)
         sums = [jnp.zeros((slots, 128), F32)] * 2
 
         def issue(chunk):
-            return product(pos_l, sources_of(feat_r, cell, depth, chunk, posc, sign))
+            return product(turned, sources_of(feat_r, cell, depth, chunk, offset, posc, sign))
 
         def consume(chunk, products):
             for i, n in enumerate(chunk):
@@ -308,11 +332,11 @@
 
         def finish():
             for i in range(2):
-                acc[i, pl.ds(cell, 1), 0:slots] = fold(sums[i])
+                acc[i, pl.ds(cell, 1), :] = fold(sums[i])
 
         return issue, consume, finish
 
-    each_target(level, order, bounds, target)
+    each_target(level, order, bounds, KP, features, target)
     diagonal = COMPRESSION + 6.0 * acc[0].reshape(2, depth, 128)
     pulled = acc[1].reshape(2, depth, 128)
     out_diag[...] = diagonal
@@ -380,15 +404,17 @@
 
     lax.fori_loop(0, depth // 8, prepare, 0)
 
-    def target(cell, slots):
+    def features(cell):
+        return [feat_l[cell + depth], pres_l[cell]]
+
+    def target(cell, slots, turned, offset):
         sign = 9 * (cell >= depth).astype(jnp.int32)
-        pos_l, pres_l_t = upright(feat_l[cell + depth], slots), upright(pres_l[cell], slots)
         sums = [jnp.zeros((slots, 128), F32)] * 3
 
         def issue(chunk):
             return (
-                product(pos_l, sources_of(feat_r, cell + depth, depth, chunk, posc, sign)),
-                product(pres_l_t, sources_of(pres_r, cell, depth, chunk)),
+                product(turned, sources_of(feat_r, cell + depth, depth, chunk, offset, posc, sign)),
+                product(turned, sources_of(pres_r, cell, depth, chunk, offset + KP)),
             )
 
         def consume(chunk, products):
@@ -403,12 +429,12 @@
 
         def finish():
             for i in range(3):
-                acc[i, pl.ds(cell, 1), 0:slots] = fold(sums[i])
+                acc[i, pl.ds(cell, 1), :] = fold(sums[i])
 
         return issue, consume, finish
 
     acc[...] = jnp.zeros_like(acc)
-    each_target(level, order, bounds, target)
+    each_target(level, order, bounds, KP + KE, features, target)
     sums = acc[...].reshape(3, 2, depth, 128)
     inner = slice(HALO, depth - HALO)
     alive = own[4, :, inner] > 0.0

time: 191 us -> 283 us (1.48)
  Pallas kernels: 130 us -> 221 us
  starting transfers between devices: 13 us -> 16.5 us
    pallas_call x6, Pallas kernels: 130 us -> 221 us  [local_call(): pl.pallas_call(kernel, out_shape=[jax.ShapeDtypeStruct(shape, dtype) for...]
  transfers between devices with their start and end apart: 10 -> 10, of which waited for: 8 -> 8; matrix products, arithmetic and copies ran while one was open for 4% -> 2% of each run, Pallas kernels for 0% -> 0%
where the time goes in v5:
time: 283 us; the launch traced here: 284 us
  Pallas kernels  221 us (78%)
  waiting for transfers between devices  30 us (11%)
  starting transfers between devices  16.5 us (6%)
  local copies, waits for them, and re-layouts  8.61 us (3%)
  other arithmetic  6.61 us (2%)
    pallas_call x6, Pallas kernels, local_call(): pl.pallas_call(kernel, out_shape=[jax.ShapeDtypeStruct(shape, dtype) for...  221 us
    ppermute x6, waiting for transfers between devices, around(): lax.ppermute(block, axis, [(i, (i + distance) % peers) for i in range(pee...  21.7 us
    ppermute x4, starting transfers between devices, from_behind(): return lax.ppermute(block, axis, route)  11 us
    ppermute x4, waiting for transfers between devices, from_behind(): return lax.ppermute(block, axis, route)  8.34 us
  transfers between devices with their start and end apart: 10, of which 8 were waited for; matrix products, arithmetic and copies ran while one was open for 2% of the time, Pallas kernels for 0%

profile of v5, /device:TPU:28, one launch (start us, length us, event | category | flops | bytes accessed | tf_op | source)
XLA Modules:
  0.0 283.8 jit_solution(17896081529104076491)
XLA Ops:
  0.6 0.9 fusion.6
  1.6 0.8 pad_maximum_fusion.4
  2.4 2.4 collective-permute-start.1
  4.7 1.3 collective-permute-start
  6.5 4.3 %collective-permute-done = f32[6,2,8,128]{3,2,1,0:T(8,128)S(1)} collective-permute-done((f32[6,2,8,128]{3,2,1,0:T(8,128)S(1)}, f32[6,2,8,128]{3,2,1,0:T(8,128)S(1)}, u32[]{:S(2)}, u32[]{:S(2)}) %collective-permute-start) | collective-permute-done | bytes 49184 | tf_op jit(solution)/shard_map/ppermute | solution.py:516
  10.7 1.0 pad_maximum_fusion.own
  11.9 0.9 select_convert_fusion
  12.8 2.6 collective-permute-start.3
  15.3 7.8 %collective-permute-done.2.left = f32[6,2,80,128]{3,2,1,0:T(8,128)S(1)} collective-permute-done((f32[6,2,80,128]{3,2,1,0:T(8,128)S(1)}, f32[6,2,80,128]{3,2,1,0:T(8,128)S(1)}, u32[]{:S(2)}, u32[]{:S(2)}) %collective-permute-start.2) | collective-permute-done | bytes 491552 | tf_op jit(solution)/shard_map/ppermute | solution.py:521
  25.1 0.7 stack.40.bounds
  25.7 0.7 fusion.1.order
  26.4 0.8 broadcast_in_dim.113.posc
  27.2 1.5 broadcast_in_dim.114.velc
  28.7 55.6 %shard_map.190 = (bf16[400,32,128]{2,1,0:T(8,128)(2,1)}, bf16[240,32,128]{2,1,0:T(8,128)(2,1)}, f32[2,80,128]{2,1,0:T(8,128)}, f32[2,80,128]{2,1,0:T(8,128)}, f3...) custom-call(s32[5,176]{1,0:T(8,128)} %fusion.1.order, s32[5,5]{1,0:T(8,128)} %stack.40.bounds, f32[6,2,80,128]{3,2,1,0:T(8,128)} %copy-done.1, ...), custom_call_target="tpu_custom_call" | custom-call | tf_op jit(solution)/shard_map/pallas_call | solution.py:503
  84.3 5.4 %collective-permute-done.4.recv.recv1 = f32[3,80,128]{2,1,0:T(8,128)S(1)} collective-permute-done((f32[3,80,128]{2,1,0:T(8,128)}, f32[3,80,128]{2,1,0:T(8,128)S(1)}, u32[]{:S(2)}, u32[]{:S(2)}) %collective-permute-start.4) | collective-permute-done | bytes 122912 | tf_op jit(solution)/shard_map/ppermute | solution.py:521
  89.7 0.8 broadcast_in_dim.115.posc
  90.5 41.9 %shard_map.191 = (f32[2,80,128]{2,1,0:T(8,128)}, f32[2,80,128]{2,1,0:T(8,128)}, f32[4,80,128]{2,1,0:T(8,128)}) custom-call(s32[5,176]{1,0:T(8,128)} %fusion.1.order, s32[5,5]{1,0:T(8,128)} %stack.40.bounds, bf16[400,32,128]{2,1,0:T(8,128)(2,1)} %get-tuple-element.22.feat_r, bf16[240,32,128]{2,1,0:T(8,128)(2,1)} %get-tuple-element.23.feat_l, ...), custom_call_target="tpu_custom_call" | custom-call | tf_op jit(solution)/shard_map/pallas_call | solution.py:503
  132.5 1.6 collective-permute-start.5
  134.1 3.2 %collective-permute-done.5.recv2 = f32[4,80,128]{2,1,0:T(8,128)S(1)} collective-permute-done((f32[4,80,128]{2,1,0:T(8,128)}, f32[4,80,128]{2,1,0:T(8,128)S(1)}, u32[]{:S(2)}, u32[]{:S(2)}) %collective-permute-start.5) | collective-permute-done | bytes 163872 | tf_op jit(solution)/shard_map/ppermute | solution.py:521
  137.2 0.7 copy-done.4
  137.9 37.8 %shard_map.192.p2 = f32[2,80,128]{2,1,0:T(8,128)} custom-call(s32[5,176]{1,0:T(8,128)} %fusion.1.order, s32[5,5]{1,0:T(8,128)} %stack.40.bounds, bf16[400,32,128]{2,1,0:T(8,128)(2,1)} %get-tuple-element.22.feat_r, bf16[240,32,128]{2,1,0:T(8,128)(2,1)} %get-tuple-element.23.feat_l, f32[6,2,80,128]{3,2,1,0:T(8,128)} %copy-done, f32[3,80,128]{2,1,0:T(8,128)} %copy-done.2, ...), custom_call_target="tpu_custom_call" | custom-call | tf_op jit(solution)/shard_map/pallas_call | solution.py:503
  175.8 5.0 %collective-permute-done.6.recv3 = f32[2,80,128]{2,1,0:T(8,128)S(1)} collective-permute-done((f32[2,80,128]{2,1,0:T(8,128)}, f32[2,80,128]{2,1,0:T(8,128)S(1)}, u32[]{:S(2)}, u32[]{:S(2)}) %collective-permute-start.6) | collective-permute-done | bytes 81952 | tf_op jit(solution)/shard_map/ppermute | solution.py:521
  181.4 34.8 %shard_map.193.p3 = f32[2,80,128]{2,1,0:T(8,128)} custom-call(s32[5,176]{1,0:T(8,128)} %fusion.1.order, s32[5,5]{1,0:T(8,128)} %stack.40.bounds, bf16[400,32,128]{2,1,0:T(8,128)(2,1)} %get-tuple-element.22.feat_r, bf16[240,32,128]{2,1,0:T(8,128)(2,1)} %get-tuple-element.23.feat_l, f32[6,2,80,128]{3,2,1,0:T(8,128)} %copy-done.1, f32[6,2,80,128]{3,2,1,0:T(8,128)} %copy-done, ...), custom_call_target="tpu_custom_call" | custom-call | tf_op jit(solution)/shard_map/pallas_call | solution.py:503
  216.3 1.2 collective-permute-start.7
  217.5 0.7 fusion.mass
  218.2 0.7 copy.34.count
  218.9 0.7 copy.35.side
  220.5 47.8 %shard_map.194 = (f32[2,64,128]{2,1,0:T(8,128)}, f32[2,2,64,128]{3,2,1,0:T(8,128)}, f32[2,2,64,128]{3,2,1,0:T(8,128)}, f32[2,2,64,128]{3,2,1,0:T(8,128)}) custom-call(s32[5,176]{1,0:T(8,128)} %fusion.1.order, s32[5,5]{1,0:T(8,128)} %stack.40.bounds, bf16[400,32,128]{2,1,0:T(8,128)(2,1)} %get-tuple-element.22.feat_r, ...), custom_call_target="tpu_custom_call" | custom-call | tf_op jit(solution)/shard_map/pallas_call | solution.py:503
  268.3 3.2 %shard_map.195 = (f32[6,8,128]{2,1,0:T(8,128)}, f32[6,8,128]{2,1,0:T(8,128)}) custom-call(s32[8,128]{1,0:T(8,128)} %bitcast.26, s32[8,1]{1,0:T(8,128)} %copy.34.count, s32[8,1]{1,0:T(8,128)} %copy.35.side, f32[2,2,64,128]{3,2,1,0:T(8,128)} %get-tuple-element.46.offsets, f32[2,2,64,128]{3,2,1,0:T(8,128)} %get-tuple-element.45.velocity, ...), custom_call_target="tpu_custom_call" | custom-call | tf_op jit(solution)/shard_map/pallas_call | solution.py:503
  271.6 5.4 %collective-permute-start.9 = (f32[6,8,128]{2,1,0:T(8,128)}, f32[6,8,128]{2,1,0:T(8,128)S(1)}, u32[]{:S(2)}, u32[]{:S(2)}) collective-permute-start(f32[6,8,128]{2,1,0:T(8,128)} %get-tuple-element.35), channel_id=1, source_target_pairs={{4,0},{8,4},{12,8},{16,12},{20,16},{24,20},{28,24},{5,1},{9,5},{13... | collective-permute-start | bytes 73736 | tf_op jit(solution)/shard_map/ppermute | solution.py:516
  277.0 1.9 collective-permute-start.8
  279.5 3.7 %collective-permute-done.8 = f32[6,8,128]{2,1,0:T(8,128)S(1)} collective-permute-done((f32[6,8,128]{2,1,0:T(8,128)}, f32[6,8,128]{2,1,0:T(8,128)S(1)}, u32[]{:S(2)}, u32[]{:S(2)}) %collective-permute-start.8) | collective-permute-done | bytes 24608 | tf_op jit(solution)/shard_map/ppermute | solution.py:516
  (54 shorter events, 5.3 us)
Async XLA Ops:
  2.4 4.1 %collective-permute-start.1 = (f32[6,2,8,128]{3,2,1,0:T(8,128)S(1)}, f32[6,2,8,128]{3,2,1,0:T(8,128)S(1)}, u32[]{:S(2)}, u32[]{:S(2)}) collective-permute-start(f32[6,2,8,128]{3,2,1,0:T(8,128)S(1)} %get-tuple-element.56), channel_id=1, source_target_pairs={{1,0},{2,1},{3,2},{5,4},{6,5},{7,6},{9,8},{10,9},{11,10},{13,12},{... | collective-permute-start | bytes 147464 | tf_op jit(solution)/shard_map/ppermute | solution.py:516
  4.7 6.0 %collective-permute-start = (f32[6,2,8,128]{3,2,1,0:T(8,128)S(1)}, f32[6,2,8,128]{3,2,1,0:T(8,128)S(1)}, u32[]{:S(2)}, u32[]{:S(2)}) collective-permute-start(f32[6,2,8,128]{3,2,1,0:T(8,128)S(1)} %get-tuple-element.55), channel_id=1, source_target_pairs={{0,1},{1,2},{2,3},{4,5},{5,6},{6,7},{8,9},{9,10},{10,11},{12,13},{... | collective-permute-start | bytes 147464 | tf_op jit(solution)/shard_map/ppermute | solution.py:516
  11.8 16.9 %copy-start = (f32[6,2,80,128]{3,2,1,0:T(8,128)}, f32[6,2,80,128]{3,2,1,0:T(8,128)S(1)}, u32[]{:S(2)}) copy-start(f32[6,2,80,128]{3,2,1,0:T(8,128)S(1)} %pad_maximum_fusion.own) | copy-start | bytes 1474564
  11.8 11.4 %collective-permute-start.2 = (f32[6,2,80,128]{3,2,1,0:T(8,128)S(1)}, f32[6,2,80,128]{3,2,1,0:T(8,128)S(1)}, u32[]{:S(2)}, u32[]{:S(2)}) collective-permute-start(f32[6,2,80,128]{3,2,1,0:T(8,128)S(1)} %pad_maximum_fusion.own), channel_id=1, source_target_pairs={{0,4},{4,8},{8,12},{12,16},{16,20},{20,24},{24,28},{28,0},{1,5},{5... | collective-permute-start | bytes 1474568 | tf_op jit(solution)/shard_map/ppermute | solution.py:521
  12.8 13.6 %collective-permute-start.3 = (f32[5,1,80,128]{3,2,1,0:T(8,128)S(1)}, f32[5,1,80,128]{3,2,1,0:T(8,128)S(1)}, u32[]{:S(2)}, u32[]{:S(2)}) collective-permute-start(f32[5,1,80,128]{3,2,1,0:T(8,128)S(1)} %slice.42), channel_id=1, source_target_pairs={{0,28},{4,0},{8,4},{12,8},{16,12},{20,16},{24,20},{28,24},{1,29},{... | collective-permute-start | bytes 614408 | tf_op jit(solution)/shard_map/ppermute | solution.py:521
  23.2 5.5 %copy-start.1 = (f32[6,2,80,128]{3,2,1,0:T(8,128)}, f32[6,2,80,128]{3,2,1,0:T(8,128)S(1)}, u32[]{:S(2)}) copy-start(f32[6,2,80,128]{3,2,1,0:T(8,128)S(1)} %collective-permute-done.2.left) | copy-start | bytes 1474564
  26.4 2.3 copy-start.3
  84.3 5.4 %collective-permute-start.4 = (f32[3,80,128]{2,1,0:T(8,128)}, f32[3,80,128]{2,1,0:T(8,128)S(1)}, u32[]{:S(2)}, u32[]{:S(2)}) collective-permute-start(f32[3,80,128]{2,1,0:T(8,128)} %get-tuple-element.24), channel_id=1, source_target_pairs={{0,4},{4,8},{8,12},{12,16},{16,20},{20,24},{24,28},{28,0},{1,5},{5... | collective-permute-start | bytes 368648 | tf_op jit(solution)/shard_map/ppermute | solution.py:521
  89.7 0.8 copy-start.2
  132.5 4.8 %collective-permute-start.5 = (f32[4,80,128]{2,1,0:T(8,128)}, f32[4,80,128]{2,1,0:T(8,128)S(1)}, u32[]{:S(2)}, u32[]{:S(2)}) collective-permute-start(f32[4,80,128]{2,1,0:T(8,128)} %get-tuple-element.27), channel_id=1, source_target_pairs={{0,28},{4,0},{8,4},{12,8},{16,12},{20,16},{24,20},{28,24},{1,29},{... | collective-permute-start | bytes 491528 | tf_op jit(solution)/shard_map/ppermute | solution.py:521
  137.2 0.7 copy-start.4
  175.7 41.8 %copy-start.5 = (f32[2,64,128]{2,1,0:T(8,128)S(1)}, f32[2,64,128]{2,1,0:T(8,128)}, u32[]{:S(2)}) copy-start(f32[2,64,128]{2,1,0:T(8,128)} %param.17) | copy-start | bytes 196612
  175.7 41.8 %copy-start.9 = (s32[2,64]{1,0:T(2,128)S(1)}, s32[2,64]{1,0:T(2,128)}, u32[]{:S(2)}) copy-start(s32[2,64]{1,0:T(2,128)} %param.19) | copy-start | bytes 1540
  175.8 42.5 %copy-start.10 = (s32[8,1]{0,1:T(1,128)S(1)}, s32[8,1]{0,1:T(1,128)}, u32[]{:S(2)}) copy-start(s32[8,1]{0,1:T(1,128)} %param.21) | copy-start | bytes 100
  175.8 43.1 %copy-start.11 = (s32[8,1]{0,1:T(1,128)S(1)}, s32[8,1]{0,1:T(1,128)}, u32[]{:S(2)}) copy-start(s32[8,1]{0,1:T(1,128)} %param.22) | copy-start | bytes 100
  175.8 5.0 %collective-permute-start.6 = (f32[2,80,128]{2,1,0:T(8,128)}, f32[2,80,128]{2,1,0:T(8,128)S(1)}, u32[]{:S(2)}, u32[]{:S(2)}) collective-permute-start(f32[2,80,128]{2,1,0:T(8,128)} %shard_map.192.p2), channel_id=1, source_target_pairs={{0,4},{4,8},{8,12},{12,16},{16,20},{20,24},{24,28},{28,0},{1,5},{5... | collective-permute-start | bytes 245768 | tf_op jit(solution)/shard_map/ppermute | solution.py:521
  180.8 0.6 copy-start.7
  216.3 3.6 %collective-permute-start.7 = (f32[2,80,128]{2,1,0:T(8,128)}, f32[2,80,128]{2,1,0:T(8,128)S(1)}, u32[]{:S(2)}, u32[]{:S(2)}) collective-permute-start(f32[2,80,128]{2,1,0:T(8,128)} %shard_map.193.p3), channel_id=1, source_target_pairs={{0,28},{4,0},{8,4},{12,8},{16,12},{20,16},{24,20},{28,24},{1,29},{... | collective-permute-start | bytes 245768 | tf_op jit(solution)/shard_map/ppermute | solution.py:521
  219.6 59.3 %copy-start.8 = (f32[2,80,128]{2,1,0:T(8,128)S(1)}, f32[2,80,128]{2,1,0:T(8,128)}, u32[]{:S(2)}) copy-start(f32[2,80,128]{2,1,0:T(8,128)} %get-tuple-element.21) | copy-start | bytes 245764
  219.9 0.6 copy-start.6
  271.6 8.0 %collective-permute-start.9 = (f32[6,8,128]{2,1,0:T(8,128)}, f32[6,8,128]{2,1,0:T(8,128)S(1)}, u32[]{:S(2)}, u32[]{:S(2)}) collective-permute-start(f32[6,8,128]{2,1,0:T(8,128)} %get-tuple-element.35), channel_id=1, source_target_pairs={{4,0},{8,4},{12,8},{16,12},{20,16},{24,20},{28,24},{5,1},{9,5},{13... | collective-permute-start | bytes 73736 | tf_op jit(solution)/shard_map/ppermute | solution.py:516
  277.0 6.3 %collective-permute-start.8 = (f32[6,8,128]{2,1,0:T(8,128)}, f32[6,8,128]{2,1,0:T(8,128)S(1)}, u32[]{:S(2)}, u32[]{:S(2)}) collective-permute-start(f32[6,8,128]{2,1,0:T(8,128)} %get-tuple-element.34), channel_id=1, source_target_pairs={{0,4},{4,8},{8,12},{12,16},{16,20},{20,24},{24,28},{1,5},{5,9},{9,... | collective-permute-start | bytes 73736 | tf_op jit(solution)/shard_map/ppermute | solution.py:516

commit v6 on v4

--- a/solution.py
+++ b/solution.py
@@ -2,6 +2,7 @@
 
 import jax
 import jax.numpy as jnp
+import ml_dtypes
 import numpy as np
 from jax import lax
 from jax.experimental import pallas as pl
@@ -18,7 +19,7 @@
 HALO = 8
 CLASSES = ((32, 16), (64, 8), (96, 6), (128, 6))
 CHUNKS = ((0, 1), (2, 3), (4, 5), (6, 7), (8,))
-AHEAD = 2
+AHEAD = 5
 KP = 32
 KD = 48
 KE = 16
@@ -100,20 +101,24 @@
     return target, source
 
 
-def sign_table(signs):
-    table = np.asarray([signs(sx, sz) for sx, sz in SHIFTS], np.float32)
-    return jnp.broadcast_to(jnp.asarray(table)[:, :, None], (*table.shape, 128)).astype(BF16)
-
-
-def position_table(cut_first, cut_second):
-    table = np.asarray([position_signs(sx, sz) for sx, sz in SHIFTS] * 2, np.float32)
-    constant = np.arange(KP) == KP - 2
-    sides = np.asarray([sx for sx, _ in SHIFTS] * 2)
-    target = np.repeat([0, 1], 9)
-    spots = lambda t, side: jnp.asarray(((target == t) & (sides == side))[:, None] & constant)
-    table = jnp.where(spots(0, cut_first[1]) & cut_first[0], FAR, jnp.asarray(table))
-    table = jnp.where(spots(1, cut_second[1]) & cut_second[0], FAR, table)
-    return jnp.broadcast_to(table[:, :, None], (18, KP, 128)).astype(BF16)
+def wide_table(table):
+    return np.repeat(np.asarray(table, np.float32)[:, :, None], 128, axis=2).astype(ml_dtypes.bfloat16)
+
+
+def velocity_table():
+    return wide_table([velocity_signs(sx, sz) for sx, sz in SHIFTS])
+
+
+def position_table():
+    tables = []
+    for cuts in ((), ((0, -1),), ((1, 1),), ((0, 1), (1, -1))):
+        for t in range(2):
+            for sx, sz in SHIFTS:
+                signs = position_signs(sx, sz)
+                if (t, sx) in cuts:
+                    signs[KP - 2] = FAR
+                tables.append(signs)
+    return wide_table(tables)
 
 
 def store_rows(rows, stage, dest, cell):
@@ -143,7 +148,7 @@
     return jnp.sum(total.T, axis=0, keepdims=True)
 
 
-def each_target(level, order, bounds, target):
+def each_target(level, order, bounds, stashes, target):
     for index, (slots, cells) in enumerate(CLASSES):
         start = bounds[level, index]
         steps = (bounds[level, index + 1] - start + cells - 1) // cells
@@ -153,27 +158,34 @@
             for u in range(cells):
                 issue, consume, finish = target(order[level, start + i * cells + u], slots)
                 for chunk in CHUNKS:
-                    waiting.append((consume, chunk, issue(chunk), finish))
+                    lanes = slice(128 * chunk[0], 128 * (chunk[-1] + 1))
+                    for stash, value in zip(stashes, issue(chunk)):
+                        stash[u, 0:slots, lanes] = value
+                    waiting.append((u, slots, consume, chunk, finish))
                     if len(waiting) > AHEAD:
-                        take(waiting.pop(0))
+                        take(stashes, *waiting.pop(0))
             for entry in waiting:
-                take(entry)
+                take(stashes, *entry)
             return carry
 
         lax.fori_loop(0, steps, step, 0)
 
 
-def take(entry):
-    consume, chunk, products, finish = entry
-    consume(chunk, products)
+def take(stashes, u, slots, consume, chunk, finish):
+    for n in chunk:
+        consume(n, *[stash[u, 0:slots, 128 * n : 128 * (n + 1)] for stash in stashes])
     if chunk is CHUNKS[-1]:
         finish()
+
+
+def stash_shape(slots):
+    return ((max(cells for _, cells in CLASSES), slots, 9 * 128), F32)
 
 
 def density_kernel(
     level, order, bounds, left, own, right, posc, velc,
     out_r, out_l, out_w, out_density, out_source, out_send,
-    stage_p, stage_d, vel_r, vel_l, wide_m, acc,
+    stage_p, stage_d, vel_r, vel_l, wide_m, acc, stash_a, stash_b,
 ):
     depth = own.shape[2]
     groups = depth // 8
@@ -204,7 +216,7 @@
     wide_m[3 * depth : 4 * depth] = right[4, 0]
 
     def target(cell, slots):
-        sign = 9 * (cell >= depth).astype(jnp.int32)
+        sign = bounds[level, len(CLASSES) + 1] + 9 * (cell >= depth).astype(jnp.int32)
         pos_l, vel_l_t = upright(out_l[cell + depth], slots), upright(vel_l[cell], slots)
         sums = [jnp.zeros((slots, 128), F32)] * 2
 
@@ -214,13 +226,11 @@
                 product(vel_l_t, sources_of(vel_r, cell, depth, chunk, velc)),
             )
 
-        def consume(chunk, products):
-            for i, n in enumerate(chunk):
-                lanes = slice(128 * i, 128 * (i + 1))
-                s = jnp.maximum(products[0][:, lanes], 0.0)
-                q = s * s * wide_m[pl.ds(cell + (n // 3) * depth + n % 3 - 1, 1), :]
-                sums[0] = sums[0] + q * s
-                sums[1] = sums[1] + q * products[1][:, lanes]
+        def consume(n, reach, closing):
+            s = jnp.maximum(reach, 0.0)
+            q = s * s * wide_m[pl.ds(cell + (n // 3) * depth + n % 3 - 1, 1), :]
+            sums[0] = sums[0] + q * s
+            sums[1] = sums[1] + q * closing
 
         def finish():
             for i in range(2):
@@ -228,7 +238,7 @@
 
         return issue, consume, finish
 
-    each_target(level, order, bounds, target)
+    each_target(level, order, bounds, (stash_a, stash_b), target)
     density = acc[0].reshape(2, depth, 128)
     div = -6.0 * acc[1].reshape(2, depth, 128)
     mass = own[4]
@@ -250,21 +260,20 @@
     return jnp.where(alive, updated, 0.0)
 
 
-def jacobi_sums(level, order, bounds, first_col, feat_r, feat_l, posc, wide_u, acc, depth):
+def jacobi_sums(level, order, bounds, first_col, feat_r, feat_l, posc, wide_u, acc, stash, depth):
     def target(cell, slots):
-        sign = 9 * (cell >= depth).astype(jnp.int32)
+        sign = bounds[level, len(CLASSES) + 1] + 9 * (cell >= depth).astype(jnp.int32)
         at = cell + first_col * depth
         pos_l = upright(feat_l[at], slots)
         sums = [jnp.zeros((slots, 128), F32)]
 
         def issue(chunk):
-            return product(pos_l, sources_of(feat_r, at, depth, chunk, posc, sign))
-
-        def consume(chunk, products):
-            for i, n in enumerate(chunk):
-                s = jnp.maximum(products[:, 128 * i : 128 * (i + 1)], 0.0)
-                lifted = wide_u[pl.ds(cell + (n // 3) * depth + n % 3 - 1, 1), :]
-                sums[0] = sums[0] + s * s * lifted
+            return (product(pos_l, sources_of(feat_r, at, depth, chunk, posc, sign)),)
+
+        def consume(n, reach):
+            s = jnp.maximum(reach, 0.0)
+            lifted = wide_u[pl.ds(cell + (n // 3) * depth + n % 3 - 1, 1), :]
+            sums[0] = sums[0] + s * s * lifted
 
         def finish():
             acc[pl.ds(cell, 1), 0:slots] = fold(sums[0])
@@ -272,13 +281,13 @@
         return issue, consume, finish
 
     acc[...] = jnp.zeros_like(acc)
-    each_target(level, order, bounds, target)
+    each_target(level, order, bounds, (stash,), target)
     return acc[...].reshape(2, depth, 128)
 
 
 def sweep1_kernel(
     level, order, bounds, feat_r, feat_l, left, own, recv, weight_own, source_own, posc,
-    out_p, out_diag, out_send, wide_w, wide_u, acc,
+    out_p, out_diag, out_send, wide_w, wide_u, acc, stash,
 ):
     depth = weight_own.shape[1]
     start_l = jnp.where(left[4] > 0.0, left[5], 0.0)
@@ -291,20 +300,19 @@
     acc[...] = jnp.zeros_like(acc)
 
     def target(cell, slots):
-        sign = 9 * (cell >= depth).astype(jnp.int32)
+        sign = bounds[level, len(CLASSES) + 1] + 9 * (cell >= depth).astype(jnp.int32)
         pos_l = upright(feat_l[cell], slots)
         sums = [jnp.zeros((slots, 128), F32)] * 2
 
         def issue(chunk):
-            return product(pos_l, sources_of(feat_r, cell, depth, chunk, posc, sign))
-
-        def consume(chunk, products):
-            for i, n in enumerate(chunk):
-                s = jnp.maximum(products[:, 128 * i : 128 * (i + 1)], 0.0)
-                q = s * s
-                at = pl.ds(cell + (n // 3) * depth + n % 3 - 1, 1)
-                sums[0] = sums[0] + q * wide_w[at, :]
-                sums[1] = sums[1] + q * wide_u[at, :]
+            return (product(pos_l, sources_of(feat_r, cell, depth, chunk, posc, sign)),)
+
+        def consume(n, reach):
+            s = jnp.maximum(reach, 0.0)
+            q = s * s
+            at = pl.ds(cell + (n // 3) * depth + n % 3 - 1, 1)
+            sums[0] = sums[0] + q * wide_w[at, :]
+            sums[1] = sums[1] + q * wide_u[at, :]
 
         def finish():
             for i in range(2):
@@ -312,7 +320,7 @@
 
         return issue, consume, finish
 
-    each_target(level, order, bounds, target)
+    each_target(level, order, bounds, (stash,), target)
     diagonal = COMPRESSION + 6.0 * acc[0].reshape(2, depth, 128)
     pulled = acc[1].reshape(2, depth, 128)
     out_diag[...] = diagonal
@@ -328,26 +336,26 @@
 
 def sweep2_kernel(
     level, order, bounds, feat_r, feat_l, own, recv1, recv2, weight_own, source_own, diag, p1, posc,
-    out_p, wide_u, acc,
+    out_p, wide_u, acc, stash,
 ):
     depth = weight_own.shape[1]
     wide_u[0:depth] = recv1[1] * p1[0]
     wide_u[depth : 2 * depth] = weight_own[0] * p1[1]
     wide_u[2 * depth : 3 * depth] = weight_own[1] * recv2[0]
     wide_u[3 * depth : 4 * depth] = recv2[2] * recv2[1]
-    pulled = jacobi_sums(level, order, bounds, 1, feat_r, feat_l, posc, wide_u, acc, depth)
+    pulled = jacobi_sums(level, order, bounds, 1, feat_r, feat_l, posc, wide_u, acc, stash, depth)
     out_p[0] = column_update(own[4, 0] > 0.0, p1[1], source_own[0], pulled[0], diag[1])
     out_p[1] = column_update(own[4, 1] > 0.0, recv2[0], source_own[1], pulled[1], recv2[3])
 
 
 def sweep3_kernel(
     level, order, bounds, feat_r, feat_l, left, own, recv1, recv3, weight_own, source_own, diag, p2, posc,
-    out_p, wide_u, acc,
+    out_p, wide_u, acc, stash,
 ):
     depth = weight_own.shape[1]
     wide_u[0 : 2 * depth] = (recv1[0:2] * recv3[...]).reshape(2 * depth, 128)
     wide_u[2 * depth : 4 * depth] = (weight_own[...] * p2[...]).reshape(2 * depth, 128)
-    pulled = jacobi_sums(level, order, bounds, 0, feat_r, feat_l, posc, wide_u, acc, depth)
+    pulled = jacobi_sums(level, order, bounds, 0, feat_r, feat_l, posc, wide_u, acc, stash, depth)
     out_p[0] = column_update(left[4, 1] > 0.0, recv3[1], recv1[2], pulled[0], diag[0])
     out_p[1] = column_update(own[4, 0] > 0.0, p2[0], source_own[0], pulled[1], diag[1])
 
@@ -355,7 +363,7 @@
 def force_kernel(
     level, order, bounds, feat_r, feat_l, own, recv1, recv2, recv4, left, right, weight_own, p3, posc,
     out_pressure, out_acc, out_velocity, out_offsets,
-    wide_p, wide_w, wide_x, wide_z, pres_r, pres_l, stage, acc,
+    wide_p, wide_w, wide_x, wide_z, pres_r, pres_l, stage, acc, stash_a, stash_b,
 ):
     depth = weight_own.shape[1]
     wide_p[0:2] = p3[...]
@@ -381,7 +389,7 @@
     lax.fori_loop(0, depth // 8, prepare, 0)
 
     def target(cell, slots):
-        sign = 9 * (cell >= depth).astype(jnp.int32)
+        sign = bounds[level, len(CLASSES) + 1] + 9 * (cell >= depth).astype(jnp.int32)
         pos_l, pres_l_t = upright(feat_l[cell + depth], slots), upright(pres_l[cell], slots)
         sums = [jnp.zeros((slots, 128), F32)] * 3
 
@@ -391,15 +399,13 @@
                 product(pres_l_t, sources_of(pres_r, cell, depth, chunk)),
             )
 
-        def consume(chunk, products):
-            for i, n in enumerate(chunk):
-                lanes = slice(128 * i, 128 * (i + 1))
-                s = jnp.maximum(products[0][:, lanes], 0.0)
-                g = s * s * products[1][:, lanes]
-                at = pl.ds(cell + (n // 3) * depth + n % 3 - 1, 1)
-                sums[0] = sums[0] + g
-                sums[1] = sums[1] + g * (wide_x[at, :] + float(n // 3 - 1))
-                sums[2] = sums[2] + g * (wide_z[at, :] + float(n % 3 - 1))
+        def consume(n, reach, lift):
+            s = jnp.maximum(reach, 0.0)
+            g = s * s * lift
+            at = pl.ds(cell + (n // 3) * depth + n % 3 - 1, 1)
+            sums[0] = sums[0] + g
+            sums[1] = sums[1] + g * (wide_x[at, :] + float(n // 3 - 1))
+            sums[2] = sums[2] + g * (wide_z[at, :] + float(n % 3 - 1))
 
         def finish():
             for i in range(3):
@@ -408,7 +414,7 @@
         return issue, consume, finish
 
     acc[...] = jnp.zeros_like(acc)
-    each_target(level, order, bounds, target)
+    each_target(level, order, bounds, (stash_a, stash_b), target)
     sums = acc[...].reshape(3, 2, depth, 128)
     inner = slice(HALO, depth - HALO)
     alive = own[4, :, inner] > 0.0
@@ -451,7 +457,7 @@
         out_down[index] = jnp.where(up, 0.0, block)
 
 
-def target_lists(count, cells):
+def target_lists(count, cells, tables):
     depth = count.shape[1]
     number = jnp.arange(2 * depth, dtype=jnp.int32)
     kinds = []
@@ -465,10 +471,12 @@
     kinds = jnp.stack(kinds)
     key = kinds * (2 * depth) + number
     rank = jnp.sum((key[:, None, :] < key[:, :, None]).astype(jnp.int32), 2)
-    bounds = jnp.stack([jnp.sum((kinds < c).astype(jnp.int32), 1) for c in range(len(CLASSES) + 1)], 1)
+    steps = jnp.arange(len(CLASSES) + 1, dtype=jnp.int32)
+    bounds = jnp.sum((kinds[:, None, :] < steps[None, :, None]).astype(jnp.int32), 2)
     place = jnp.arange(2 * depth + max(c for _, c in CLASSES), dtype=jnp.int32)
     order = jnp.sum(jnp.where(rank[:, None, :] == place[None, :, None], number, 0), 2)
-    return jnp.where(place < bounds[:, -1:], order, HALO), bounds
+    order = jnp.where(place < bounds[:, -1:], order, HALO)
+    return order, jnp.concatenate([bounds, tables[np.arange(ITERS + 2) % 2][:, None]], 1)
 
 
 def local_call(kernel, out_shapes, scratch, scalars, *operands):
@@ -510,13 +518,13 @@
     depth = cells + 2 * HALO
     first = lax.axis_index("col") == 0
     last = lax.axis_index("col") == lax.axis_size("col") - 1
-    here = position_table((first, -1), (last, 1))
-    back = position_table((first, 1), (first, -1))
-    velc = sign_table(velocity_signs)
+    here = jnp.where(first, 1, jnp.where(last, 2, 0))
+    back = jnp.where(first, 3, 0)
+    posc, velc = position_table(), velocity_table()
     plane = (2, depth, slots)
 
     live = jnp.stack([left[4, 1], own[4, 0], own[4, 1]]) > 0.0
-    lists = target_lists(jnp.sum(live.astype(jnp.int32), -1), cells)
+    lists = target_lists(jnp.sum(live.astype(jnp.int32), -1), cells, 18 * jnp.stack([here, back]))
     long = (4 * depth, slots)
     sums = (2 * depth, slots)
 
@@ -537,29 +545,31 @@
             ((2 * depth, KD, slots), BF16),
             (long, F32),
             ((2, *sums), F32),
+            stash_shape(slots),
+            stash_shape(slots),
         ],
-        lists, left, own, right, here, velc,
+        lists, left, own, right, posc, velc,
     )
     recv1 = around(send1, "col", 1)
     p1, diag, send2 = local_call(
         functools.partial(sweep1_kernel, 1),
         [(plane, F32), (plane, F32), ((4, depth, slots), F32)],
-        [(long, F32), (long, F32), ((2, *sums), F32)],
-        lists, feat_r, feat_l, left, own, recv1, weight, source, back,
+        [(long, F32), (long, F32), ((2, *sums), F32), stash_shape(slots)],
+        lists, feat_r, feat_l, left, own, recv1, weight, source, posc,
     )
     recv2 = around(send2, "col", -1)
     (p2,) = local_call(
         functools.partial(sweep2_kernel, 2),
         [(plane, F32)],
-        [(long, F32), (sums, F32)],
-        lists, feat_r, feat_l, own, recv1, recv2, weight, source, diag, p1, here,
+        [(long, F32), (sums, F32), stash_shape(slots)],
+        lists, feat_r, feat_l, own, recv1, recv2, weight, source, diag, p1, posc,
     )
     recv3 = around(p2, "col", 1)
     (p3,) = local_call(
         functools.partial(sweep3_kernel, 3),
         [(plane, F32)],
-        [(long, F32), (sums, F32)],
-        lists, feat_r, feat_l, left, own, recv1, recv3, weight, source, diag, p2, back,
+        [(long, F32), (sums, F32), stash_shape(slots)],
+        lists, feat_r, feat_l, left, own, recv1, recv3, weight, source, diag, p2, posc,
     )
     recv4 = around(p3, "col", -1)
     inner = (2, cells, slots)
@@ -573,8 +583,10 @@
             ((2 * depth, KE, slots), BF16),
             ((8 * KE, slots), F32),
             ((3, *sums), F32),
+            stash_shape(slots),
+            stash_shape(slots),
         ],
-        lists, feat_r, feat_l, own, recv1, recv2, recv4, left, right, weight, p3, here,
+        lists, feat_r, feat_l, own, recv1, recv2, recv4, left, right, weight, p3, posc,
     )
     density_ratio = density_ratio[:, HALO : HALO + cells]
     blocks = leaving_slot.shape[0]

time: 191 us -> 198 us (1.037); the launches traced: 189 us -> 199 us
  Pallas kernels: 130 us -> 143 us
    pallas_call x6, Pallas kernels: 130 us -> 143 us  [local_call(): pl.pallas_call(kernel, out_shape=[jax.ShapeDtypeStruct(shape, dtype) for...]
    broadcast_in_dim x3 -> x1, local copies, waits for them, and re-layouts: 3.07 us -> 0.1 us  [target_lists(): tables[np.arange(ITERS + 2) % 2][:, None]]
  transfers between devices with their start and end apart: 10 -> 10, of which waited for: 8 -> 7; matrix products, arithmetic and copies ran while one was open for 4% -> 4% of each run, Pallas kernels for 0% -> 0%
where the time goes in v6:
time: 198 us; the launch traced here: 199 us
  Pallas kernels  143 us (72%)
  waiting for transfers between devices  29.3 us (15%)
  starting transfers between devices  12.5 us (6%)
  other arithmetic  7.15 us (4%)
  local copies, waits for them, and re-layouts  6.63 us (3%)
    pallas_call x6, Pallas kernels, local_call(): pl.pallas_call(kernel, out_shape=[jax.ShapeDtypeStruct(shape, dtype) for...  143 us
    ppermute x6, waiting for transfers between devices, around(): lax.ppermute(block, axis, [(i, (i + distance) % peers) for i in range(pee...  21.6 us
    ppermute x4, starting transfers between devices, from_behind(): return lax.ppermute(block, axis, route)  9.74 us
    ppermute x4, waiting for transfers between devices, from_behind(): return lax.ppermute(block, axis, route)  7.67 us
    unnamed x26, local copies, waits for them, and re-layouts  4.62 us
  transfers between devices with their start and end apart: 10, of which 7 were waited for; matrix products, arithmetic and copies ran while one was open for 4% of the time, Pallas kernels for 0%

profile of v6, /device:TPU:28, one launch (start us, length us, event | category | flops | bytes accessed | tf_op | source)
XLA Modules:
  0.0 199.4 jit_solution(12326049607723743526)
XLA Ops:
  0.6 0.9 fusion.6
  1.6 0.8 pad_maximum_fusion.4
  2.4 2.4 %collective-permute-start.1 = (f32[6,2,8,128]{3,2,1,0:T(8,128)S(1)}, f32[6,2,8,128]{3,2,1,0:T(8,128)S(1)}, u32[]{:S(2)}, u32[]{:S(2)}) collective-permute-start(f32[6,2,8,128]{3,2,1,0:T(8,128)S(1)} %get-tuple-element.57), channel_id=1, source_target_pairs={{1,0},{2,1},{3,2},{5,4},{6,5},{7,6},{9,8},{10,9},{11,10},{13,12},{... | collective-permute-start | bytes 147464 | tf_op jit(solution)/shard_map/ppermute | solution.py:498
  4.7 1.3 collective-permute-start
  6.0 0.7 pad_clamp_fusion
  6.7 4.0 %collective-permute-done = f32[6,2,8,128]{3,2,1,0:T(8,128)S(1)} collective-permute-done((f32[6,2,8,128]{3,2,1,0:T(8,128)S(1)}, f32[6,2,8,128]{3,2,1,0:T(8,128)S(1)}, u32[]{:S(2)}, u32[]{:S(2)}) %collective-permute-start) | collective-permute-done | bytes 49184 | tf_op jit(solution)/shard_map/ppermute | solution.py:498
  10.7 1.0 pad_maximum_fusion.own
  11.9 0.6 gather_fusion
  12.7 2.7 %collective-permute-start.3 = (f32[5,1,80,128]{3,2,1,0:T(8,128)S(1)}, f32[5,1,80,128]{3,2,1,0:T(8,128)S(1)}, u32[]{:S(2)}, u32[]{:S(2)}) collective-permute-start(f32[5,1,80,128]{3,2,1,0:T(8,128)S(1)} %slice.48), channel_id=1, source_target_pairs={{0,28},{4,0},{8,4},{12,8},{16,12},{20,16},{24,20},{28,24},{1,29},{... | collective-permute-start | bytes 614408 | tf_op jit(solution)/shard_map/ppermute | solution.py:503
  15.4 7.8 %collective-permute-done.2.left = f32[6,2,80,128]{3,2,1,0:T(8,128)S(1)} collective-permute-done((f32[6,2,80,128]{3,2,1,0:T(8,128)S(1)}, f32[6,2,80,128]{3,2,1,0:T(8,128)S(1)}, u32[]{:S(2)}, u32[]{:S(2)}) %collective-permute-start.2) | collective-permute-done | bytes 491552 | tf_op jit(solution)/shard_map/ppermute | solution.py:503
  24.8 0.7 pad_add_fusion.bounds
  25.4 0.7 fusion.1.order
  26.1 0.7 copy-done.3
  26.8 44.1 %shard_map.163 = (bf16[400,32,128]{2,1,0:T(8,128)(2,1)}, bf16[240,32,128]{2,1,0:T(8,128)(2,1)}, f32[2,80,128]{2,1,0:T(8,128)}, f32[2,80,128]{2,1,0:T(8,128)}, f3...) custom-call(s32[5,176]{1,0:T(8,128)} %fusion.1.order, s32[5,6]{1,0:T(8,128)} %pad_add_fusion.bounds, ...), custom_call_target="tpu_custom_call" | custom-call | tf_op jit(solution)/shard_map/pallas_call | solution.py:485
  70.9 5.4 %collective-permute-done.4.recv.recv1 = f32[3,80,128]{2,1,0:T(8,128)S(1)} collective-permute-done((f32[3,80,128]{2,1,0:T(8,128)}, f32[3,80,128]{2,1,0:T(8,128)S(1)}, u32[]{:S(2)}, u32[]{:S(2)}) %collective-permute-start.4) | collective-permute-done | bytes 122912 | tf_op jit(solution)/shard_map/ppermute | solution.py:503
  76.3 0.7 copy-done.2
  76.9 25.0 %shard_map.164 = (f32[2,80,128]{2,1,0:T(8,128)}, f32[2,80,128]{2,1,0:T(8,128)}, f32[4,80,128]{2,1,0:T(8,128)}) custom-call(s32[5,176]{1,0:T(8,128)} %fusion.1.order, s32[5,6]{1,0:T(8,128)} %pad_add_fusion.bounds, bf16[400,32,128]{2,1,0:T(8,128)(2,1)} %get-tuple-element.22.feat_r, bf16[240,32,128]{2,1,0:T(8,128)(2,1)} %get-tuple-element.23.feat_l, ...), custom_call_target="tpu_custom_call" | custom-call | tf_op jit(solution)/shard_map/pallas_call | solution.py:485
  101.9 3.2 %collective-permute-done.5.recv2 = f32[4,80,128]{2,1,0:T(8,128)S(1)} collective-permute-done((f32[4,80,128]{2,1,0:T(8,128)}, f32[4,80,128]{2,1,0:T(8,128)S(1)}, u32[]{:S(2)}, u32[]{:S(2)}) %collective-permute-start.5) | collective-permute-done | bytes 163872 | tf_op jit(solution)/shard_map/ppermute | solution.py:503
  105.1 0.7 copy-done.4
  105.7 19.8 %shard_map.165.p2 = f32[2,80,128]{2,1,0:T(8,128)} custom-call(s32[5,176]{1,0:T(8,128)} %fusion.1.order, s32[5,6]{1,0:T(8,128)} %pad_add_fusion.bounds, bf16[400,32,128]{2,1,0:T(8,128)(2,1)} %get-tuple-element.22.feat_r, bf16[240,32,128]{2,1,0:T(8,128)(2,1)} %get-tuple-element.23.feat_l, f32[6,2,80,128]{3,2,1,0:T(8,128)} %copy-done, f32[3,80,128]{2,1,0:T(8,128)} %copy-done.2, ...), custom_call_target="tpu_custom_call" | custom-call | tf_op jit(solution)/shard_map/pallas_call | solution.py:485
  125.6 5.0 %collective-permute-done.6.recv3 = f32[2,80,128]{2,1,0:T(8,128)S(1)} collective-permute-done((f32[2,80,128]{2,1,0:T(8,128)}, f32[2,80,128]{2,1,0:T(8,128)S(1)}, u32[]{:S(2)}, u32[]{:S(2)}) %collective-permute-start.6) | collective-permute-done | bytes 81952 | tf_op jit(solution)/shard_map/ppermute | solution.py:503
  130.5 0.6 copy-done.7
  131.2 19.5 %shard_map.166.p3 = f32[2,80,128]{2,1,0:T(8,128)} custom-call(s32[5,176]{1,0:T(8,128)} %fusion.1.order, s32[5,6]{1,0:T(8,128)} %pad_add_fusion.bounds, bf16[400,32,128]{2,1,0:T(8,128)(2,1)} %get-tuple-element.22.feat_r, bf16[240,32,128]{2,1,0:T(8,128)(2,1)} %get-tuple-element.23.feat_l, f32[6,2,80,128]{3,2,1,0:T(8,128)} %copy-done.1, ...), custom_call_target="tpu_custom_call" | custom-call | tf_op jit(solution)/shard_map/pallas_call | solution.py:485
  150.7 0.7 fusion.mass
  151.4 0.7 copy.27.count
  152.1 0.7 copy.28.side
  153.7 31.4 %shard_map.167 = (f32[2,64,128]{2,1,0:T(8,128)}, f32[2,2,64,128]{3,2,1,0:T(8,128)}, f32[2,2,64,128]{3,2,1,0:T(8,128)}, f32[2,2,64,128]{3,2,1,0:T(8,128)}) custom-call(s32[5,176]{1,0:T(8,128)} %fusion.1.order, s32[5,6]{1,0:T(8,128)} %pad_add_fusion.bounds, bf16[400,32,128]{2,1,0:T(8,128)(2,1)} %get-tuple-element.22.feat_r, ...), custom_call_target="tpu_custom_call" | custom-call | tf_op jit(solution)/shard_map/pallas_call | solution.py:485
  185.1 3.2 %shard_map.168 = (f32[6,8,128]{2,1,0:T(8,128)}, f32[6,8,128]{2,1,0:T(8,128)}) custom-call(s32[8,128]{1,0:T(8,128)} %bitcast.23, s32[8,1]{1,0:T(8,128)} %copy.27.count, s32[8,1]{1,0:T(8,128)} %copy.28.side, f32[2,2,64,128]{3,2,1,0:T(8,128)} %get-tuple-element.52.offsets, f32[2,2,64,128]{3,2,1,0:T(8,128)} %get-tuple-element.51.velocity, ...), custom_call_target="tpu_custom_call" | custom-call | tf_op jit(solution)/shard_map/pallas_call | solution.py:485
  188.3 4.2 %collective-permute-start.9 = (f32[6,8,128]{2,1,0:T(8,128)}, f32[6,8,128]{2,1,0:T(8,128)S(1)}, u32[]{:S(2)}, u32[]{:S(2)}) collective-permute-start(f32[6,8,128]{2,1,0:T(8,128)} %get-tuple-element.35), channel_id=1, source_target_pairs={{4,0},{8,4},{12,8},{16,12},{20,16},{24,20},{28,24},{5,1},{9,5},{13... | collective-permute-start | bytes 73736 | tf_op jit(solution)/shard_map/ppermute | solution.py:498
  192.5 1.9 collective-permute-start.8
  194.4 0.6 slice.42
  195.1 3.7 %collective-permute-done.8 = f32[6,8,128]{2,1,0:T(8,128)S(1)} collective-permute-done((f32[6,8,128]{2,1,0:T(8,128)}, f32[6,8,128]{2,1,0:T(8,128)S(1)}, u32[]{:S(2)}, u32[]{:S(2)}) %collective-permute-start.8) | collective-permute-done | bytes 24608 | tf_op jit(solution)/shard_map/ppermute | solution.py:498
  (51 shorter events, 3.5 us)
Async XLA Ops:
  2.4 4.4 %collective-permute-start.1 = (f32[6,2,8,128]{3,2,1,0:T(8,128)S(1)}, f32[6,2,8,128]{3,2,1,0:T(8,128)S(1)}, u32[]{:S(2)}, u32[]{:S(2)}) collective-permute-start(f32[6,2,8,128]{3,2,1,0:T(8,128)S(1)} %get-tuple-element.57), channel_id=1, source_target_pairs={{1,0},{2,1},{3,2},{5,4},{6,5},{7,6},{9,8},{10,9},{11,10},{13,12},{... | collective-permute-start | bytes 147464 | tf_op jit(solution)/shard_map/ppermute | solution.py:498
  4.7 6.0 %collective-permute-start = (f32[6,2,8,128]{3,2,1,0:T(8,128)S(1)}, f32[6,2,8,128]{3,2,1,0:T(8,128)S(1)}, u32[]{:S(2)}, u32[]{:S(2)}) collective-permute-start(f32[6,2,8,128]{3,2,1,0:T(8,128)S(1)} %get-tuple-element.56), channel_id=1, source_target_pairs={{0,1},{1,2},{2,3},{4,5},{5,6},{6,7},{8,9},{9,10},{10,11},{12,13},{... | collective-permute-start | bytes 147464 | tf_op jit(solution)/shard_map/ppermute | solution.py:498
  11.8 14.3 %copy-start = (f32[6,2,80,128]{3,2,1,0:T(8,128)}, f32[6,2,80,128]{3,2,1,0:T(8,128)S(1)}, u32[]{:S(2)}) copy-start(f32[6,2,80,128]{3,2,1,0:T(8,128)S(1)} %pad_maximum_fusion.own) | copy-start | bytes 1474564
  11.8 11.4 %collective-permute-start.2 = (f32[6,2,80,128]{3,2,1,0:T(8,128)S(1)}, f32[6,2,80,128]{3,2,1,0:T(8,128)S(1)}, u32[]{:S(2)}, u32[]{:S(2)}) collective-permute-start(f32[6,2,80,128]{3,2,1,0:T(8,128)S(1)} %pad_maximum_fusion.own), channel_id=1, source_target_pairs={{0,4},{4,8},{8,12},{12,16},{16,20},{20,24},{24,28},{28,0},{1,5},{5... | collective-permute-start | bytes 1474568 | tf_op jit(solution)/shard_map/ppermute | solution.py:503
  12.7 13.4 %collective-permute-start.3 = (f32[5,1,80,128]{3,2,1,0:T(8,128)S(1)}, f32[5,1,80,128]{3,2,1,0:T(8,128)S(1)}, u32[]{:S(2)}, u32[]{:S(2)}) collective-permute-start(f32[5,1,80,128]{3,2,1,0:T(8,128)S(1)} %slice.48), channel_id=1, source_target_pairs={{0,28},{4,0},{8,4},{12,8},{16,12},{20,16},{24,20},{28,24},{1,29},{... | collective-permute-start | bytes 614408 | tf_op jit(solution)/shard_map/ppermute | solution.py:503
  23.2 2.9 %copy-start.1 = (f32[6,2,80,128]{3,2,1,0:T(8,128)}, f32[6,2,80,128]{3,2,1,0:T(8,128)S(1)}, u32[]{:S(2)}) copy-start(f32[6,2,80,128]{3,2,1,0:T(8,128)S(1)} %collective-permute-done.2.left) | copy-start | bytes 1474564
  26.1 0.7 copy-start.3
  70.9 5.4 %collective-permute-start.4 = (f32[3,80,128]{2,1,0:T(8,128)}, f32[3,80,128]{2,1,0:T(8,128)S(1)}, u32[]{:S(2)}, u32[]{:S(2)}) collective-permute-start(f32[3,80,128]{2,1,0:T(8,128)} %get-tuple-element.24), channel_id=1, source_target_pairs={{0,4},{4,8},{8,12},{12,16},{16,20},{20,24},{24,28},{28,0},{1,5},{5... | collective-permute-start | bytes 368648 | tf_op jit(solution)/shard_map/ppermute | solution.py:503
  76.3 0.7 copy-start.2
  101.9 3.2 %collective-permute-start.5 = (f32[4,80,128]{2,1,0:T(8,128)}, f32[4,80,128]{2,1,0:T(8,128)S(1)}, u32[]{:S(2)}, u32[]{:S(2)}) collective-permute-start(f32[4,80,128]{2,1,0:T(8,128)} %get-tuple-element.27), channel_id=1, source_target_pairs={{0,28},{4,0},{8,4},{12,8},{16,12},{20,16},{24,20},{28,24},{1,29},{... | collective-permute-start | bytes 491528 | tf_op jit(solution)/shard_map/ppermute | solution.py:503
  105.0 0.7 copy-start.4
  125.5 25.2 %copy-start.5 = (f32[2,64,128]{2,1,0:T(8,128)S(1)}, f32[2,64,128]{2,1,0:T(8,128)}, u32[]{:S(2)}) copy-start(f32[2,64,128]{2,1,0:T(8,128)} %param.14) | copy-start | bytes 196612
  125.5 25.2 %copy-start.9 = (s32[2,64]{1,0:T(2,128)S(1)}, s32[2,64]{1,0:T(2,128)}, u32[]{:S(2)}) copy-start(s32[2,64]{1,0:T(2,128)} %param.16) | copy-start | bytes 1540
  125.5 25.9 %copy-start.10 = (s32[8,1]{0,1:T(1,128)S(1)}, s32[8,1]{0,1:T(1,128)}, u32[]{:S(2)}) copy-start(s32[8,1]{0,1:T(1,128)} %param.18) | copy-start | bytes 100
  125.5 26.6 %copy-start.11 = (s32[8,1]{0,1:T(1,128)S(1)}, s32[8,1]{0,1:T(1,128)}, u32[]{:S(2)}) copy-start(s32[8,1]{0,1:T(1,128)} %param.19) | copy-start | bytes 100
  125.5 5.0 %collective-permute-start.6 = (f32[2,80,128]{2,1,0:T(8,128)}, f32[2,80,128]{2,1,0:T(8,128)S(1)}, u32[]{:S(2)}, u32[]{:S(2)}) collective-permute-start(f32[2,80,128]{2,1,0:T(8,128)} %shard_map.165.p2), channel_id=1, source_target_pairs={{0,4},{4,8},{8,12},{12,16},{16,20},{20,24},{24,28},{28,0},{1,5},{5... | collective-permute-start | bytes 245768 | tf_op jit(solution)/shard_map/ppermute | solution.py:503
  130.5 0.6 copy-start.7
  150.7 2.4 %collective-permute-start.7 = (f32[2,80,128]{2,1,0:T(8,128)}, f32[2,80,128]{2,1,0:T(8,128)S(1)}, u32[]{:S(2)}, u32[]{:S(2)}) collective-permute-start(f32[2,80,128]{2,1,0:T(8,128)} %shard_map.166.p3), channel_id=1, source_target_pairs={{0,28},{4,0},{8,4},{12,8},{16,12},{20,16},{24,20},{28,24},{1,29},{... | collective-permute-start | bytes 245768 | tf_op jit(solution)/shard_map/ppermute | solution.py:503
  152.7 41.7 %copy-start.8 = (f32[2,80,128]{2,1,0:T(8,128)S(1)}, f32[2,80,128]{2,1,0:T(8,128)}, u32[]{:S(2)}) copy-start(f32[2,80,128]{2,1,0:T(8,128)} %get-tuple-element.21) | copy-start | bytes 245764
  153.0 0.6 copy-start.6
  188.3 6.8 %collective-permute-start.9 = (f32[6,8,128]{2,1,0:T(8,128)}, f32[6,8,128]{2,1,0:T(8,128)S(1)}, u32[]{:S(2)}, u32[]{:S(2)}) collective-permute-start(f32[6,8,128]{2,1,0:T(8,128)} %get-tuple-element.35), channel_id=1, source_target_pairs={{4,0},{8,4},{12,8},{16,12},{20,16},{24,20},{28,24},{5,1},{9,5},{13... | collective-permute-start | bytes 73736 | tf_op jit(solution)/shard_map/ppermute | solution.py:498
  192.5 6.3 %collective-permute-start.8 = (f32[6,8,128]{2,1,0:T(8,128)}, f32[6,8,128]{2,1,0:T(8,128)S(1)}, u32[]{:S(2)}, u32[]{:S(2)}) collective-permute-start(f32[6,8,128]{2,1,0:T(8,128)} %get-tuple-element.34), channel_id=1, source_target_pairs={{0,4},{4,8},{8,12},{12,16},{16,20},{20,24},{24,28},{1,5},{5,9},{9,... | collective-permute-start | bytes 73736 | tf_op jit(solution)/shard_map/ppermute | solution.py:498

commit v7 on v4

--- a/solution.py
+++ b/solution.py
@@ -2,6 +2,7 @@
 
 import jax
 import jax.numpy as jnp
+import ml_dtypes
 import numpy as np
 from jax import lax
 from jax.experimental import pallas as pl
@@ -20,8 +21,6 @@
 CHUNKS = ((0, 1), (2, 3), (4, 5), (6, 7), (8,))
 AHEAD = 2
 KP = 32
-KD = 48
-KE = 16
 FAR = -64.0
 SHIFTS = [(sx, sz) for sx in (-1, 0, 1) for sz in (-1, 0, 1)]
 F32 = jnp.float32
@@ -66,54 +65,20 @@
     return [1] * 6 + [sx] * 3 + [-sx] * 3 + [1] * 6 + [sz] * 3 + [-sz] * 3 + [1] * 6 + [-(sx * sx + sz * sz), 0]
 
 
-def velocity_rows(x, z, vx, vz):
-    one, zero = jnp.ones_like(x), jnp.zeros_like(x)
-    x, z = x - 0.5, z - 0.5
-    xs, zs, vxs, vzs = split3(x), split3(z), split3(vx), split3(vz)
-    dots = split3(vx * x + vz * z)
-    ones = [one] * 3
-    pad = [zero] * 6
-    minus = lambda rows: [-v for v in rows]
-    target = dots + left_six(vxs) + left_six(vzs) + left_six(xs) + left_six(zs) + ones + vxs + vzs + ones + ones + pad
-    source = (
-        ones
-        + minus(right_six(xs) + right_six(zs) + right_six(vxs) + right_six(vzs))
-        + dots
-        + ones
-        + ones
-        + vxs
-        + vzs
-        + pad
-    )
-    return target, source
-
-
-def velocity_signs(sx, sz):
-    return [1] * 30 + [-sx] * 3 + [-sz] * 3 + [sx] * 3 + [sz] * 3 + [0] * 6
-
-
-def pressure_rows(weight, lifted, pressure):
-    one, zero = jnp.ones_like(weight), jnp.zeros_like(weight)
-    pad = [zero] * 7
-    target = [one] * 3 + left_six(split3(pressure)) + pad
-    source = split3(lifted) + [-v for v in right_six(split3(weight))] + pad
-    return target, source
-
-
-def sign_table(signs):
-    table = np.asarray([signs(sx, sz) for sx, sz in SHIFTS], np.float32)
-    return jnp.broadcast_to(jnp.asarray(table)[:, :, None], (*table.shape, 128)).astype(BF16)
-
-
-def position_table(cut_first, cut_second):
-    table = np.asarray([position_signs(sx, sz) for sx, sz in SHIFTS] * 2, np.float32)
-    constant = np.arange(KP) == KP - 2
-    sides = np.asarray([sx for sx, _ in SHIFTS] * 2)
-    target = np.repeat([0, 1], 9)
-    spots = lambda t, side: jnp.asarray(((target == t) & (sides == side))[:, None] & constant)
-    table = jnp.where(spots(0, cut_first[1]) & cut_first[0], FAR, jnp.asarray(table))
-    table = jnp.where(spots(1, cut_second[1]) & cut_second[0], FAR, table)
-    return jnp.broadcast_to(table[:, :, None], (18, KP, 128)).astype(BF16)
+def wide_table(table):
+    return np.repeat(np.asarray(table, np.float32)[:, :, None], 128, axis=2).astype(ml_dtypes.bfloat16)
+
+
+def position_table():
+    tables = []
+    for cuts in ((), ((0, -1),), ((1, 1),), ((0, 1), (1, -1))):
+        for t in range(2):
+            for sx, sz in SHIFTS:
+                signs = position_signs(sx, sz)
+                if (t, sx) in cuts:
+                    signs[KP - 2] = FAR
+                tables.append(signs)
+    return wide_table(tables)
 
 
 def store_rows(rows, stage, dest, cell):
@@ -125,6 +90,10 @@
 
 def upright(rows, slots):
     return rows.astype(F32).T[:slots].astype(BF16)
+
+
+def spread(row, slots):
+    return jnp.broadcast_to(row, (128, 128)).T[:slots]
 
 
 def sources_of(feat, cell, depth, chunk, table=None, first=0):
@@ -171,9 +140,9 @@
 
 
 def density_kernel(
-    level, order, bounds, left, own, right, posc, velc,
+    level, order, bounds, left, own, right, posc,
     out_r, out_l, out_w, out_density, out_source, out_send,
-    stage_p, stage_d, vel_r, vel_l, wide_m, acc,
+    stage_p, wide_m, wide_x, wide_z, wide_vx, wide_vz, acc,
 ):
     depth = own.shape[2]
     groups = depth // 8
@@ -182,45 +151,42 @@
     def prepare(group, carry):
         rows = pl.ds(pl.multiple_of(group * 8, 8), 8)
         for col, (ref, at) in enumerate(blocks):
-            x, z, vx, vz = (ref[f, at, rows, :] for f in range(4))
+            x, z = ref[0, at, rows, :], ref[1, at, rows, :]
             cell = pl.multiple_of(col * depth + group * 8, 8)
             target, source = position_rows(x, z)
             store_rows(source, stage_p, out_r, cell)
             if 1 <= col <= 3:
                 store_rows(target, stage_p, out_l, pl.multiple_of((col - 1) * depth + group * 8, 8))
-            if col >= 1:
-                target, source = velocity_rows(x, z, vx, vz)
-                store_rows(source, stage_d, vel_r, pl.multiple_of((col - 1) * depth + group * 8, 8))
-                if 2 <= col <= 3:
-                    store_rows(target, stage_d, vel_l, pl.multiple_of((col - 2) * depth + group * 8, 8))
         return carry
 
     lax.fori_loop(0, groups, prepare, 0)
     acc[...] = jnp.zeros_like(acc)
 
-    wide_m[0:depth] = left[4, 1]
-    wide_m[depth : 2 * depth] = own[4, 0]
-    wide_m[2 * depth : 3 * depth] = own[4, 1]
-    wide_m[3 * depth : 4 * depth] = right[4, 0]
+    wides = (wide_x, wide_z, wide_vx, wide_vz, wide_m)
+    for field, wide in enumerate(wides):
+        wide[0:depth] = left[field, 1]
+        wide[depth : 2 * depth] = own[field, 0]
+        wide[2 * depth : 3 * depth] = own[field, 1]
+        wide[3 * depth : 4 * depth] = right[field, 0]
 
     def target(cell, slots):
-        sign = 9 * (cell >= depth).astype(jnp.int32)
-        pos_l, vel_l_t = upright(out_l[cell + depth], slots), upright(vel_l[cell], slots)
+        sign = bounds[level, len(CLASSES) + 1] + 9 * (cell >= depth).astype(jnp.int32)
+        pos_l = upright(out_l[cell + depth], slots)
+        x, z, vx, vz = [spread(w[pl.ds(cell + depth, 1), :], slots) for w in wides[:4]]
         sums = [jnp.zeros((slots, 128), F32)] * 2
 
         def issue(chunk):
-            return (
-                product(pos_l, sources_of(out_r, cell + depth, depth, chunk, posc, sign)),
-                product(vel_l_t, sources_of(vel_r, cell, depth, chunk, velc)),
-            )
+            return product(pos_l, sources_of(out_r, cell + depth, depth, chunk, posc, sign))
 
         def consume(chunk, products):
             for i, n in enumerate(chunk):
-                lanes = slice(128 * i, 128 * (i + 1))
-                s = jnp.maximum(products[0][:, lanes], 0.0)
-                q = s * s * wide_m[pl.ds(cell + (n // 3) * depth + n % 3 - 1, 1), :]
+                s = jnp.maximum(products[:, 128 * i : 128 * (i + 1)], 0.0)
+                at = pl.ds(cell + (n // 3) * depth + n % 3 - 1, 1)
+                q = s * s * wide_m[at, :]
+                closing = (vx - wide_vx[at, :]) * (x - (wide_x[at, :] + float(n // 3 - 1)))
+                closing = closing + (vz - wide_vz[at, :]) * (z - (wide_z[at, :] + float(n % 3 - 1)))
                 sums[0] = sums[0] + q * s
-                sums[1] = sums[1] + q * products[1][:, lanes]
+                sums[1] = sums[1] + q * closing
 
         def finish():
             for i in range(2):
@@ -252,7 +218,7 @@
 
 def jacobi_sums(level, order, bounds, first_col, feat_r, feat_l, posc, wide_u, acc, depth):
     def target(cell, slots):
-        sign = 9 * (cell >= depth).astype(jnp.int32)
+        sign = bounds[level, len(CLASSES) + 1] + 9 * (cell >= depth).astype(jnp.int32)
         at = cell + first_col * depth
         pos_l = upright(feat_l[at], slots)
         sums = [jnp.zeros((slots, 128), F32)]
@@ -291,7 +257,7 @@
     acc[...] = jnp.zeros_like(acc)
 
     def target(cell, slots):
-        sign = 9 * (cell >= depth).astype(jnp.int32)
+        sign = bounds[level, len(CLASSES) + 1] + 9 * (cell >= depth).astype(jnp.int32)
         pos_l = upright(feat_l[cell], slots)
         sums = [jnp.zeros((slots, 128), F32)] * 2
 
@@ -355,48 +321,33 @@
 def force_kernel(
     level, order, bounds, feat_r, feat_l, own, recv1, recv2, recv4, left, right, weight_own, p3, posc,
     out_pressure, out_acc, out_velocity, out_offsets,
-    wide_p, wide_w, wide_x, wide_z, pres_r, pres_l, stage, acc,
+    wide_p, wide_w, wide_x, wide_z, acc,
 ):
     depth = weight_own.shape[1]
-    wide_p[0:2] = p3[...]
-    wide_p[2:4] = recv4[...]
-    wide_w[0] = recv1[1]
-    wide_w[1:3] = weight_own[...]
-    wide_w[3] = recv2[2]
+    wide_p[0 : 2 * depth] = p3[...].reshape(2 * depth, 128)
+    wide_p[2 * depth : 4 * depth] = recv4[...].reshape(2 * depth, 128)
+    wide_w[0:depth] = recv1[1]
+    wide_w[depth : 3 * depth] = weight_own[...].reshape(2 * depth, 128)
+    wide_w[3 * depth : 4 * depth] = recv2[2]
     for field, wide in ((0, wide_x), (1, wide_z)):
         wide[0:depth] = left[field, 1] - 0.5
         wide[depth : 3 * depth] = own[field].reshape(2 * depth, 128) - 0.5
         wide[3 * depth : 4 * depth] = right[field, 0] - 0.5
 
-    def prepare(group, carry):
-        rows = pl.ds(pl.multiple_of(group * 8, 8), 8)
-        for col in range(4):
-            pressure, weight = wide_p[col, rows, :], wide_w[col, rows, :]
-            target, source = pressure_rows(weight, weight * pressure, pressure)
-            store_rows(source, stage, pres_r, pl.multiple_of(col * depth + group * 8, 8))
-            if 1 <= col <= 2:
-                store_rows(target, stage, pres_l, pl.multiple_of((col - 1) * depth + group * 8, 8))
-        return carry
-
-    lax.fori_loop(0, depth // 8, prepare, 0)
-
     def target(cell, slots):
-        sign = 9 * (cell >= depth).astype(jnp.int32)
-        pos_l, pres_l_t = upright(feat_l[cell + depth], slots), upright(pres_l[cell], slots)
+        sign = bounds[level, len(CLASSES) + 1] + 9 * (cell >= depth).astype(jnp.int32)
+        pos_l = upright(feat_l[cell + depth], slots)
+        here = spread(wide_p[pl.ds(cell + depth, 1), :], slots)
         sums = [jnp.zeros((slots, 128), F32)] * 3
 
         def issue(chunk):
-            return (
-                product(pos_l, sources_of(feat_r, cell + depth, depth, chunk, posc, sign)),
-                product(pres_l_t, sources_of(pres_r, cell, depth, chunk)),
-            )
+            return product(pos_l, sources_of(feat_r, cell + depth, depth, chunk, posc, sign))
 
         def consume(chunk, products):
             for i, n in enumerate(chunk):
-                lanes = slice(128 * i, 128 * (i + 1))
-                s = jnp.maximum(products[0][:, lanes], 0.0)
-                g = s * s * products[1][:, lanes]
+                s = jnp.maximum(products[:, 128 * i : 128 * (i + 1)], 0.0)
                 at = pl.ds(cell + (n // 3) * depth + n % 3 - 1, 1)
+                g = (s * wide_w[at, :]) * (s * (wide_p[at, :] - here))
                 sums[0] = sums[0] + g
                 sums[1] = sums[1] + g * (wide_x[at, :] + float(n // 3 - 1))
                 sums[2] = sums[2] + g * (wide_z[at, :] + float(n % 3 - 1))
@@ -451,7 +402,7 @@
         out_down[index] = jnp.where(up, 0.0, block)
 
 
-def target_lists(count, cells):
+def target_lists(count, cells, tables):
     depth = count.shape[1]
     number = jnp.arange(2 * depth, dtype=jnp.int32)
     kinds = []
@@ -465,10 +416,12 @@
     kinds = jnp.stack(kinds)
     key = kinds * (2 * depth) + number
     rank = jnp.sum((key[:, None, :] < key[:, :, None]).astype(jnp.int32), 2)
-    bounds = jnp.stack([jnp.sum((kinds < c).astype(jnp.int32), 1) for c in range(len(CLASSES) + 1)], 1)
+    steps = jnp.arange(len(CLASSES) + 1, dtype=jnp.int32)
+    bounds = jnp.sum((kinds[:, None, :] < steps[None, :, None]).astype(jnp.int32), 2)
     place = jnp.arange(2 * depth + max(c for _, c in CLASSES), dtype=jnp.int32)
     order = jnp.sum(jnp.where(rank[:, None, :] == place[None, :, None], number, 0), 2)
-    return jnp.where(place < bounds[:, -1:], order, HALO), bounds
+    order = jnp.where(place < bounds[:, -1:], order, HALO)
+    return order, jnp.concatenate([bounds, tables[np.arange(ITERS + 2) % 2][:, None]], 1)
 
 
 def local_call(kernel, out_shapes, scratch, scalars, *operands):
@@ -510,13 +463,13 @@
     depth = cells + 2 * HALO
     first = lax.axis_index("col") == 0
     last = lax.axis_index("col") == lax.axis_size("col") - 1
-    here = position_table((first, -1), (last, 1))
-    back = position_table((first, 1), (first, -1))
-    velc = sign_table(velocity_signs)
+    here = jnp.where(first, 1, jnp.where(last, 2, 0))
+    back = jnp.where(first, 3, 0)
+    posc = position_table()
     plane = (2, depth, slots)
 
     live = jnp.stack([left[4, 1], own[4, 0], own[4, 1]]) > 0.0
-    lists = target_lists(jnp.sum(live.astype(jnp.int32), -1), cells)
+    lists = target_lists(jnp.sum(live.astype(jnp.int32), -1), cells, 18 * jnp.stack([here, back]))
     long = (4 * depth, slots)
     sums = (2 * depth, slots)
 
@@ -532,49 +485,43 @@
         ],
         [
             ((8 * KP, slots), F32),
-            ((8 * KD, slots), F32),
-            ((4 * depth, KD, slots), BF16),
-            ((2 * depth, KD, slots), BF16),
+            (long, F32),
+            (long, F32),
+            (long, F32),
+            (long, F32),
             (long, F32),
             ((2, *sums), F32),
         ],
-        lists, left, own, right, here, velc,
+        lists, left, own, right, posc,
     )
     recv1 = around(send1, "col", 1)
     p1, diag, send2 = local_call(
         functools.partial(sweep1_kernel, 1),
         [(plane, F32), (plane, F32), ((4, depth, slots), F32)],
         [(long, F32), (long, F32), ((2, *sums), F32)],
-        lists, feat_r, feat_l, left, own, recv1, weight, source, back,
+        lists, feat_r, feat_l, left, own, recv1, weight, source, posc,
     )
     recv2 = around(send2, "col", -1)
     (p2,) = local_call(
         functools.partial(sweep2_kernel, 2),
         [(plane, F32)],
         [(long, F32), (sums, F32)],
-        lists, feat_r, feat_l, own, recv1, recv2, weight, source, diag, p1, here,
+        lists, feat_r, feat_l, own, recv1, recv2, weight, source, diag, p1, posc,
     )
     recv3 = around(p2, "col", 1)
     (p3,) = local_call(
         functools.partial(sweep3_kernel, 3),
         [(plane, F32)],
         [(long, F32), (sums, F32)],
-        lists, feat_r, feat_l, left, own, recv1, recv3, weight, source, diag, p2, back,
+        lists, feat_r, feat_l, left, own, recv1, recv3, weight, source, diag, p2, posc,
     )
     recv4 = around(p3, "col", -1)
     inner = (2, cells, slots)
     pressure, acceleration, velocity_new, offsets_new = local_call(
         functools.partial(force_kernel, 4),
         [(inner, F32), ((2, *inner), F32), ((2, *inner), F32), ((2, *inner), F32)],
-        [((4, depth, slots), F32)] * 2
-        + [(long, F32)] * 2
-        + [
-            ((4 * depth, KE, slots), BF16),
-            ((2 * depth, KE, slots), BF16),
-            ((8 * KE, slots), F32),
-            ((3, *sums), F32),
-        ],
-        lists, feat_r, feat_l, own, recv1, recv2, recv4, left, right, weight, p3, here,
+        [(long, F32)] * 4 + [((3, *sums), F32)],
+        lists, feat_r, feat_l, own, recv1, recv2, recv4, left, right, weight, p3, posc,
     )
     density_ratio = density_ratio[:, HALO : HALO + cells]
     blocks = leaving_slot.shape[0]

time: 191 us -> 206 us (1.079)
  Pallas kernels: 130 us -> 144 us
  starting transfers between devices: 13 us -> 16.3 us
    pallas_call x6, Pallas kernels: 130 us -> 144 us  [local_call(): pl.pallas_call(kernel, out_shape=[jax.ShapeDtypeStruct(shape, dtype) for...]
    broadcast_in_dim x3 -> x1, local copies, waits for them, and re-layouts: 3.07 us -> 0.1 us  [target_lists(): tables[np.arange(ITERS + 2) % 2][:, None]]
  transfers between devices with their start and end apart: 10 -> 10, of which waited for: 8 -> 7; matrix products, arithmetic and copies ran while one was open for 4% -> 3% of each run, Pallas kernels for 0% -> 0%
where the time goes in v7:
time: 206 us; the launch traced here: 203 us
  Pallas kernels  144 us (70%)
  waiting for transfers between devices  28.4 us (14%)
  starting transfers between devices  16.3 us (8%)
  other arithmetic  7.15 us (3%)
  local copies, waits for them, and re-layouts  6.63 us (3%)
    pallas_call x6, Pallas kernels, local_call(): pl.pallas_call(kernel, out_shape=[jax.ShapeDtypeStruct(shape, dtype) for...  144 us
    ppermute x6, waiting for transfers between devices, around(): lax.ppermute(block, axis, [(i, (i + distance) % peers) for i in range(pee...  20.7 us
    ppermute x4, starting transfers between devices, from_behind(): return lax.ppermute(block, axis, route)  11.4 us
    ppermute x4, waiting for transfers between devices, from_behind(): return lax.ppermute(block, axis, route)  7.67 us
    ppermute x6, starting transfers between devices, around(): lax.ppermute(block, axis, [(i, (i + distance) % peers) for i in range(pee...  4.88 us
    unnamed x26, local copies, waits for them, and re-layouts  4.62 us
  transfers between devices with their start and end apart: 10, of which 7 were waited for; matrix products, arithmetic and copies ran while one was open for 3% of the time, Pallas kernels for 0%

profile of v7, /device:TPU:28, one launch (start us, length us, event | category | flops | bytes accessed | tf_op | source)
XLA Modules:
  0.0 203.1 jit_solution(2852934369774931372)
XLA Ops:
  0.6 0.9 fusion.6
  1.6 0.8 pad_maximum_fusion.4
  2.4 2.4 %collective-permute-start.1 = (f32[6,2,8,128]{3,2,1,0:T(8,128)S(1)}, f32[6,2,8,128]{3,2,1,0:T(8,128)S(1)}, u32[]{:S(2)}, u32[]{:S(2)}) collective-permute-start(f32[6,2,8,128]{3,2,1,0:T(8,128)S(1)} %get-tuple-element.57), channel_id=1, source_target_pairs={{1,0},{2,1},{3,2},{5,4},{6,5},{7,6},{9,8},{10,9},{11,10},{13,12},{... | collective-permute-start | bytes 147464 | tf_op jit(solution)/shard_map/ppermute | solution.py:443
  4.7 1.3 collective-permute-start
  6.0 0.7 pad_clamp_fusion
  6.7 4.0 %collective-permute-done = f32[6,2,8,128]{3,2,1,0:T(8,128)S(1)} collective-permute-done((f32[6,2,8,128]{3,2,1,0:T(8,128)S(1)}, f32[6,2,8,128]{3,2,1,0:T(8,128)S(1)}, u32[]{:S(2)}, u32[]{:S(2)}) %collective-permute-start) | collective-permute-done | bytes 49184 | tf_op jit(solution)/shard_map/ppermute | solution.py:443
  10.7 1.0 pad_maximum_fusion.own
  11.9 0.6 gather_fusion
  12.7 2.7 %collective-permute-start.3 = (f32[5,1,80,128]{3,2,1,0:T(8,128)S(1)}, f32[5,1,80,128]{3,2,1,0:T(8,128)S(1)}, u32[]{:S(2)}, u32[]{:S(2)}) collective-permute-start(f32[5,1,80,128]{3,2,1,0:T(8,128)S(1)} %slice.48), channel_id=1, source_target_pairs={{0,28},{4,0},{8,4},{12,8},{16,12},{20,16},{24,20},{28,24},{1,29},{... | collective-permute-start | bytes 614408 | tf_op jit(solution)/shard_map/ppermute | solution.py:448
  15.4 7.8 %collective-permute-done.2.left = f32[6,2,80,128]{3,2,1,0:T(8,128)S(1)} collective-permute-done((f32[6,2,80,128]{3,2,1,0:T(8,128)S(1)}, f32[6,2,80,128]{3,2,1,0:T(8,128)S(1)}, u32[]{:S(2)}, u32[]{:S(2)}) %collective-permute-start.2) | collective-permute-done | bytes 491552 | tf_op jit(solution)/shard_map/ppermute | solution.py:448
  24.8 0.7 pad_add_fusion.bounds
  25.4 0.7 fusion.1.order
  26.1 0.7 copy-done.3
  26.8 48.4 %shard_map.154 = (bf16[400,32,128]{2,1,0:T(8,128)(2,1)}, bf16[240,32,128]{2,1,0:T(8,128)(2,1)}, f32[2,80,128]{2,1,0:T(8,128)}, f32[2,80,128]{2,1,0:T(8,128)}, f3...) custom-call(s32[5,176]{1,0:T(8,128)} %fusion.1.order, s32[5,6]{1,0:T(8,128)} %pad_add_fusion.bounds, ...), custom_call_target="tpu_custom_call" | custom-call | tf_op jit(solution)/shard_map/pallas_call | solution.py:430
  75.6 5.0 %collective-permute-done.4.recv.recv1 = f32[3,80,128]{2,1,0:T(8,128)S(1)} collective-permute-done((f32[3,80,128]{2,1,0:T(8,128)}, f32[3,80,128]{2,1,0:T(8,128)S(1)}, u32[]{:S(2)}, u32[]{:S(2)}) %collective-permute-start.4) | collective-permute-done | bytes 122912 | tf_op jit(solution)/shard_map/ppermute | solution.py:448
  80.6 0.7 copy-done.2
  81.3 23.7 %shard_map.155 = (f32[2,80,128]{2,1,0:T(8,128)}, f32[2,80,128]{2,1,0:T(8,128)}, f32[4,80,128]{2,1,0:T(8,128)}) custom-call(s32[5,176]{1,0:T(8,128)} %fusion.1.order, s32[5,6]{1,0:T(8,128)} %pad_add_fusion.bounds, bf16[400,32,128]{2,1,0:T(8,128)(2,1)} %get-tuple-element.22.feat_r, bf16[240,32,128]{2,1,0:T(8,128)(2,1)} %get-tuple-element.23.feat_l, ...), custom_call_target="tpu_custom_call" | custom-call | tf_op jit(solution)/shard_map/pallas_call | solution.py:430
  105.3 3.2 %collective-permute-done.5.recv2 = f32[4,80,128]{2,1,0:T(8,128)S(1)} collective-permute-done((f32[4,80,128]{2,1,0:T(8,128)}, f32[4,80,128]{2,1,0:T(8,128)S(1)}, u32[]{:S(2)}, u32[]{:S(2)}) %collective-permute-start.5) | collective-permute-done | bytes 163872 | tf_op jit(solution)/shard_map/ppermute | solution.py:448
  108.4 0.7 copy-done.4
  109.1 18.2 %shard_map.156.p2 = f32[2,80,128]{2,1,0:T(8,128)} custom-call(s32[5,176]{1,0:T(8,128)} %fusion.1.order, s32[5,6]{1,0:T(8,128)} %pad_add_fusion.bounds, bf16[400,32,128]{2,1,0:T(8,128)(2,1)} %get-tuple-element.22.feat_r, bf16[240,32,128]{2,1,0:T(8,128)(2,1)} %get-tuple-element.23.feat_l, f32[6,2,80,128]{3,2,1,0:T(8,128)} %copy-done, f32[3,80,128]{2,1,0:T(8,128)} %copy-done.2, ...), custom_call_target="tpu_custom_call" | custom-call | tf_op jit(solution)/shard_map/pallas_call | solution.py:430
  127.4 1.3 collective-permute-start.6
  128.7 4.4 %collective-permute-done.6.recv3 = f32[2,80,128]{2,1,0:T(8,128)S(1)} collective-permute-done((f32[2,80,128]{2,1,0:T(8,128)}, f32[2,80,128]{2,1,0:T(8,128)S(1)}, u32[]{:S(2)}, u32[]{:S(2)}) %collective-permute-start.6) | collective-permute-done | bytes 81952 | tf_op jit(solution)/shard_map/ppermute | solution.py:448
  133.8 17.7 %shard_map.157.p3 = f32[2,80,128]{2,1,0:T(8,128)} custom-call(s32[5,176]{1,0:T(8,128)} %fusion.1.order, s32[5,6]{1,0:T(8,128)} %pad_add_fusion.bounds, bf16[400,32,128]{2,1,0:T(8,128)(2,1)} %get-tuple-element.22.feat_r, bf16[240,32,128]{2,1,0:T(8,128)(2,1)} %get-tuple-element.23.feat_l, f32[6,2,80,128]{3,2,1,0:T(8,128)} %copy-done.1, ...), custom_call_target="tpu_custom_call" | custom-call | tf_op jit(solution)/shard_map/pallas_call | solution.py:430
  151.6 0.7 fusion.mass
  152.3 0.7 copy.26.count
  153.0 0.7 copy.27.side
  154.6 32.6 %shard_map.158 = (f32[2,64,128]{2,1,0:T(8,128)}, f32[2,2,64,128]{3,2,1,0:T(8,128)}, f32[2,2,64,128]{3,2,1,0:T(8,128)}, f32[2,2,64,128]{3,2,1,0:T(8,128)}) custom-call(s32[5,176]{1,0:T(8,128)} %fusion.1.order, s32[5,6]{1,0:T(8,128)} %pad_add_fusion.bounds, bf16[400,32,128]{2,1,0:T(8,128)(2,1)} %get-tuple-element.22.feat_r, ...), custom_call_target="tpu_custom_call" | custom-call | tf_op jit(solution)/shard_map/pallas_call | solution.py:430
  187.2 3.2 %shard_map.159 = (f32[6,8,128]{2,1,0:T(8,128)}, f32[6,8,128]{2,1,0:T(8,128)}) custom-call(s32[8,128]{1,0:T(8,128)} %bitcast.23, s32[8,1]{1,0:T(8,128)} %copy.26.count, s32[8,1]{1,0:T(8,128)} %copy.27.side, f32[2,2,64,128]{3,2,1,0:T(8,128)} %get-tuple-element.52.offsets, f32[2,2,64,128]{3,2,1,0:T(8,128)} %get-tuple-element.51.velocity, ...), custom_call_target="tpu_custom_call" | custom-call | tf_op jit(solution)/shard_map/pallas_call | solution.py:430
  190.4 5.8 %collective-permute-start.9 = (f32[6,8,128]{2,1,0:T(8,128)}, f32[6,8,128]{2,1,0:T(8,128)S(1)}, u32[]{:S(2)}, u32[]{:S(2)}) collective-permute-start(f32[6,8,128]{2,1,0:T(8,128)} %get-tuple-element.35), channel_id=1, source_target_pairs={{4,0},{8,4},{12,8},{16,12},{20,16},{24,20},{28,24},{5,1},{9,5},{13... | collective-permute-start | bytes 73736 | tf_op jit(solution)/shard_map/ppermute | solution.py:443
  196.2 1.9 collective-permute-start.8
  198.2 0.6 slice.42
  198.8 3.7 %collective-permute-done.8 = f32[6,8,128]{2,1,0:T(8,128)S(1)} collective-permute-done((f32[6,8,128]{2,1,0:T(8,128)}, f32[6,8,128]{2,1,0:T(8,128)S(1)}, u32[]{:S(2)}, u32[]{:S(2)}) %collective-permute-start.8) | collective-permute-done | bytes 24608 | tf_op jit(solution)/shard_map/ppermute | solution.py:443
  (51 shorter events, 4.9 us)
Async XLA Ops:
  2.4 4.4 %collective-permute-start.1 = (f32[6,2,8,128]{3,2,1,0:T(8,128)S(1)}, f32[6,2,8,128]{3,2,1,0:T(8,128)S(1)}, u32[]{:S(2)}, u32[]{:S(2)}) collective-permute-start(f32[6,2,8,128]{3,2,1,0:T(8,128)S(1)} %get-tuple-element.57), channel_id=1, source_target_pairs={{1,0},{2,1},{3,2},{5,4},{6,5},{7,6},{9,8},{10,9},{11,10},{13,12},{... | collective-permute-start | bytes 147464 | tf_op jit(solution)/shard_map/ppermute | solution.py:443
  4.7 6.0 %collective-permute-start = (f32[6,2,8,128]{3,2,1,0:T(8,128)S(1)}, f32[6,2,8,128]{3,2,1,0:T(8,128)S(1)}, u32[]{:S(2)}, u32[]{:S(2)}) collective-permute-start(f32[6,2,8,128]{3,2,1,0:T(8,128)S(1)} %get-tuple-element.56), channel_id=1, source_target_pairs={{0,1},{1,2},{2,3},{4,5},{5,6},{6,7},{8,9},{9,10},{10,11},{12,13},{... | collective-permute-start | bytes 147464 | tf_op jit(solution)/shard_map/ppermute | solution.py:443
  11.8 14.3 %copy-start = (f32[6,2,80,128]{3,2,1,0:T(8,128)}, f32[6,2,80,128]{3,2,1,0:T(8,128)S(1)}, u32[]{:S(2)}) copy-start(f32[6,2,80,128]{3,2,1,0:T(8,128)S(1)} %pad_maximum_fusion.own) | copy-start | bytes 1474564
  11.8 11.4 %collective-permute-start.2 = (f32[6,2,80,128]{3,2,1,0:T(8,128)S(1)}, f32[6,2,80,128]{3,2,1,0:T(8,128)S(1)}, u32[]{:S(2)}, u32[]{:S(2)}) collective-permute-start(f32[6,2,80,128]{3,2,1,0:T(8,128)S(1)} %pad_maximum_fusion.own), channel_id=1, source_target_pairs={{0,4},{4,8},{8,12},{12,16},{16,20},{20,24},{24,28},{28,0},{1,5},{5... | collective-permute-start | bytes 1474568 | tf_op jit(solution)/shard_map/ppermute | solution.py:448
  12.7 13.4 %collective-permute-start.3 = (f32[5,1,80,128]{3,2,1,0:T(8,128)S(1)}, f32[5,1,80,128]{3,2,1,0:T(8,128)S(1)}, u32[]{:S(2)}, u32[]{:S(2)}) collective-permute-start(f32[5,1,80,128]{3,2,1,0:T(8,128)S(1)} %slice.48), channel_id=1, source_target_pairs={{0,28},{4,0},{8,4},{12,8},{16,12},{20,16},{24,20},{28,24},{1,29},{... | collective-permute-start | bytes 614408 | tf_op jit(solution)/shard_map/ppermute | solution.py:448
  23.2 2.9 %copy-start.1 = (f32[6,2,80,128]{3,2,1,0:T(8,128)}, f32[6,2,80,128]{3,2,1,0:T(8,128)S(1)}, u32[]{:S(2)}) copy-start(f32[6,2,80,128]{3,2,1,0:T(8,128)S(1)} %collective-permute-done.2.left) | copy-start | bytes 1474564
  26.1 0.7 copy-start.3
  75.2 5.4 %collective-permute-start.4 = (f32[3,80,128]{2,1,0:T(8,128)}, f32[3,80,128]{2,1,0:T(8,128)S(1)}, u32[]{:S(2)}, u32[]{:S(2)}) collective-permute-start(f32[3,80,128]{2,1,0:T(8,128)} %get-tuple-element.24), channel_id=1, source_target_pairs={{0,4},{4,8},{8,12},{12,16},{16,20},{20,24},{24,28},{28,0},{1,5},{5... | collective-permute-start | bytes 368648 | tf_op jit(solution)/shard_map/ppermute | solution.py:448
  80.6 0.7 copy-start.2
  105.0 3.5 %collective-permute-start.5 = (f32[4,80,128]{2,1,0:T(8,128)}, f32[4,80,128]{2,1,0:T(8,128)S(1)}, u32[]{:S(2)}, u32[]{:S(2)}) collective-permute-start(f32[4,80,128]{2,1,0:T(8,128)} %get-tuple-element.27), channel_id=1, source_target_pairs={{0,28},{4,0},{8,4},{12,8},{16,12},{20,16},{24,20},{28,24},{1,29},{... | collective-permute-start | bytes 491528 | tf_op jit(solution)/shard_map/ppermute | solution.py:448
  108.4 0.7 copy-start.4
  127.3 24.2 %copy-start.5 = (f32[2,64,128]{2,1,0:T(8,128)S(1)}, f32[2,64,128]{2,1,0:T(8,128)}, u32[]{:S(2)}) copy-start(f32[2,64,128]{2,1,0:T(8,128)} %param.13) | copy-start | bytes 196612
  127.3 24.2 %copy-start.9 = (s32[2,64]{1,0:T(2,128)S(1)}, s32[2,64]{1,0:T(2,128)}, u32[]{:S(2)}) copy-start(s32[2,64]{1,0:T(2,128)} %param.15) | copy-start | bytes 1540
  127.3 24.9 %copy-start.10 = (s32[8,1]{0,1:T(1,128)S(1)}, s32[8,1]{0,1:T(1,128)}, u32[]{:S(2)}) copy-start(s32[8,1]{0,1:T(1,128)} %param.17) | copy-start | bytes 100
  127.3 25.6 %copy-start.11 = (s32[8,1]{0,1:T(1,128)S(1)}, s32[8,1]{0,1:T(1,128)}, u32[]{:S(2)}) copy-start(s32[8,1]{0,1:T(1,128)} %param.18) | copy-start | bytes 100
  127.4 5.8 %collective-permute-start.6 = (f32[2,80,128]{2,1,0:T(8,128)}, f32[2,80,128]{2,1,0:T(8,128)S(1)}, u32[]{:S(2)}, u32[]{:S(2)}) collective-permute-start(f32[2,80,128]{2,1,0:T(8,128)} %shard_map.156.p2), channel_id=1, source_target_pairs={{0,4},{4,8},{8,12},{12,16},{16,20},{20,24},{24,28},{28,0},{1,5},{5... | collective-permute-start | bytes 245768 | tf_op jit(solution)/shard_map/ppermute | solution.py:448
  133.1 0.6 copy-start.7
  151.4 2.5 %collective-permute-start.7 = (f32[2,80,128]{2,1,0:T(8,128)}, f32[2,80,128]{2,1,0:T(8,128)S(1)}, u32[]{:S(2)}, u32[]{:S(2)}) collective-permute-start(f32[2,80,128]{2,1,0:T(8,128)} %shard_map.157.p3), channel_id=1, source_target_pairs={{0,28},{4,0},{8,4},{12,8},{16,12},{20,16},{24,20},{28,24},{1,29},{... | collective-permute-start | bytes 245768 | tf_op jit(solution)/shard_map/ppermute | solution.py:448
  153.6 44.5 %copy-start.8 = (f32[2,80,128]{2,1,0:T(8,128)S(1)}, f32[2,80,128]{2,1,0:T(8,128)}, u32[]{:S(2)}) copy-start(f32[2,80,128]{2,1,0:T(8,128)} %get-tuple-element.21) | copy-start | bytes 245764
  153.9 0.6 copy-start.6
  190.4 8.4 %collective-permute-start.9 = (f32[6,8,128]{2,1,0:T(8,128)}, f32[6,8,128]{2,1,0:T(8,128)S(1)}, u32[]{:S(2)}, u32[]{:S(2)}) collective-permute-start(f32[6,8,128]{2,1,0:T(8,128)} %get-tuple-element.35), channel_id=1, source_target_pairs={{4,0},{8,4},{12,8},{16,12},{20,16},{24,20},{28,24},{5,1},{9,5},{13... | collective-permute-start | bytes 73736 | tf_op jit(solution)/shard_map/ppermute | solution.py:443
  196.2 6.3 %collective-permute-start.8 = (f32[6,8,128]{2,1,0:T(8,128)}, f32[6,8,128]{2,1,0:T(8,128)S(1)}, u32[]{:S(2)}, u32[]{:S(2)}) collective-permute-start(f32[6,8,128]{2,1,0:T(8,128)} %get-tuple-element.34), channel_id=1, source_target_pairs={{0,4},{4,8},{8,12},{12,16},{16,20},{20,24},{24,28},{1,5},{5,9},{9,... | collective-permute-start | bytes 73736 | tf_op jit(solution)/shard_map/ppermute | solution.py:443

commit v8 on v4

--- a/solution.py
+++ b/solution.py
@@ -2,6 +2,7 @@
 
 import jax
 import jax.numpy as jnp
+import ml_dtypes
 import numpy as np
 from jax import lax
 from jax.experimental import pallas as pl
@@ -36,6 +37,9 @@
     return [high, mid, rest - mid]
 
 
+ORDER = [*range(6), *range(12, 18), *range(24, 28), *range(6, 12), *range(18, 24), *range(28, 32)]
+
+
 def left_six(parts):
     h, m, l = parts
     return [h, h, h, m, m, l]
@@ -59,11 +63,12 @@
     source = (
         right_six(xs) + ones + x2 + right_six(zs) + ones + z2 + ones + split3(-square) + [one, zero]
     )
-    return target, source
+    return [target[i] for i in ORDER], [source[i] for i in ORDER]
 
 
 def position_signs(sx, sz):
-    return [1] * 6 + [sx] * 3 + [-sx] * 3 + [1] * 6 + [sz] * 3 + [-sz] * 3 + [1] * 6 + [-(sx * sx + sz * sz), 0]
+    signs = [1] * 6 + [sx] * 3 + [-sx] * 3 + [1] * 6 + [sz] * 3 + [-sz] * 3 + [1] * 6 + [-(sx * sx + sz * sz), 0]
+    return [signs[i] for i in ORDER]
 
 
 def velocity_rows(x, z, vx, vz):
@@ -100,20 +105,24 @@
     return target, source
 
 
-def sign_table(signs):
-    table = np.asarray([signs(sx, sz) for sx, sz in SHIFTS], np.float32)
-    return jnp.broadcast_to(jnp.asarray(table)[:, :, None], (*table.shape, 128)).astype(BF16)
-
-
-def position_table(cut_first, cut_second):
-    table = np.asarray([position_signs(sx, sz) for sx, sz in SHIFTS] * 2, np.float32)
-    constant = np.arange(KP) == KP - 2
-    sides = np.asarray([sx for sx, _ in SHIFTS] * 2)
-    target = np.repeat([0, 1], 9)
-    spots = lambda t, side: jnp.asarray(((target == t) & (sides == side))[:, None] & constant)
-    table = jnp.where(spots(0, cut_first[1]) & cut_first[0], FAR, jnp.asarray(table))
-    table = jnp.where(spots(1, cut_second[1]) & cut_second[0], FAR, table)
-    return jnp.broadcast_to(table[:, :, None], (18, KP, 128)).astype(BF16)
+def wide_table(table):
+    return np.repeat(np.asarray(table, np.float32)[:, :, None], 128, axis=2).astype(ml_dtypes.bfloat16)
+
+
+def velocity_table():
+    return wide_table([velocity_signs(sx, sz) for sx, sz in SHIFTS])[:, 16:]
+
+
+def position_table():
+    tables = []
+    for cuts in ((), ((0, -1),), ((1, 1),), ((0, 1), (1, -1))):
+        for t in range(2):
+            for sx, sz in SHIFTS:
+                signs = position_signs(sx, sz)
+                if (t, sx) in cuts:
+                    signs[KP - 2] = FAR
+                tables.append(signs)
+    return wide_table(tables)[:, 16:]
 
 
 def store_rows(rows, stage, dest, cell):
@@ -131,7 +140,10 @@
     parts = []
     for n in chunk:
         part = feat[cell + (n // 3) * depth + n % 3 - 1]
-        parts.append(part if table is None else part * table[first + n])
+        if table is not None:
+            fixed = part.shape[0] - table.shape[1]
+            part = jnp.concatenate([part[:fixed], part[fixed:] * table[first + n]], axis=0)
+        parts.append(part)
     return jnp.concatenate(parts, axis=1) if len(parts) > 1 else parts[0]
 
 
@@ -204,7 +216,7 @@
     wide_m[3 * depth : 4 * depth] = right[4, 0]
 
     def target(cell, slots):
-        sign = 9 * (cell >= depth).astype(jnp.int32)
+        sign = bounds[level, len(CLASSES) + 1] + 9 * (cell >= depth).astype(jnp.int32)
         pos_l, vel_l_t = upright(out_l[cell + depth], slots), upright(vel_l[cell], slots)
         sums = [jnp.zeros((slots, 128), F32)] * 2
 
@@ -252,7 +264,7 @@
 
 def jacobi_sums(level, order, bounds, first_col, feat_r, feat_l, posc, wide_u, acc, depth):
     def target(cell, slots):
-        sign = 9 * (cell >= depth).astype(jnp.int32)
+        sign = bounds[level, len(CLASSES) + 1] + 9 * (cell >= depth).astype(jnp.int32)
         at = cell + first_col * depth
         pos_l = upright(feat_l[at], slots)
         sums = [jnp.zeros((slots, 128), F32)]
@@ -291,7 +303,7 @@
     acc[...] = jnp.zeros_like(acc)
 
     def target(cell, slots):
-        sign = 9 * (cell >= depth).astype(jnp.int32)
+        sign = bounds[level, len(CLASSES) + 1] + 9 * (cell >= depth).astype(jnp.int32)
         pos_l = upright(feat_l[cell], slots)
         sums = [jnp.zeros((slots, 128), F32)] * 2
 
@@ -381,7 +393,7 @@
     lax.fori_loop(0, depth // 8, prepare, 0)
 
     def target(cell, slots):
-        sign = 9 * (cell >= depth).astype(jnp.int32)
+        sign = bounds[level, len(CLASSES) + 1] + 9 * (cell >= depth).astype(jnp.int32)
         pos_l, pres_l_t = upright(feat_l[cell + depth], slots), upright(pres_l[cell], slots)
         sums = [jnp.zeros((slots, 128), F32)] * 3
 
@@ -451,7 +463,7 @@
         out_down[index] = jnp.where(up, 0.0, block)
 
 
-def target_lists(count, cells):
+def target_lists(count, cells, tables):
     depth = count.shape[1]
     number = jnp.arange(2 * depth, dtype=jnp.int32)
     kinds = []
@@ -465,10 +477,12 @@
     kinds = jnp.stack(kinds)
     key = kinds * (2 * depth) + number
     rank = jnp.sum((key[:, None, :] < key[:, :, None]).astype(jnp.int32), 2)
-    bounds = jnp.stack([jnp.sum((kinds < c).astype(jnp.int32), 1) for c in range(len(CLASSES) + 1)], 1)
+    steps = jnp.arange(len(CLASSES) + 1, dtype=jnp.int32)
+    bounds = jnp.sum((kinds[:, None, :] < steps[None, :, None]).astype(jnp.int32), 2)
     place = jnp.arange(2 * depth + max(c for _, c in CLASSES), dtype=jnp.int32)
     order = jnp.sum(jnp.where(rank[:, None, :] == place[None, :, None], number, 0), 2)
-    return jnp.where(place < bounds[:, -1:], order, HALO), bounds
+    order = jnp.where(place < bounds[:, -1:], order, HALO)
+    return order, jnp.concatenate([bounds, tables[np.arange(ITERS + 2) % 2][:, None]], 1)
 
 
 def local_call(kernel, out_shapes, scratch, scalars, *operands):
@@ -510,13 +524,13 @@
     depth = cells + 2 * HALO
     first = lax.axis_index("col") == 0
     last = lax.axis_index("col") == lax.axis_size("col") - 1
-    here = position_table((first, -1), (last, 1))
-    back = position_table((first, 1), (first, -1))
-    velc = sign_table(velocity_signs)
+    here = jnp.where(first, 1, jnp.where(last, 2, 0))
+    back = jnp.where(first, 3, 0)
+    posc, velc = position_table(), velocity_table()
     plane = (2, depth, slots)
 
     live = jnp.stack([left[4, 1], own[4, 0], own[4, 1]]) > 0.0
-    lists = target_lists(jnp.sum(live.astype(jnp.int32), -1), cells)
+    lists = target_lists(jnp.sum(live.astype(jnp.int32), -1), cells, 18 * jnp.stack([here, back]))
     long = (4 * depth, slots)
     sums = (2 * depth, slots)
 
@@ -538,28 +552,28 @@
             (long, F32),
             ((2, *sums), F32),
         ],
-        lists, left, own, right, here, velc,
+        lists, left, own, right, posc, velc,
     )
     recv1 = around(send1, "col", 1)
     p1, diag, send2 = local_call(
         functools.partial(sweep1_kernel, 1),
         [(plane, F32), (plane, F32), ((4, depth, slots), F32)],
         [(long, F32), (long, F32), ((2, *sums), F32)],
-        lists, feat_r, feat_l, left, own, recv1, weight, source, back,
+        lists, feat_r, feat_l, left, own, recv1, weight, source, posc,
     )
     recv2 = around(send2, "col", -1)
     (p2,) = local_call(
         functools.partial(sweep2_kernel, 2),
         [(plane, F32)],
         [(long, F32), (sums, F32)],
-        lists, feat_r, feat_l, own, recv1, recv2, weight, source, diag, p1, here,
+        lists, feat_r, feat_l, own, recv1, recv2, weight, source, diag, p1, posc,
     )
     recv3 = around(p2, "col", 1)
     (p3,) = local_call(
         functools.partial(sweep3_kernel, 3),
         [(plane, F32)],
         [(long, F32), (sums, F32)],
-        lists, feat_r, feat_l, left, own, recv1, recv3, weight, source, diag, p2, back,
+        lists, feat_r, feat_l, left, own, recv1, recv3, weight, source, diag, p2, posc,
     )
     recv4 = around(p3, "col", -1)
     inner = (2, cells, slots)
@@ -574,7 +588,7 @@
             ((8 * KE, slots), F32),
             ((3, *sums), F32),
         ],
-        lists, feat_r, feat_l, own, recv1, recv2, recv4, left, right, weight, p3, here,
+        lists, feat_r, feat_l, own, recv1, recv2, recv4, left, right, weight, p3, posc,
     )
     density_ratio = density_ratio[:, HALO : HALO + cells]
     blocks = leaving_slot.shape[0]

time: 191 us -> 185 us (0.969)
  Pallas kernels: 130 us -> 128 us
  local copies, waits for them, and re-layouts: 8.61 us -> 6.63 us
    broadcast_in_dim x3 -> x1, local copies, waits for them, and re-layouts: 3.07 us -> 0.1 us  [target_lists(): tables[np.arange(ITERS + 2) % 2][:, None]]
    pallas_call x6, Pallas kernels: 130 us -> 128 us  [local_call(): pl.pallas_call(kernel, out_shape=[jax.ShapeDtypeStruct(shape, dtype) for...]
  transfers between devices with their start and end apart: 10 -> 10, of which waited for: 8 -> 7; matrix products, arithmetic and copies ran while one was open for 4% -> 4% of each run, Pallas kernels for 0% -> 0%
where the time goes in v8:
time: 185 us; the launch traced here: 183 us
  Pallas kernels  128 us (69%)
  waiting for transfers between devices  27.9 us (15%)
  starting transfers between devices  12.9 us (7%)
  other arithmetic  7.15 us (4%)
  local copies, waits for them, and re-layouts  6.63 us (4%)
    pallas_call x6, Pallas kernels, local_call(): pl.pallas_call(kernel, out_shape=[jax.ShapeDtypeStruct(shape, dtype) for...  128 us
    ppermute x6, waiting for transfers between devices, around(): lax.ppermute(block, axis, [(i, (i + distance) % peers) for i in range(pee...  20.2 us
    ppermute x4, starting transfers between devices, from_behind(): return lax.ppermute(block, axis, route)  7.96 us
    ppermute x4, waiting for transfers between devices, from_behind(): return lax.ppermute(block, axis, route)  7.67 us
    ppermute x6, starting transfers between devices, around(): lax.ppermute(block, axis, [(i, (i + distance) % peers) for i in range(pee...  4.91 us
    unnamed x26, local copies, waits for them, and re-layouts  4.62 us
  transfers between devices with their start and end apart: 10, of which 7 were waited for; matrix products, arithmetic and copies ran while one was open for 4% of the time, Pallas kernels for 0%

profile of v8, /device:TPU:28, one launch (start us, length us, event | category | flops | bytes accessed | tf_op | source)
XLA Modules:
  0.0 183.3 jit_solution(14243967213031591384)
XLA Ops:
  0.6 0.9 fusion.6
  1.6 0.8 pad_maximum_fusion.4
  2.4 2.4 %collective-permute-start.1 = (f32[6,2,8,128]{3,2,1,0:T(8,128)S(1)}, f32[6,2,8,128]{3,2,1,0:T(8,128)S(1)}, u32[]{:S(2)}, u32[]{:S(2)}) collective-permute-start(f32[6,2,8,128]{3,2,1,0:T(8,128)S(1)} %get-tuple-element.57), channel_id=1, source_target_pairs={{1,0},{2,1},{3,2},{5,4},{6,5},{7,6},{9,8},{10,9},{11,10},{13,12},{... | collective-permute-start | bytes 147464 | tf_op jit(solution)/shard_map/ppermute | solution.py:504
  4.7 1.3 collective-permute-start
  6.0 0.7 pad_clamp_fusion
  6.7 4.0 %collective-permute-done = f32[6,2,8,128]{3,2,1,0:T(8,128)S(1)} collective-permute-done((f32[6,2,8,128]{3,2,1,0:T(8,128)S(1)}, f32[6,2,8,128]{3,2,1,0:T(8,128)S(1)}, u32[]{:S(2)}, u32[]{:S(2)}) %collective-permute-start) | collective-permute-done | bytes 49184 | tf_op jit(solution)/shard_map/ppermute | solution.py:504
  10.7 1.0 pad_maximum_fusion.own
  11.9 0.6 gather_fusion
  12.7 2.7 %collective-permute-start.3 = (f32[5,1,80,128]{3,2,1,0:T(8,128)S(1)}, f32[5,1,80,128]{3,2,1,0:T(8,128)S(1)}, u32[]{:S(2)}, u32[]{:S(2)}) collective-permute-start(f32[5,1,80,128]{3,2,1,0:T(8,128)S(1)} %slice.48), channel_id=1, source_target_pairs={{0,28},{4,0},{8,4},{12,8},{16,12},{20,16},{24,20},{28,24},{1,29},{... | collective-permute-start | bytes 614408 | tf_op jit(solution)/shard_map/ppermute | solution.py:509
  15.4 7.8 %collective-permute-done.2.left = f32[6,2,80,128]{3,2,1,0:T(8,128)S(1)} collective-permute-done((f32[6,2,80,128]{3,2,1,0:T(8,128)S(1)}, f32[6,2,80,128]{3,2,1,0:T(8,128)S(1)}, u32[]{:S(2)}, u32[]{:S(2)}) %collective-permute-start.2) | collective-permute-done | bytes 491552 | tf_op jit(solution)/shard_map/ppermute | solution.py:509
  24.8 0.7 pad_add_fusion.bounds
  25.4 0.7 fusion.1.order
  26.1 0.7 copy-done.3
  26.8 37.2 %shard_map.163 = (bf16[400,32,128]{2,1,0:T(8,128)(2,1)}, bf16[240,32,128]{2,1,0:T(8,128)(2,1)}, f32[2,80,128]{2,1,0:T(8,128)}, f32[2,80,128]{2,1,0:T(8,128)}, f3...) custom-call(s32[5,176]{1,0:T(8,128)} %fusion.1.order, s32[5,6]{1,0:T(8,128)} %pad_add_fusion.bounds, ...), custom_call_target="tpu_custom_call" | custom-call | tf_op jit(solution)/shard_map/pallas_call | solution.py:491
  64.0 5.4 %collective-permute-done.4.recv.recv1 = f32[3,80,128]{2,1,0:T(8,128)S(1)} collective-permute-done((f32[3,80,128]{2,1,0:T(8,128)}, f32[3,80,128]{2,1,0:T(8,128)S(1)}, u32[]{:S(2)}, u32[]{:S(2)}) %collective-permute-start.4) | collective-permute-done | bytes 122912 | tf_op jit(solution)/shard_map/ppermute | solution.py:509
  69.4 0.7 copy-done.2
  70.1 22.5 %shard_map.164 = (f32[2,80,128]{2,1,0:T(8,128)}, f32[2,80,128]{2,1,0:T(8,128)}, f32[4,80,128]{2,1,0:T(8,128)}) custom-call(s32[5,176]{1,0:T(8,128)} %fusion.1.order, s32[5,6]{1,0:T(8,128)} %pad_add_fusion.bounds, bf16[400,32,128]{2,1,0:T(8,128)(2,1)} %get-tuple-element.22.feat_r, bf16[240,32,128]{2,1,0:T(8,128)(2,1)} %get-tuple-element.23.feat_l, ...), custom_call_target="tpu_custom_call" | custom-call | tf_op jit(solution)/shard_map/pallas_call | solution.py:491
  92.6 0.7 collective-permute-start.5
  93.3 3.2 %collective-permute-done.5.recv2 = f32[4,80,128]{2,1,0:T(8,128)S(1)} collective-permute-done((f32[4,80,128]{2,1,0:T(8,128)}, f32[4,80,128]{2,1,0:T(8,128)S(1)}, u32[]{:S(2)}, u32[]{:S(2)}) %collective-permute-start.5) | collective-permute-done | bytes 163872 | tf_op jit(solution)/shard_map/ppermute | solution.py:509
  96.5 0.7 copy-done.4
  97.2 17.8 %shard_map.165.p2 = f32[2,80,128]{2,1,0:T(8,128)} custom-call(s32[5,176]{1,0:T(8,128)} %fusion.1.order, s32[5,6]{1,0:T(8,128)} %pad_add_fusion.bounds, bf16[400,32,128]{2,1,0:T(8,128)(2,1)} %get-tuple-element.22.feat_r, bf16[240,32,128]{2,1,0:T(8,128)(2,1)} %get-tuple-element.23.feat_l, f32[6,2,80,128]{3,2,1,0:T(8,128)} %copy-done, f32[3,80,128]{2,1,0:T(8,128)} %copy-done.2, ...), custom_call_target="tpu_custom_call" | custom-call | tf_op jit(solution)/shard_map/pallas_call | solution.py:491
  115.0 1.4 collective-permute-start.6
  116.4 3.6 %collective-permute-done.6.recv3 = f32[2,80,128]{2,1,0:T(8,128)S(1)} collective-permute-done((f32[2,80,128]{2,1,0:T(8,128)}, f32[2,80,128]{2,1,0:T(8,128)S(1)}, u32[]{:S(2)}, u32[]{:S(2)}) %collective-permute-start.6) | collective-permute-done | bytes 81952 | tf_op jit(solution)/shard_map/ppermute | solution.py:509
  120.7 16.9 %shard_map.166.p3 = f32[2,80,128]{2,1,0:T(8,128)} custom-call(s32[5,176]{1,0:T(8,128)} %fusion.1.order, s32[5,6]{1,0:T(8,128)} %pad_add_fusion.bounds, bf16[400,32,128]{2,1,0:T(8,128)(2,1)} %get-tuple-element.22.feat_r, bf16[240,32,128]{2,1,0:T(8,128)(2,1)} %get-tuple-element.23.feat_l, f32[6,2,80,128]{3,2,1,0:T(8,128)} %copy-done.1, ...), custom_call_target="tpu_custom_call" | custom-call | tf_op jit(solution)/shard_map/pallas_call | solution.py:491
  137.6 0.7 fusion.mass
  138.3 0.7 copy.27.count
  139.0 0.7 copy.28.side
  140.6 30.2 %shard_map.167 = (f32[2,64,128]{2,1,0:T(8,128)}, f32[2,2,64,128]{3,2,1,0:T(8,128)}, f32[2,2,64,128]{3,2,1,0:T(8,128)}, f32[2,2,64,128]{3,2,1,0:T(8,128)}) custom-call(s32[5,176]{1,0:T(8,128)} %fusion.1.order, s32[5,6]{1,0:T(8,128)} %pad_add_fusion.bounds, bf16[400,32,128]{2,1,0:T(8,128)(2,1)} %get-tuple-element.22.feat_r, ...), custom_call_target="tpu_custom_call" | custom-call | tf_op jit(solution)/shard_map/pallas_call | solution.py:491
  170.8 3.2 %shard_map.168 = (f32[6,8,128]{2,1,0:T(8,128)}, f32[6,8,128]{2,1,0:T(8,128)}) custom-call(s32[8,128]{1,0:T(8,128)} %bitcast.23, s32[8,1]{1,0:T(8,128)} %copy.27.count, s32[8,1]{1,0:T(8,128)} %copy.28.side, f32[2,2,64,128]{3,2,1,0:T(8,128)} %get-tuple-element.52.offsets, f32[2,2,64,128]{3,2,1,0:T(8,128)} %get-tuple-element.51.velocity, ...), custom_call_target="tpu_custom_call" | custom-call | tf_op jit(solution)/shard_map/pallas_call | solution.py:491
  174.0 2.4 %collective-permute-start.9 = (f32[6,8,128]{2,1,0:T(8,128)}, f32[6,8,128]{2,1,0:T(8,128)S(1)}, u32[]{:S(2)}, u32[]{:S(2)}) collective-permute-start(f32[6,8,128]{2,1,0:T(8,128)} %get-tuple-element.35), channel_id=1, source_target_pairs={{4,0},{8,4},{12,8},{16,12},{20,16},{24,20},{28,24},{5,1},{9,5},{13... | collective-permute-start | bytes 73736 | tf_op jit(solution)/shard_map/ppermute | solution.py:504
  176.4 1.9 %collective-permute-start.8 = (f32[6,8,128]{2,1,0:T(8,128)}, f32[6,8,128]{2,1,0:T(8,128)S(1)}, u32[]{:S(2)}, u32[]{:S(2)}) collective-permute-start(f32[6,8,128]{2,1,0:T(8,128)} %get-tuple-element.34), channel_id=1, source_target_pairs={{0,4},{4,8},{8,12},{12,16},{16,20},{20,24},{24,28},{1,5},{5,9},{9,... | collective-permute-start | bytes 73736 | tf_op jit(solution)/shard_map/ppermute | solution.py:504
  179.0 3.7 %collective-permute-done.8 = f32[6,8,128]{2,1,0:T(8,128)S(1)} collective-permute-done((f32[6,8,128]{2,1,0:T(8,128)}, f32[6,8,128]{2,1,0:T(8,128)S(1)}, u32[]{:S(2)}, u32[]{:S(2)}) %collective-permute-start.8) | collective-permute-done | bytes 24608 | tf_op jit(solution)/shard_map/ppermute | solution.py:504
  (51 shorter events, 4.7 us)
Async XLA Ops:
  2.4 4.4 %collective-permute-start.1 = (f32[6,2,8,128]{3,2,1,0:T(8,128)S(1)}, f32[6,2,8,128]{3,2,1,0:T(8,128)S(1)}, u32[]{:S(2)}, u32[]{:S(2)}) collective-permute-start(f32[6,2,8,128]{3,2,1,0:T(8,128)S(1)} %get-tuple-element.57), channel_id=1, source_target_pairs={{1,0},{2,1},{3,2},{5,4},{6,5},{7,6},{9,8},{10,9},{11,10},{13,12},{... | collective-permute-start | bytes 147464 | tf_op jit(solution)/shard_map/ppermute | solution.py:504
  4.7 6.0 %collective-permute-start = (f32[6,2,8,128]{3,2,1,0:T(8,128)S(1)}, f32[6,2,8,128]{3,2,1,0:T(8,128)S(1)}, u32[]{:S(2)}, u32[]{:S(2)}) collective-permute-start(f32[6,2,8,128]{3,2,1,0:T(8,128)S(1)} %get-tuple-element.56), channel_id=1, source_target_pairs={{0,1},{1,2},{2,3},{4,5},{5,6},{6,7},{8,9},{9,10},{10,11},{12,13},{... | collective-permute-start | bytes 147464 | tf_op jit(solution)/shard_map/ppermute | solution.py:504
  11.8 14.3 %copy-start = (f32[6,2,80,128]{3,2,1,0:T(8,128)}, f32[6,2,80,128]{3,2,1,0:T(8,128)S(1)}, u32[]{:S(2)}) copy-start(f32[6,2,80,128]{3,2,1,0:T(8,128)S(1)} %pad_maximum_fusion.own) | copy-start | bytes 1474564
  11.8 11.4 %collective-permute-start.2 = (f32[6,2,80,128]{3,2,1,0:T(8,128)S(1)}, f32[6,2,80,128]{3,2,1,0:T(8,128)S(1)}, u32[]{:S(2)}, u32[]{:S(2)}) collective-permute-start(f32[6,2,80,128]{3,2,1,0:T(8,128)S(1)} %pad_maximum_fusion.own), channel_id=1, source_target_pairs={{0,4},{4,8},{8,12},{12,16},{16,20},{20,24},{24,28},{28,0},{1,5},{5... | collective-permute-start | bytes 1474568 | tf_op jit(solution)/shard_map/ppermute | solution.py:509
  12.7 13.4 %collective-permute-start.3 = (f32[5,1,80,128]{3,2,1,0:T(8,128)S(1)}, f32[5,1,80,128]{3,2,1,0:T(8,128)S(1)}, u32[]{:S(2)}, u32[]{:S(2)}) collective-permute-start(f32[5,1,80,128]{3,2,1,0:T(8,128)S(1)} %slice.48), channel_id=1, source_target_pairs={{0,28},{4,0},{8,4},{12,8},{16,12},{20,16},{24,20},{28,24},{1,29},{... | collective-permute-start | bytes 614408 | tf_op jit(solution)/shard_map/ppermute | solution.py:509
  23.2 2.9 %copy-start.1 = (f32[6,2,80,128]{3,2,1,0:T(8,128)}, f32[6,2,80,128]{3,2,1,0:T(8,128)S(1)}, u32[]{:S(2)}) copy-start(f32[6,2,80,128]{3,2,1,0:T(8,128)S(1)} %collective-permute-done.2.left) | copy-start | bytes 1474564
  26.1 0.7 copy-start.3
  64.0 5.4 %collective-permute-start.4 = (f32[3,80,128]{2,1,0:T(8,128)}, f32[3,80,128]{2,1,0:T(8,128)S(1)}, u32[]{:S(2)}, u32[]{:S(2)}) collective-permute-start(f32[3,80,128]{2,1,0:T(8,128)} %get-tuple-element.24), channel_id=1, source_target_pairs={{0,4},{4,8},{8,12},{12,16},{16,20},{20,24},{24,28},{28,0},{1,5},{5... | collective-permute-start | bytes 368648 | tf_op jit(solution)/shard_map/ppermute | solution.py:509
  69.4 0.7 copy-start.2
  92.6 3.9 %collective-permute-start.5 = (f32[4,80,128]{2,1,0:T(8,128)}, f32[4,80,128]{2,1,0:T(8,128)S(1)}, u32[]{:S(2)}, u32[]{:S(2)}) collective-permute-start(f32[4,80,128]{2,1,0:T(8,128)} %get-tuple-element.27), channel_id=1, source_target_pairs={{0,28},{4,0},{8,4},{12,8},{16,12},{20,16},{24,20},{28,24},{1,29},{... | collective-permute-start | bytes 491528 | tf_op jit(solution)/shard_map/ppermute | solution.py:509
  96.5 0.7 copy-start.4
  115.0 22.6 %copy-start.5 = (f32[2,64,128]{2,1,0:T(8,128)S(1)}, f32[2,64,128]{2,1,0:T(8,128)}, u32[]{:S(2)}) copy-start(f32[2,64,128]{2,1,0:T(8,128)} %param.14) | copy-start | bytes 196612
  115.0 22.6 %copy-start.9 = (s32[2,64]{1,0:T(2,128)S(1)}, s32[2,64]{1,0:T(2,128)}, u32[]{:S(2)}) copy-start(s32[2,64]{1,0:T(2,128)} %param.16) | copy-start | bytes 1540
  115.0 23.3 %copy-start.10 = (s32[8,1]{0,1:T(1,128)S(1)}, s32[8,1]{0,1:T(1,128)}, u32[]{:S(2)}) copy-start(s32[8,1]{0,1:T(1,128)} %param.18) | copy-start | bytes 100
  115.0 24.0 %copy-start.11 = (s32[8,1]{0,1:T(1,128)S(1)}, s32[8,1]{0,1:T(1,128)}, u32[]{:S(2)}) copy-start(s32[8,1]{0,1:T(1,128)} %param.19) | copy-start | bytes 100
  115.0 5.0 %collective-permute-start.6 = (f32[2,80,128]{2,1,0:T(8,128)}, f32[2,80,128]{2,1,0:T(8,128)S(1)}, u32[]{:S(2)}, u32[]{:S(2)}) collective-permute-start(f32[2,80,128]{2,1,0:T(8,128)} %shard_map.165.p2), channel_id=1, source_target_pairs={{0,4},{4,8},{8,12},{12,16},{16,20},{20,24},{24,28},{28,0},{1,5},{5... | collective-permute-start | bytes 245768 | tf_op jit(solution)/shard_map/ppermute | solution.py:509
  120.0 0.6 copy-start.7
  137.6 2.4 %collective-permute-start.7 = (f32[2,80,128]{2,1,0:T(8,128)}, f32[2,80,128]{2,1,0:T(8,128)S(1)}, u32[]{:S(2)}, u32[]{:S(2)}) collective-permute-start(f32[2,80,128]{2,1,0:T(8,128)} %shard_map.166.p3), channel_id=1, source_target_pairs={{0,28},{4,0},{8,4},{12,8},{16,12},{20,16},{24,20},{28,24},{1,29},{... | collective-permute-start | bytes 245768 | tf_op jit(solution)/shard_map/ppermute | solution.py:509
  139.6 38.7 %copy-start.8 = (f32[2,80,128]{2,1,0:T(8,128)S(1)}, f32[2,80,128]{2,1,0:T(8,128)}, u32[]{:S(2)}) copy-start(f32[2,80,128]{2,1,0:T(8,128)} %get-tuple-element.21) | copy-start | bytes 245764
  139.9 0.6 copy-start.6
  174.0 5.0 %collective-permute-start.9 = (f32[6,8,128]{2,1,0:T(8,128)}, f32[6,8,128]{2,1,0:T(8,128)S(1)}, u32[]{:S(2)}, u32[]{:S(2)}) collective-permute-start(f32[6,8,128]{2,1,0:T(8,128)} %get-tuple-element.35), channel_id=1, source_target_pairs={{4,0},{8,4},{12,8},{16,12},{20,16},{24,20},{28,24},{5,1},{9,5},{13... | collective-permute-start | bytes 73736 | tf_op jit(solution)/shard_map/ppermute | solution.py:504
  176.4 6.3 %collective-permute-start.8 = (f32[6,8,128]{2,1,0:T(8,128)}, f32[6,8,128]{2,1,0:T(8,128)S(1)}, u32[]{:S(2)}, u32[]{:S(2)}) collective-permute-start(f32[6,8,128]{2,1,0:T(8,128)} %get-tuple-element.34), channel_id=1, source_target_pairs={{0,4},{4,8},{8,12},{12,16},{16,20},{20,24},{24,28},{1,5},{5,9},{9,... | collective-permute-start | bytes 73736 | tf_op jit(solution)/shard_map/ppermute | solution.py:504
